TPU v7x, 128 devices: a whole 4x4x4 slice. The times are simulated.
128 devices in a mesh: blk: 32 (over x, z, core), mem: 4 (over y).
Axes of the slice: x: 4, y: 4, z: 4, core: 2. Of those that a mesh axis runs over, the one named last changes fastest.
Arguments:
- anomalies: bfloat16 [128, 524288], P('mem', 'blk'), may hold values from -6 to 6
- increments: bfloat16 [8, 524288], P(None, ('blk', 'mem')), may hold values from -6 to 6
- taper_table: float32 [8], replicated, may hold values from 0.2 to 1
- taper_modes: float32 [8], replicated, may hold values from 0.05 to 0.5
- pair_code: int32 [512], P(('blk', 'mem')), may hold values from 0 to 3, as said below
- pair_class: int32 [512], P(('blk', 'mem')), may hold values from 0 to 7
- pair_count: int32 [128], P(('blk', 'mem')), may hold values from 1 to 4, as said below
Outputs:
- covariance_product: float32 [8, 524288], P(None, ('blk', 'mem'))
Inputs may be any that keep to these rules, and one draw needn't show every extreme that they name: `pair_code`: within one device's 4 slots the codes are distinct; slots beyond the device's count hold codes too and are not listed. `pair_count`: some device lists all 4 slots.
All inputs are finite; a program needn't handle non-finite values.
Results may differ from a plain program's by a relative error of at most 0.0029.
Values may be sent and summed in bfloat16 or wider, within the bound.
No kernel may reach another device: no remote copies, remote signals or barrier semaphores. Data moves between devices by JAX's collectives and lax.ppermute only.
A program may use at most 128 MiB of HBM per device.

v0:
```python
import math

import jax
import jax.numpy as jnp
from jax import lax
from jax.sharding import PartitionSpec as P

BLOCK = 2048
MODES = 8
PERIOD = 12288


def shifted(block, axis, distance):
    devices = range(lax.axis_size(axis))
    route = [((i - distance) % len(devices), i) for i in devices]
    return lax.ppermute(block, axis, route)


def phases(start):
    mode_ids = jnp.arange(MODES, dtype=jnp.int32)
    places = jnp.arange(BLOCK, dtype=jnp.int32) + start
    angle = (mode_ids[:, None] * places[None, :] % PERIOD).astype(jnp.float32) * jnp.float32(
        2.0 * math.pi / PERIOD
    )
    return (jnp.cos(angle), jnp.sin(angle))


def taper_tile(taper_modes, offset):
    hi = lax.Precision.HIGHEST
    base_cos, base_sin = phases(jnp.int32(0))
    left_basis = jnp.concatenate(
        [base_cos * taper_modes[:, None], base_sin * taper_modes[:, None]], 0
    )
    far_cos, far_sin = phases(offset * BLOCK)
    right_basis = jnp.concatenate([far_cos, far_sin], 0)
    return lax.dot_general(left_basis, right_basis, (((0,), (0,)), ((), ())), precision=hi)


def make_tile(first_x, second_x, taper_modes, offset, weight):
    gram = lax.dot_general(
        first_x, second_x, (((0,), (0,)), ((), ())), preferred_element_type=jnp.float32
    )
    return (gram * taper_tile(taper_modes, offset) * weight).astype(jnp.bfloat16)


def apply_first(tile, second_v):
    return lax.dot_general(
        second_v, tile, (((1,), (1,)), ((), ())), preferred_element_type=jnp.float32
    )


def apply_second(tile, first_v):
    return jnp.dot(first_v, tile, preferred_element_type=jnp.float32)


def body(anomalies, increments, taper_table, taper_modes, pair_code, pair_class, pair_count):
    moved = lax.all_to_all(anomalies, "mem", split_axis=1, concat_axis=0, tiled=True)
    members = moved.shape[0]
    nblk = moved.shape[1] // BLOCK
    own = moved.reshape(members, nblk, BLOCK).transpose(1, 0, 2)
    cols = increments.shape[0]
    vown = increments.reshape(cols, nblk, BLOCK).transpose(1, 0, 2)
    scale = jnp.float32(1.0 / (members - 1))
    class_ids = jnp.arange(taper_table.shape[0], dtype=jnp.int32)
    diag_taper = taper_tile(taper_modes, jnp.int32(0))

    def taper(klass):
        return jnp.sum(jnp.where(class_ids == klass, taper_table, jnp.float32(0.0)))

    def diagonal(index, acc):
        block_x = lax.dynamic_index_in_dim(own, index, 0, keepdims=False)
        block_v = lax.dynamic_index_in_dim(vown, index, 0, keepdims=False)
        gram = lax.dot_general(
            block_x, block_x, (((0,), (0,)), ((), ())), preferred_element_type=jnp.float32
        )
        tile = (gram * diag_taper).astype(jnp.bfloat16)
        return acc.at[index].add(apply_first(tile, block_v))

    local = lax.fori_loop(0, nblk, diagonal, jnp.zeros((nblk, cols, BLOCK), jnp.float32))
    nextx, nextv = shifted((own, vown), ("blk", "mem"), -1)
    window_x = jnp.concatenate([own, nextx], 0)
    window_v = jnp.concatenate([vown, nextv], 0)
    totals = jnp.concatenate([local, jnp.zeros_like(local)], 0)

    def pairwise(slot, acc):
        code = pair_code[slot]
        first = code // nblk
        offset = code % nblk + 1
        second = first + offset
        first_x = lax.dynamic_index_in_dim(window_x, first, 0, keepdims=False)
        second_x = lax.dynamic_index_in_dim(window_x, second, 0, keepdims=False)
        first_v = lax.dynamic_index_in_dim(window_v, first, 0, keepdims=False)
        second_v = lax.dynamic_index_in_dim(window_v, second, 0, keepdims=False)
        tile = make_tile(first_x, second_x, taper_modes, offset, taper(pair_class[slot]))
        acc = acc.at[first].add(apply_first(tile, second_v))
        return acc.at[second].add(apply_second(tile, first_v))

    totals = lax.fori_loop(0, pair_count[0], pairwise, totals)
    back = shifted(totals[nblk:], ("blk", "mem"), 1)
    result = (totals[:nblk] + back) * scale
    return result.transpose(1, 0, 2).reshape(cols, nblk * BLOCK)


def solution(mesh):
    in_specs = (
        P("mem", "blk"),
        P(None, ("blk", "mem")),
        P(),
        P(),
        P(("blk", "mem")),
        P(("blk", "mem")),
        P(("blk", "mem")),
    )
    out_specs = P(None, ("blk", "mem"))
    return jax.shard_map(body, mesh=mesh, in_specs=in_specs, out_specs=out_specs, check_vma=False)
```

profile of v0, /device:TPU:5, one launch (start us, length us, event | category | flops | bytes accessed | tf_op | source)
XLA Modules:
  0.0 210.6 jit_solution(14822902630443834270)
XLA Ops:
  0.0 2.3 %copy.13 = bf16[4,4,8,4096]{3,2,0,1:T(8,128)(2,1)} copy(bf16[4,4,8,4096]{3,2,1,0:T(8,128)(2,1)} %bitcast.99) | data formatting | bytes 2097152 | tf_op jit(solution)/shard_map/all_to_all | solution.py:57
  2.3 4.2 %all-to-all-start = ((bf16[32,4,4096]{2,0,1:T(8,128)(2,1)}), bf16[32,4,4096]{2,0,1:T(8,128)(2,1)S(1)}, u32[]{:S(2)}, u32[]{:S(2)}) async-start(bf16[32,4,4096]{2,0,1:T(8,128)(2,1)} %bitcast.62), calls=%async_computation | async-start | bytes 2097152 | tf_op jit(solution)/shard_map/all_to_all | solution.py:57
  6.5 3.8 %collective-permute-start = (bf16[2,8,2048]{2,1,0:T(8,128)(2,1)}, bf16[2,8,2048]{2,1,0:T(8,128)(2,1)S(1)}, u32[]{:S(2)}, u32[]{:S(2)}) collective-permute-start(bf16[2,8,2048]{2,1,0:T(8,128)(2,1)} %bitcast.100), channel_id=1, source_target_pairs={{1,0},{2,1},{3,2},{4,3},{5,4},{6,5},{7,6},{8,7},{9,8},{10,9},{11,1... | collective-permute-start | bytes 196616 | tf_op jit(solution)/shard_map/ppermute | solution.py:16
  10.3 0.9 broadcast_multiply_fusion.1
  11.5 16.0 %fusion.53 = f32[2048,2048]{1,0:T(8,128)} fusion(f32[8,2048]{1,0:T(8,128)S(1)} %get-tuple-element.386, f32[8,2048]{1,0:T(8,128)S(1)} %get-tuple-element.385, f32[8,2048]{1,0:T(8,128)S(1)} %get-tuple-element.387, f32[8,2048]{1,0:T(8,128)S(1)} %get-tuple-element.388), kind=kOutput, calls=%fused_computation.70 | convolution fusion | flops 805371904 | bytes 17039360 | tf_op jit(solution)/shard_map/dot_general | solution.py:36
  29.7 23.2 %while.30 = (s32[]{:T(128)}, f32[2,8,2048]{2,1,0:T(8,128)S(1)}, bf16[2,8,2048]{2,1,0:T(8,128)(2,1)S(1)}, bf16[2,128,2048]{2,1,0:T(8,128)(2,1)S(1)}, f32[2048,204...) while((s32[]{:T(128)}, f32[2,8,2048]{2,1,0:T(8,128)S(1)}, bf16[2,8,2048]{2,1,0:T(8,128)(2,1)S(1)}, ...), condition=%wide.region_2.3_spmd, body=%wide.region_0.2_spmd.sunk | while | flops 1149272064 | bytes 17467496 | solution.py:79
  30.4 10.8 %fusion.88 = f32[2,8,2048]{2,1,0:T(8,128)S(1)} fusion(f32[2,8,2048]{2,1,0:T(8,128)S(1)} %get-tuple-element.497, s32[]{:T(128)} %get-tuple-element.496, f32[2048,2048]{1,0:T(8,128)} %get-tuple-element.508, bf16[2,128,2048]{2,1,0:T(8,128)(2,1)S(1)} %get-tuple-element.507, bf16[2,8,2048]{2,1,0:T(8,128)(2,1)S(1)} %get-tuple-element.506, ...), kind=kOutput, calls=%fused_computation.6.clone.1 | convolution fusion | flops 1149272064 | bytes 17467392 | tf_op jit(solution)/shard_map/while/body/eval_jaxpr/dot_general | solution.py:47
  42.0 10.8 %fusion.88 = f32[2,8,2048]{2,1,0:T(8,128)S(1)} fusion(f32[2,8,2048]{2,1,0:T(8,128)S(1)} %get-tuple-element.497, s32[]{:T(128)} %get-tuple-element.496, f32[2048,2048]{1,0:T(8,128)} %get-tuple-element.508, bf16[2,128,2048]{2,1,0:T(8,128)(2,1)S(1)} %get-tuple-element.507, bf16[2,8,2048]{2,1,0:T(8,128)(2,1)S(1)} %get-tuple-element.506, ...), kind=kOutput, calls=%fused_computation.6.clone.1 | convolution fusion | flops 1149272064 | bytes 17467392 | tf_op jit(solution)/shard_map/while/body/eval_jaxpr/dot_general | solution.py:47
  52.9 3.2 %pad_maximum_fusion = bf16[4,128,2048]{2,0,1:T(4,128)(2,1)S(1)} fusion(bf16[2,128,2048]{2,0,1:T(2,128)(2,1)} %collective-permute-done.1, bf16[2,128,2048]{2,0,1:T(2,128)(2,1)S(1)} %bitcast.97), kind=kLoop, calls=%fused_computation.68 | loop fusion | flops 4194304 | bytes 4194304 | tf_op jit(solution)/shard_map/concatenate | solution.py:81
  56.2 1.2 copy.10
  57.4 145.2 %while.31 = (s32[]{:T(128)}, f32[4,8,2048]{2,1,0:T(8,128)S(1)}, s32[]{:T(128)}, s32[4]{0:T(128)S(1)}, bf16[4,8,2048]{2,1,0:T(8,128)(2,1)S(1)}, /*index=5*/bf16[4...) while((s32[]{:T(128)}, f32[4,8,2048]{2,1,0:T(8,128)S(1)}, ...), condition=%wide.region_7.8_spmd.clone, body=%wide.region_3.7_spmd.clone.sunk | while | flops 2026309632 | bytes 60637816 | solution.py:98
  61.1 16.0 %fusion.98 = f32[2048,2048]{1,0:T(8,128)} fusion(f32[8,2048]{1,0:T(8,128)S(1)} %get-tuple-element.482, f32[8,2048]{1,0:T(8,128)S(1)} %get-tuple-element.483, f32[8,2048]{1,0:T(8,128)S(1)} %get-tuple-element.484, f32[8,2048]{1,0:T(8,128)S(1)} %get-tuple-element.485), kind=kOutput, calls=%fused_computation.26.clone.1 | convolution fusion | flops 805371904 | bytes 17039360 | tf_op jit(solution)/shard_map/while/body/dot_general | solution.py:36
  78.3 1.2 fusion.99
  79.5 8.7 %multiply_convert_fusion.3 = bf16[2048,2048]{1,0:T(8,128)(2,1)S(1)} fusion(f32[2048,2048]{1,0:T(8,128)} %fusion.98, f32[]{:T(128)} %fusion.99, bf16[4,128,2048]{2,1,0:T(8,128)(2,1)S(1)} %get-tuple-element.551, s32[]{:T(128)} %select_n.167, s32[]{:T(128)} %select_n.165), kind=kOutput, calls=%fused_computation.13.clone.1 | convolution fusion | flops 1086324736 | bytes 26214412 | tf_op jit(solution)/shard_map/while/body/dot_general | solution.py:40
  89.0 2.8 %fusion.100 = f32[4,8,2048]{2,1,0:T(8,128)S(1)} fusion(f32[4,8,2048]{2,1,0:T(8,128)S(1)} %get-tuple-element.530, s32[]{:T(128)} %select_n.165, bf16[2048,2048]{1,0:T(8,128)(2,1)S(1)} %multiply_convert_fusion.3, bf16[4,8,2048]{2,1,0:T(8,128)(2,1)S(1)} %get-tuple-element.550, s32[]{:T(128)} %select_n.167, pred[]{:T(512)} %get-tuple-element.486), kind=kOutput, calls=%fused_computation.21.clone.1 | convolution fusion | flops 67141632 | bytes 8552457 | tf_op jit(solution)/shard_map/while/body/dot_general | solution.py:47
  91.8 1.9 fusion.101
  97.2 16.0 %fusion.98 = f32[2048,2048]{1,0:T(8,128)} fusion(f32[8,2048]{1,0:T(8,128)S(1)} %get-tuple-element.482, f32[8,2048]{1,0:T(8,128)S(1)} %get-tuple-element.483, f32[8,2048]{1,0:T(8,128)S(1)} %get-tuple-element.484, f32[8,2048]{1,0:T(8,128)S(1)} %get-tuple-element.485), kind=kOutput, calls=%fused_computation.26.clone.1 | convolution fusion | flops 805371904 | bytes 17039360 | tf_op jit(solution)/shard_map/while/body/dot_general | solution.py:36
  114.4 1.2 fusion.99
  115.6 8.7 %multiply_convert_fusion.3 = bf16[2048,2048]{1,0:T(8,128)(2,1)S(1)} fusion(f32[2048,2048]{1,0:T(8,128)} %fusion.98, f32[]{:T(128)} %fusion.99, bf16[4,128,2048]{2,1,0:T(8,128)(2,1)S(1)} %get-tuple-element.551, s32[]{:T(128)} %select_n.167, s32[]{:T(128)} %select_n.165), kind=kOutput, calls=%fused_computation.13.clone.1 | convolution fusion | flops 1086324736 | bytes 26214412 | tf_op jit(solution)/shard_map/while/body/dot_general | solution.py:40
  125.0 2.8 %fusion.100 = f32[4,8,2048]{2,1,0:T(8,128)S(1)} fusion(f32[4,8,2048]{2,1,0:T(8,128)S(1)} %get-tuple-element.530, s32[]{:T(128)} %select_n.165, bf16[2048,2048]{1,0:T(8,128)(2,1)S(1)} %multiply_convert_fusion.3, bf16[4,8,2048]{2,1,0:T(8,128)(2,1)S(1)} %get-tuple-element.550, s32[]{:T(128)} %select_n.167, pred[]{:T(512)} %get-tuple-element.486), kind=kOutput, calls=%fused_computation.21.clone.1 | convolution fusion | flops 67141632 | bytes 8552457 | tf_op jit(solution)/shard_map/while/body/dot_general | solution.py:47
  127.9 1.9 fusion.101
  133.3 16.0 %fusion.98 = f32[2048,2048]{1,0:T(8,128)} fusion(f32[8,2048]{1,0:T(8,128)S(1)} %get-tuple-element.482, f32[8,2048]{1,0:T(8,128)S(1)} %get-tuple-element.483, f32[8,2048]{1,0:T(8,128)S(1)} %get-tuple-element.484, f32[8,2048]{1,0:T(8,128)S(1)} %get-tuple-element.485), kind=kOutput, calls=%fused_computation.26.clone.1 | convolution fusion | flops 805371904 | bytes 17039360 | tf_op jit(solution)/shard_map/while/body/dot_general | solution.py:36
  150.5 1.2 fusion.99
  151.7 8.7 %multiply_convert_fusion.3 = bf16[2048,2048]{1,0:T(8,128)(2,1)S(1)} fusion(f32[2048,2048]{1,0:T(8,128)} %fusion.98, f32[]{:T(128)} %fusion.99, bf16[4,128,2048]{2,1,0:T(8,128)(2,1)S(1)} %get-tuple-element.551, s32[]{:T(128)} %select_n.167, s32[]{:T(128)} %select_n.165), kind=kOutput, calls=%fused_computation.13.clone.1 | convolution fusion | flops 1086324736 | bytes 26214412 | tf_op jit(solution)/shard_map/while/body/dot_general | solution.py:40
  161.1 2.8 %fusion.100 = f32[4,8,2048]{2,1,0:T(8,128)S(1)} fusion(f32[4,8,2048]{2,1,0:T(8,128)S(1)} %get-tuple-element.530, s32[]{:T(128)} %select_n.165, bf16[2048,2048]{1,0:T(8,128)(2,1)S(1)} %multiply_convert_fusion.3, bf16[4,8,2048]{2,1,0:T(8,128)(2,1)S(1)} %get-tuple-element.550, s32[]{:T(128)} %select_n.167, pred[]{:T(512)} %get-tuple-element.486), kind=kOutput, calls=%fused_computation.21.clone.1 | convolution fusion | flops 67141632 | bytes 8552457 | tf_op jit(solution)/shard_map/while/body/dot_general | solution.py:47
  164.0 1.9 fusion.101
  169.4 16.0 %fusion.98 = f32[2048,2048]{1,0:T(8,128)} fusion(f32[8,2048]{1,0:T(8,128)S(1)} %get-tuple-element.482, f32[8,2048]{1,0:T(8,128)S(1)} %get-tuple-element.483, f32[8,2048]{1,0:T(8,128)S(1)} %get-tuple-element.484, f32[8,2048]{1,0:T(8,128)S(1)} %get-tuple-element.485), kind=kOutput, calls=%fused_computation.26.clone.1 | convolution fusion | flops 805371904 | bytes 17039360 | tf_op jit(solution)/shard_map/while/body/dot_general | solution.py:36
  186.6 1.2 fusion.99
  187.8 8.7 %multiply_convert_fusion.3 = bf16[2048,2048]{1,0:T(8,128)(2,1)S(1)} fusion(f32[2048,2048]{1,0:T(8,128)} %fusion.98, f32[]{:T(128)} %fusion.99, bf16[4,128,2048]{2,1,0:T(8,128)(2,1)S(1)} %get-tuple-element.551, s32[]{:T(128)} %select_n.167, s32[]{:T(128)} %select_n.165), kind=kOutput, calls=%fused_computation.13.clone.1 | convolution fusion | flops 1086324736 | bytes 26214412 | tf_op jit(solution)/shard_map/while/body/dot_general | solution.py:40
  197.2 2.8 %fusion.100 = f32[4,8,2048]{2,1,0:T(8,128)S(1)} fusion(f32[4,8,2048]{2,1,0:T(8,128)S(1)} %get-tuple-element.530, s32[]{:T(128)} %select_n.165, bf16[2048,2048]{1,0:T(8,128)(2,1)S(1)} %multiply_convert_fusion.3, bf16[4,8,2048]{2,1,0:T(8,128)(2,1)S(1)} %get-tuple-element.550, s32[]{:T(128)} %select_n.167, pred[]{:T(512)} %get-tuple-element.486), kind=kOutput, calls=%fused_computation.21.clone.1 | convolution fusion | flops 67141632 | bytes 8552457 | tf_op jit(solution)/shard_map/while/body/dot_general | solution.py:47
  200.0 1.9 fusion.101
  202.7 7.2 %collective-permute-done.2 = f32[2,8,2048]{2,1,0:T(8,128)S(1)} collective-permute-done((f32[2,8,2048]{2,1,0:T(8,128)S(1)}, f32[2,8,2048]{2,1,0:T(8,128)S(1)}, u32[]{:S(2)}, u32[]{:S(2)}) %collective-permute-start.2) | collective-permute-done | bytes 131104 | tf_op jit(solution)/shard_map/ppermute | solution.py:16
  (49 shorter events, 14.9 us)
Async XLA Ops:
  2.3 25.2 %all-to-all-start = ((bf16[32,4,4096]{2,0,1:T(8,128)(2,1)}), bf16[32,4,4096]{2,0,1:T(8,128)(2,1)S(1)}, u32[]{:S(2)}, u32[]{:S(2)}) async-start(bf16[32,4,4096]{2,0,1:T(8,128)(2,1)} %bitcast.62), calls=%async_computation | async-start | bytes 2097152 | tf_op jit(solution)/shard_map/all_to_all | solution.py:57
  6.5 21.0 %collective-permute-start = (bf16[2,8,2048]{2,1,0:T(8,128)(2,1)}, bf16[2,8,2048]{2,1,0:T(8,128)(2,1)S(1)}, u32[]{:S(2)}, u32[]{:S(2)}) collective-permute-start(bf16[2,8,2048]{2,1,0:T(8,128)(2,1)} %bitcast.100), channel_id=1, source_target_pairs={{1,0},{2,1},{3,2},{4,3},{5,4},{6,5},{7,6},{8,7},{9,8},{10,9},{11,1... | collective-permute-start | bytes 196616 | tf_op jit(solution)/shard_map/ppermute | solution.py:16
  11.5 16.0 %copy-start = (bf16[8,4096]{1,0:T(8,128)(2,1)S(1)}, bf16[8,4096]{1,0:T(8,128)(2,1)}, u32[]{:S(2)}) copy-start(bf16[8,4096]{1,0:T(8,128)(2,1)} %param.18) | copy-start | bytes 196612
  11.5 18.1 %copy-start.3 = (s32[3]{0:T(128)S(1)}, s32[3]{0:T(128)}, u32[]{:S(2)}) copy-start(s32[3]{0:T(128)} %constant.231.clone.1) | copy-start | bytes 40
  28.7 24.2 %collective-permute-start.1 = (bf16[2,128,2048]{2,0,1:T(2,128)(2,1)S(1)}, bf16[2,128,2048]{2,0,1:T(2,128)(2,1)}, u32[]{:S(2)}, u32[]{:S(2)}) collective-permute-start(bf16[2,128,2048]{2,0,1:T(2,128)(2,1)S(1)} %bitcast.96), channel_id=1, source_target_pairs={{1,0},{2,1},{3,2},{4,3},{5,4},{6,5},{7,6},{8,7},{9,8},{10,9},{11,1... | collective-permute-start | bytes 3145736 | tf_op jit(solution)/shard_map/ppermute | solution.py:16
  52.8 4.5 %copy-start.1 = (f32[8]{0:T(128)S(1)}, f32[8]{0:T(128)}, u32[]{:S(2)}) copy-start(f32[8]{0:T(128)} %param.20) | copy-start | bytes 100
  52.8 4.5 %copy-start.2 = (s32[3]{0:T(128)S(1)}, s32[3]{0:T(128)}, u32[]{:S(2)}) copy-start(s32[3]{0:T(128)} %constant.239.clone.2) | copy-start | bytes 40
  52.8 4.5 %copy-start.4 = (s32[4]{0:T(128)S(1)}, s32[4]{0:T(128)}, u32[]{:S(2)}) copy-start(s32[4]{0:T(128)} %param.21) | copy-start | bytes 52
  52.9 4.5 %copy-start.5 = (s32[4]{0:T(128)S(1)}, s32[4]{0:T(128)}, u32[]{:S(2)}) copy-start(s32[4]{0:T(128)} %param.22) | copy-start | bytes 52
  52.9 4.5 %copy-start.6 = (f32[8]{0:T(128)S(1)}, f32[8]{0:T(128)}, u32[]{:S(2)}) copy-start(f32[8]{0:T(128)} %param.19) | copy-start | bytes 100
  202.6 7.3 %collective-permute-start.2 = (f32[2,8,2048]{2,1,0:T(8,128)S(1)}, f32[2,8,2048]{2,1,0:T(8,128)S(1)}, u32[]{:S(2)}, u32[]{:S(2)}) collective-permute-start(f32[2,8,2048]{2,1,0:T(8,128)S(1)} %slice.80), channel_id=1, source_target_pairs={{127,0},{0,1},{1,2},{2,3},{3,4},{4,5},{5,6},{6,7},{7,8},{8,9},{9,1... | collective-permute-start | bytes 393224 | tf_op jit(solution)/shard_map/ppermute | solution.py:16
where the time goes:
time: 211 us
  matrix products  155 us (73%)
  other arithmetic  16.8 us (8%)
  loops' own time  12.8 us (6%)
  local copies, waits for them, and re-layouts  9.43 us (4%)
  starting transfers between devices  8.99 us (4%)
  waiting for transfers between devices  7.25 us (3%)
    dot_general x5, matrix products, taper_tile(): lax.dot_general(left_basis, right_basis, (((0,), (0,)), ((), ())), precis...  79.9 us
    dot_general x4, matrix products, make_tile(): lax.dot_general(first_x, second_x, (((0,), (0,)), ((), ())), preferred_el...  34.7 us
    dot_general x6, matrix products, apply_first(): lax.dot_general(second_v, tile, (((1,), (1,)), ((), ())), preferred_eleme...  32.9 us
    another operation x1, loops' own time, body(): totals = lax.fori_loop(0, pair_count[0], pairwise, totals)  12.8 us
    dot_general x4, matrix products, apply_second(): return jnp.dot(first_v, tile, preferred_element_type=jnp.float32)  7.58 us
    ppermute x3, waiting for transfers between devices, shifted(): return lax.ppermute(block, axis, route)  7.25 us
    ppermute x3, starting transfers between devices, shifted(): return lax.ppermute(block, axis, route)  4.81 us
    reduce_sum x4, other arithmetic, taper(): return jnp.sum(jnp.where(class_ids == klass, taper_table, jnp.float32(0.0)))  4.76 us
  transfers between devices with their start and end apart: 4, of which 1 were waited for; matrix products, arithmetic and copies ran while one was open for 19% of the time, Pallas kernels for 0%

commit v1 on v0

v1 whole, which is shorter than its diff:
```python
import functools
import math

import jax
import jax.numpy as jnp
import numpy as np
from jax import lax
from jax.experimental import pallas as pl
from jax.experimental.pallas import tpu as pltpu
from jax.sharding import PartitionSpec as P

BLOCK = 2048
MODES = 8
RANK = 2 * MODES
COLS = 8
LANES = 128
PERIOD = 12288
PAIR = 2
NCODE = 4
TAIL = 256
F32 = jnp.float32
BF16 = jnp.bfloat16


def basis_table():
    turn = np.outer(np.arange(MODES), np.arange(BLOCK)) % PERIOD
    angle = turn * (2.0 * math.pi / PERIOD)
    return np.concatenate([np.cos(angle), np.sin(angle)], 0).astype(np.float32)


def turn_table():
    mode = (np.arange(LANES) // COLS) % MODES
    sign = np.where(np.arange(LANES) < LANES // 2, -1.0, 1.0)
    rows = []
    for o in (1, 2):
        angle = ((mode * o * BLOCK) % PERIOD) * (2.0 * math.pi / PERIOD)
        rows += [np.cos(angle), np.sin(angle) * sign]
    rows += [np.zeros(LANES)] * 4
    return np.stack(rows).astype(np.float32)


def split(value):
    high = value.astype(BF16)
    low = (value - high.astype(F32)).astype(BF16)
    return high, low


def turned(value, turns, o, back):
    c = turns[2 * o - 2 : 2 * o - 1, :]
    s = turns[2 * o - 1 : 2 * o, :]
    other = pltpu.roll(value, LANES // 2, 1)
    return value * c - other * s if back else value * c + other * s


def message_kernel(code, klass, count, table, v_ref, out_ref):
    n = v_ref.shape[1]
    out_ref[:, :n] = v_ref[...]
    row = lax.broadcasted_iota(jnp.int32, (8, LANES), 0)
    w = jnp.zeros((8, LANES), F32)
    for slot in range(NCODE):
        rho = jnp.where(slot < count[0], table[klass[slot]], F32(0.0))
        w = w + jnp.where(row % NCODE == code[slot], rho, F32(0.0))
    high, low = split(w)
    rest = (w - high.astype(F32) - low.astype(F32)).astype(BF16)
    first = row < NCODE
    out_ref[:, n : n + LANES] = jnp.where(first, high.astype(F32), low.astype(F32)).astype(BF16)
    out_ref[:, n + LANES :] = rest


def weights_of(msg_ref):
    n = msg_ref.shape[1] - TAIL
    both = msg_ref[:, n : n + LANES].astype(F32)
    rest = msg_ref[:, n + LANES :].astype(F32)
    return both[:NCODE] + both[NCODE:] + rest[:NCODE]


def project(x, v, basis):
    wide = (basis[:, None, :] * v[None, :, :].astype(F32)).reshape(RANK * COLS, v.shape[1])
    high, low = split(wide)
    both = jnp.concatenate([high, low], 0)
    out = lax.dot_general(x, both, (((1,), (1,)), ((), ())), preferred_element_type=F32)
    return out[:, :LANES] + out[:, LANES:]


def project_kernel(x_ref, m0, m1, m2, m3, basis_ref, turns_ref, z_ref, zp_ref, um_ref, w_ref, u_sc, w_sc):
    me = lax.axis_index("mem")
    basis = basis_ref[...]
    for d, msg in enumerate((m0, m1, m2, m3)):
        src = (me + 4 - d) & 3
        w_sc[src] = weights_of(msg)
        for j in range(PAIR):
            k = src * PAIR + j
            x = x_ref[:, pl.ds(pl.multiple_of(k * BLOCK, BLOCK), BLOCK)]
            u_sc[k] = project(x, msg[:, j * BLOCK : (j + 1) * BLOCK], basis)
    turns = turns_ref[...]
    nblk = u_sc.shape[0]

    def rho(k, o):
        c = (k % PAIR) * PAIR + o - 1
        return w_sc[k // PAIR][c : c + 1, :]

    for k in range(nblk):
        z = u_sc[k]
        for o in (1, 2):
            if k + o < nblk:
                z = z + turned(u_sc[k + o], turns, o, False) * rho(k, o)
            if k - o >= 0:
                z = z + turned(u_sc[k - o], turns, o, True) * rho(k - o, o)
        z_ref[k] = z
    last = nblk - 1
    zp_ref[0] = turned(u_sc[last - 1], turns, 2, True) * rho(last - 1, 2) + turned(
        u_sc[last], turns, 1, True
    ) * rho(last, 1)
    zp_ref[1] = turned(u_sc[last], turns, 2, True) * rho(last, 2)
    um_ref[0] = u_sc[0]
    um_ref[1] = u_sc[1]
    w_ref[...] = w_sc[nblk // PAIR - 1]


def expand_kernel(modes, x_ref, z_ref, zin_ref, uin_ref, w_ref, basis_ref, turns_ref, *rest):
    outs, (z_sc, l_sc) = rest[:-2], rest[-2:]
    me = lax.axis_index("mem")
    scale = F32(1.0 / 127.0)
    for r in range(RANK):
        l_sc[r : r + 1, :] = basis_ref[r : r + 1, :] * (modes[r % MODES] * scale)
    turns = turns_ref[...]
    nblk = z_ref.shape[0]
    z_sc[...] = z_ref[...]
    z_sc[0] = z_sc[0] + zin_ref[0]
    z_sc[1] = z_sc[1] + zin_ref[1]
    last = nblk - 1
    z_sc[last - 1] = z_sc[last - 1] + turned(uin_ref[0], turns, 2, False) * w_ref[1:2, :]
    z_sc[last] = (
        z_sc[last]
        + turned(uin_ref[0], turns, 1, False) * w_ref[2:3, :]
        + turned(uin_ref[1], turns, 2, False) * w_ref[3:4, :]
    )
    left = l_sc[...]
    for d, out in enumerate(outs):
        tgt = (me + d) & 3
        for j in range(PAIR):
            k = tgt * PAIR + j
            x = x_ref[:, pl.ds(pl.multiple_of(k * BLOCK, BLOCK), BLOCK)]
            high, low = split(z_sc[k])
            t = lax.dot_general(
                jnp.concatenate([high, low], 0),
                jnp.concatenate([x, x], 0),
                (((0,), (0,)), ((), ())),
                preferred_element_type=F32,
            )
            out[:, j * BLOCK : (j + 1) * BLOCK] = jnp.sum(
                t.reshape(RANK, COLS, BLOCK) * left[:, None, :], axis=0
            )


def route(n, distance):
    return [((i - distance) % n, i) for i in range(n)]


VM = pl.BlockSpec(memory_space=pltpu.VMEM)
SM = pl.BlockSpec(memory_space=pltpu.SMEM)
LIMIT = pltpu.CompilerParams(vmem_limit_bytes=40 * 1024 * 1024)


def body(anomalies, increments, taper_table, taper_modes, pair_code, pair_class, pair_count):
    members, wide = anomalies.shape
    cols, width = increments.shape
    nmem = lax.axis_size("mem")
    nblk = wide // BLOCK
    basis = jnp.asarray(basis_table())
    turns = jnp.asarray(turn_table())
    msg = pl.pallas_call(
        message_kernel,
        out_shape=jax.ShapeDtypeStruct((cols, width + TAIL), BF16),
        in_specs=[SM, SM, SM, SM, VM],
        out_specs=VM,
        name="message",
    )(pair_code, pair_class, pair_count, taper_table, increments)
    msgs = [msg] + [lax.ppermute(msg, "mem", route(nmem, d)) for d in range(1, nmem)]
    shape = jax.ShapeDtypeStruct
    z, zp, um, w = pl.pallas_call(
        project_kernel,
        out_shape=[
            shape((nblk, members, LANES), F32),
            shape((PAIR, members, LANES), F32),
            shape((PAIR, members, LANES), F32),
            shape((NCODE, LANES), F32),
        ],
        in_specs=[VM] * 7,
        out_specs=[VM] * 4,
        scratch_shapes=[
            pltpu.VMEM((nblk, members, LANES), F32),
            pltpu.VMEM((nmem, NCODE, LANES), F32),
        ],
        compiler_params=LIMIT,
        name="project",
    )(anomalies, *msgs, basis, turns)
    nb = lax.axis_size("blk")
    zin = lax.ppermute(zp, "blk", route(nb, 1))
    uin = lax.ppermute(um, "blk", route(nb, -1))
    outs = pl.pallas_call(
        expand_kernel,
        out_shape=[shape((cols, width), F32)] * nmem,
        in_specs=[SM] + [VM] * 7,
        out_specs=[VM] * nmem,
        scratch_shapes=[
            pltpu.VMEM((nblk, members, LANES), F32),
            pltpu.VMEM((RANK, BLOCK), F32),
        ],
        compiler_params=LIMIT,
        name="expand",
    )(taper_modes, anomalies, z, zin, uin, w, basis, turns)
    total = outs[0]
    for d in range(1, nmem):
        total = total + lax.ppermute(outs[d], "mem", route(nmem, d))
    return total


def solution(mesh):
    in_specs = (
        P("mem", "blk"),
        P(None, ("blk", "mem")),
        P(),
        P(),
        P(("blk", "mem")),
        P(("blk", "mem")),
        P(("blk", "mem")),
    )
    out_specs = P(None, ("blk", "mem"))
    return jax.shard_map(body, mesh=mesh, in_specs=in_specs, out_specs=out_specs, check_vma=False)
```

time: 211 us -> 36.4 us (0.17)
  the two profiles are of different devices: /device:TPU:5 before, /device:TPU:0 now
where the time goes in v1:
time: 36.4 us; the launch traced here: 36.2 us
  starting transfers between devices  13.7 us (38%)
  waiting for transfers between devices  12 us (33%)
  Pallas kernels  6.23 us (17%)
  local copies, waits for them, and re-layouts  2.77 us (8%)
  between operations  0.74 us (2%)
  other arithmetic  0.7 us (2%)
    ppermute x3, waiting for transfers between devices, body(): lax.ppermute(msg, 'mem', route(nmem, d))  5.24 us
    ppermute x3, waiting for transfers between devices, body(): total = total + lax.ppermute(outs[d], 'mem', route(nmem, d))  5.17 us
    ppermute x1, starting transfers between devices, body(): uin = lax.ppermute(um, 'blk', route(nb, -1))  5.05 us
    ppermute x3, starting transfers between devices, body(): lax.ppermute(msg, 'mem', route(nmem, d))  4.7 us
    ppermute x3, starting transfers between devices, body(): total = total + lax.ppermute(outs[d], 'mem', route(nmem, d))  3.9 us
    pallas_call x1, Pallas kernels, body(): pl.pallas_call(project_kernel, out_shape=[shape((nblk, members, LANES), F...  2.82 us
    unnamed x12, local copies, waits for them, and re-layouts  2.77 us
    pallas_call x1, Pallas kernels, body(): pl.pallas_call(expand_kernel, out_shape=[shape((cols, width), F32)] * nme...  1.9 us
  transfers between devices with their start and end apart: 8, of which 6 were waited for; matrix products, arithmetic and copies ran while one was open for 0% of the time, Pallas kernels for 0%

profile of v1, /device:TPU:0, one launch (start us, length us, event | category | flops | bytes accessed | tf_op | source)
XLA Modules:
  0.0 36.2 jit_solution(6811245405006150024)
XLA Ops:
  0.0 0.0 copy-start.2
  0.7 0.0 copy-start.4
  0.7 1.5 %message.1.m0 = bf16[8,4352]{1,0:T(8,128)(2,1)} custom-call(s32[4]{0:T(128)} %code.1, s32[4]{0:T(128)} %klass.1, s32[1]{0:T(128)S(6)} %copy.10.count, f32[8]{0:T(128)} %table.1, bf16[8,4096]{1,0:T(8,128)(2,1)} %v_ref.1), custom_call_target="tpu_custom_call" | custom-call | tf_op jit(solution)/shard_map/message/pallas_call | solution.py:172
  2.2 3.1 %collective-permute-start.2 = (bf16[8,4352]{1,0:T(8,128)(2,1)}, bf16[8,4352]{1,0:T(8,128)(2,1)S(1)}, u32[]{:S(2)}, u32[]{:S(2)}) collective-permute-start(bf16[8,4352]{1,0:T(8,128)(2,1)} %message.1.m0), channel_id=1, source_target_pairs={{1,0},{2,1},{3,2},{0,3},{5,4},{6,5},{7,6},{4,7},{9,8},{10,9},{11,1... | collective-permute-start | bytes 208904 | tf_op jit(solution)/shard_map/ppermute | solution.py:179
  5.3 0.6 %collective-permute-start.1 = (bf16[8,4352]{1,0:T(8,128)(2,1)}, bf16[8,4352]{1,0:T(8,128)(2,1)S(1)}, u32[]{:S(2)}, u32[]{:S(2)}) collective-permute-start(bf16[8,4352]{1,0:T(8,128)(2,1)} %message.1.m0), channel_id=1, source_target_pairs={{2,0},{3,1},{0,2},{1,3},{6,4},{7,5},{4,6},{5,7},{10,8},{11,9},{8,1... | collective-permute-start | bytes 208904 | tf_op jit(solution)/shard_map/ppermute | solution.py:179
  5.9 1.0 %collective-permute-start = (bf16[8,4352]{1,0:T(8,128)(2,1)}, bf16[8,4352]{1,0:T(8,128)(2,1)S(1)}, u32[]{:S(2)}, u32[]{:S(2)}) collective-permute-start(bf16[8,4352]{1,0:T(8,128)(2,1)} %message.1.m0), channel_id=1, source_target_pairs={{3,0},{0,1},{1,2},{2,3},{7,4},{4,5},{5,6},{6,7},{11,8},{8,9},{9,10... | collective-permute-start | bytes 208904 | tf_op jit(solution)/shard_map/ppermute | solution.py:179
  6.9 0.9 %collective-permute-done.2.m3 = bf16[8,4352]{1,0:T(8,128)(2,1)S(1)} collective-permute-done((bf16[8,4352]{1,0:T(8,128)(2,1)}, bf16[8,4352]{1,0:T(8,128)(2,1)S(1)}, u32[]{:S(2)}, u32[]{:S(2)}) %collective-permute-start.2) | collective-permute-done | bytes 69664 | tf_op jit(solution)/shard_map/ppermute | solution.py:179
  7.8 3.6 %collective-permute-done.1.m2 = bf16[8,4352]{1,0:T(8,128)(2,1)S(1)} collective-permute-done((bf16[8,4352]{1,0:T(8,128)(2,1)}, bf16[8,4352]{1,0:T(8,128)(2,1)S(1)}, u32[]{:S(2)}, u32[]{:S(2)}) %collective-permute-start.1) | collective-permute-done | bytes 69664 | tf_op jit(solution)/shard_map/ppermute | solution.py:179
  11.5 0.7 %collective-permute-done.m1 = bf16[8,4352]{1,0:T(8,128)(2,1)S(1)} collective-permute-done((bf16[8,4352]{1,0:T(8,128)(2,1)}, bf16[8,4352]{1,0:T(8,128)(2,1)S(1)}, u32[]{:S(2)}, u32[]{:S(2)}) %collective-permute-start) | collective-permute-done | bytes 69664 | tf_op jit(solution)/shard_map/ppermute | solution.py:179
  12.2 0.0 copy-done.2
  12.2 0.0 copy-done.4
  12.2 0.0 copy-start
  12.2 1.2 %copy-done = bf16[32,16384]{1,0:T(8,128)(2,1)S(1)} copy-done((bf16[32,16384]{1,0:T(8,128)(2,1)S(1)}, bf16[32,16384]{1,0:T(8,128)(2,1)}, u32[]{:S(2)}) %copy-start) | copy-done | bytes 1048600
  13.4 0.0 copy-start.3
  13.4 0.9 %copy-done.3 = bf16[8,4352]{1,0:T(8,128)(2,1)S(1)} copy-done((bf16[8,4352]{1,0:T(8,128)(2,1)S(1)}, bf16[8,4352]{1,0:T(8,128)(2,1)}, u32[]{:S(2)}) %copy-start.3) | copy-done | bytes 69656
  14.3 0.0 copy-start.1
  14.3 2.8 %project.1 = (f32[8,32,128]{2,1,0:T(8,128)S(1)}, f32[2,32,128]{2,1,0:T(8,128)S(1)}, f32[2,32,128]{2,1,0:T(8,128)S(1)}, f32[4,128]{1,0:T(4,128)S(1)}) custom-call(bf16[32,16384]{1,0:T(8,128)(2,1)S(1)} %copy-done, bf16[8,4352]{1,0:T(8,128)(2,1)S(1)} %copy-done.3, bf16[8,4352]{1,0:T(8,128)(2,1)S(1)} %collective-permute-done.m1, ...), custom_call_target="tpu_custom_call" | custom-call | tf_op jit(solution)/shard_map/project/pallas_call | solution.py:181
  17.1 0.1 collective-permute-start.3
  17.2 5.1 %collective-permute-start.4 = (f32[2,32,128]{2,1,0:T(8,128)S(1)}, f32[2,32,128]{2,1,0:T(8,128)S(1)}, u32[]{:S(2)}, u32[]{:S(2)}) collective-permute-start(f32[2,32,128]{2,1,0:T(8,128)S(1)} %get-tuple-element.15), channel_id=1, source_target_pairs={{4,0},{8,4},{12,8},{16,12},{20,16},{24,20},{28,24},{32,28},{36,32}... | collective-permute-start | bytes 98312 | tf_op jit(solution)/shard_map/ppermute | solution.py:200
  22.2 1.6 %collective-permute-done.3.zin_ref = f32[2,32,128]{2,1,0:T(8,128)S(1)} collective-permute-done((f32[2,32,128]{2,1,0:T(8,128)S(1)}, f32[2,32,128]{2,1,0:T(8,128)S(1)}, u32[]{:S(2)}, u32[]{:S(2)}) %collective-permute-start.3) | collective-permute-done | bytes 32800 | tf_op jit(solution)/shard_map/ppermute | solution.py:199
  23.8 0.0 collective-permute-done.4.uin_ref
  23.8 0.0 copy-start.5
  23.8 0.0 copy-done.1
  23.8 0.6 %copy-done.5 = f32[8]{0:T(128)S(1)} copy-done((f32[8]{0:T(128)S(1)}, f32[8]{0:T(128)}, u32[]{:S(2)}) %copy-start.5) | copy-done | bytes 56
  24.5 1.9 %expand.1 = (f32[8,4096]{1,0:T(8,128)S(1)}, f32[8,4096]{1,0:T(8,128)S(1)}, f32[8,4096]{1,0:T(8,128)S(1)}, f32[8,4096]{1,0:T(8,128)S(1)}) custom-call(f32[8]{0:T(128)S(1)} %copy-done.5, bf16[32,16384]{1,0:T(8,128)(2,1)S(1)} %copy-done.1, f32[8,32,128]{2,1,0:T(8,128)S(1)} %get-tuple-element.13.z_ref, f32[2,32,128]{2,1,0:T(8,128)S(1)} %collective-permute-done.3.zin_ref, ...), custom_call_target="tpu_custom_call" | custom-call | tf_op jit(solution)/shard_map/expand/pallas_call | solution.py:201
  26.4 0.1 collective-permute-start.5
  26.5 2.0 %collective-permute-start.6 = (f32[8,4096]{1,0:T(8,128)S(1)}, f32[8,4096]{1,0:T(8,128)S(1)}, u32[]{:S(2)}, u32[]{:S(2)}) collective-permute-start(f32[8,4096]{1,0:T(8,128)S(1)} %get-tuple-element.19), channel_id=1, source_target_pairs={{2,0},{3,1},{0,2},{1,3},{6,4},{7,5},{4,6},{5,7},{10,8},{11,9},{8,1... | collective-permute-start | bytes 393224 | tf_op jit(solution)/shard_map/ppermute | solution.py:215
  28.5 1.8 %collective-permute-start.7 = (f32[8,4096]{1,0:T(8,128)S(1)}, f32[8,4096]{1,0:T(8,128)S(1)}, u32[]{:S(2)}, u32[]{:S(2)}) collective-permute-start(f32[8,4096]{1,0:T(8,128)S(1)} %get-tuple-element.20), channel_id=1, source_target_pairs={{1,0},{2,1},{3,2},{0,3},{5,4},{6,5},{7,6},{4,7},{9,8},{10,9},{11,1... | collective-permute-start | bytes 393224 | tf_op jit(solution)/shard_map/ppermute | solution.py:215
  30.3 4.6 %collective-permute-done.5 = f32[8,4096]{1,0:T(8,128)S(1)} collective-permute-done((f32[8,4096]{1,0:T(8,128)S(1)}, f32[8,4096]{1,0:T(8,128)S(1)}, u32[]{:S(2)}, u32[]{:S(2)}) %collective-permute-start.5) | collective-permute-done | bytes 131104 | tf_op jit(solution)/shard_map/ppermute | solution.py:215
  34.9 0.0 collective-permute-done.6
  34.9 0.6 %collective-permute-done.7 = f32[8,4096]{1,0:T(8,128)S(1)} collective-permute-done((f32[8,4096]{1,0:T(8,128)S(1)}, f32[8,4096]{1,0:T(8,128)S(1)}, u32[]{:S(2)}, u32[]{:S(2)}) %collective-permute-start.7) | collective-permute-done | bytes 131104 | tf_op jit(solution)/shard_map/ppermute | solution.py:215
  35.5 0.7 %add_add_fusion = f32[8,4096]{1,0:T(8,128)} fusion(f32[8,4096]{1,0:T(8,128)S(1)} %collective-permute-done.7, f32[8,4096]{1,0:T(8,128)S(1)} %collective-permute-done.6, f32[8,4096]{1,0:T(8,128)S(1)} %get-tuple-element.17, f32[8,4096]{1,0:T(8,128)S(1)} %collective-permute-done.5), kind=kLoop, calls=%fused_computation | loop fusion | flops 98304 | bytes 655360 | tf_op jit(solution)/shard_map/add | solution.py:215
Async XLA Ops:
  0.0 12.2 %copy-start.2 = (f32[16,2048]{1,0:T(8,128)S(1)}, f32[16,2048]{1,0:T(8,128)}, u32[]{:S(2)}) copy-start(f32[16,2048]{1,0:T(8,128)} %constant.4.clone.basis_ref) | copy-start | bytes 393220
  0.7 11.5 %copy-start.4 = (f32[8,128]{1,0:T(8,128)S(1)}, f32[8,128]{1,0:T(8,128)}, u32[]{:S(2)}) copy-start(f32[8,128]{1,0:T(8,128)} %constant.5.clone.turns_ref) | copy-start | bytes 12292
  2.2 5.6 %collective-permute-start.2 = (bf16[8,4352]{1,0:T(8,128)(2,1)}, bf16[8,4352]{1,0:T(8,128)(2,1)S(1)}, u32[]{:S(2)}, u32[]{:S(2)}) collective-permute-start(bf16[8,4352]{1,0:T(8,128)(2,1)} %message.1.m0), channel_id=1, source_target_pairs={{1,0},{2,1},{3,2},{0,3},{5,4},{6,5},{7,6},{4,7},{9,8},{10,9},{11,1... | collective-permute-start | bytes 208904 | tf_op jit(solution)/shard_map/ppermute | solution.py:179
  5.3 6.2 %collective-permute-start.1 = (bf16[8,4352]{1,0:T(8,128)(2,1)}, bf16[8,4352]{1,0:T(8,128)(2,1)S(1)}, u32[]{:S(2)}, u32[]{:S(2)}) collective-permute-start(bf16[8,4352]{1,0:T(8,128)(2,1)} %message.1.m0), channel_id=1, source_target_pairs={{2,0},{3,1},{0,2},{1,3},{6,4},{7,5},{4,6},{5,7},{10,8},{11,9},{8,1... | collective-permute-start | bytes 208904 | tf_op jit(solution)/shard_map/ppermute | solution.py:179
  5.9 6.2 %collective-permute-start = (bf16[8,4352]{1,0:T(8,128)(2,1)}, bf16[8,4352]{1,0:T(8,128)(2,1)S(1)}, u32[]{:S(2)}, u32[]{:S(2)}) collective-permute-start(bf16[8,4352]{1,0:T(8,128)(2,1)} %message.1.m0), channel_id=1, source_target_pairs={{3,0},{0,1},{1,2},{2,3},{7,4},{4,5},{5,6},{6,7},{11,8},{8,9},{9,10... | collective-permute-start | bytes 208904 | tf_op jit(solution)/shard_map/ppermute | solution.py:179
  12.2 1.2 %copy-start = (bf16[32,16384]{1,0:T(8,128)(2,1)S(1)}, bf16[32,16384]{1,0:T(8,128)(2,1)}, u32[]{:S(2)}) copy-start(bf16[32,16384]{1,0:T(8,128)(2,1)} %x_ref.3) | copy-start | bytes 3145732
  13.4 0.9 %copy-start.3 = (bf16[8,4352]{1,0:T(8,128)(2,1)S(1)}, bf16[8,4352]{1,0:T(8,128)(2,1)}, u32[]{:S(2)}) copy-start(bf16[8,4352]{1,0:T(8,128)(2,1)} %message.1.m0) | copy-start | bytes 208900
  14.3 9.6 %copy-start.1 = (bf16[32,16384]{1,0:T(8,128)(2,1)S(1)}, bf16[32,16384]{1,0:T(8,128)(2,1)}, u32[]{:S(2)}) copy-start(bf16[32,16384]{1,0:T(8,128)(2,1)} %x_ref.3) | copy-start | bytes 3145732
  17.1 6.7 %collective-permute-start.3 = (f32[2,32,128]{2,1,0:T(8,128)S(1)}, f32[2,32,128]{2,1,0:T(8,128)S(1)}, u32[]{:S(2)}, u32[]{:S(2)}) collective-permute-start(f32[2,32,128]{2,1,0:T(8,128)S(1)} %get-tuple-element.14), channel_id=1, source_target_pairs={{124,0},{0,4},{4,8},{8,12},{12,16},{16,20},{20,24},{24,28},{28,32}... | collective-permute-start | bytes 98312 | tf_op jit(solution)/shard_map/ppermute | solution.py:199
  17.2 6.7 %collective-permute-start.4 = (f32[2,32,128]{2,1,0:T(8,128)S(1)}, f32[2,32,128]{2,1,0:T(8,128)S(1)}, u32[]{:S(2)}, u32[]{:S(2)}) collective-permute-start(f32[2,32,128]{2,1,0:T(8,128)S(1)} %get-tuple-element.15), channel_id=1, source_target_pairs={{4,0},{8,4},{12,8},{16,12},{20,16},{24,20},{28,24},{32,28},{36,32}... | collective-permute-start | bytes 98312 | tf_op jit(solution)/shard_map/ppermute | solution.py:200
  23.8 0.7 %copy-start.5 = (f32[8]{0:T(128)S(1)}, f32[8]{0:T(128)}, u32[]{:S(2)}) copy-start(f32[8]{0:T(128)} %modes.1) | copy-start | bytes 100
  26.4 8.5 %collective-permute-start.5 = (f32[8,4096]{1,0:T(8,128)S(1)}, f32[8,4096]{1,0:T(8,128)S(1)}, u32[]{:S(2)}, u32[]{:S(2)}) collective-permute-start(f32[8,4096]{1,0:T(8,128)S(1)} %get-tuple-element.18), channel_id=1, source_target_pairs={{3,0},{0,1},{1,2},{2,3},{7,4},{4,5},{5,6},{6,7},{11,8},{8,9},{9,10... | collective-permute-start | bytes 393224 | tf_op jit(solution)/shard_map/ppermute | solution.py:215
  26.5 8.4 %collective-permute-start.6 = (f32[8,4096]{1,0:T(8,128)S(1)}, f32[8,4096]{1,0:T(8,128)S(1)}, u32[]{:S(2)}, u32[]{:S(2)}) collective-permute-start(f32[8,4096]{1,0:T(8,128)S(1)} %get-tuple-element.19), channel_id=1, source_target_pairs={{2,0},{3,1},{0,2},{1,3},{6,4},{7,5},{4,6},{5,7},{10,8},{11,9},{8,1... | collective-permute-start | bytes 393224 | tf_op jit(solution)/shard_map/ppermute | solution.py:215
  28.5 7.0 %collective-permute-start.7 = (f32[8,4096]{1,0:T(8,128)S(1)}, f32[8,4096]{1,0:T(8,128)S(1)}, u32[]{:S(2)}, u32[]{:S(2)}) collective-permute-start(f32[8,4096]{1,0:T(8,128)S(1)} %get-tuple-element.20), channel_id=1, source_target_pairs={{1,0},{2,1},{3,2},{0,3},{5,4},{6,5},{7,6},{4,7},{9,8},{10,9},{11,1... | collective-permute-start | bytes 393224 | tf_op jit(solution)/shard_map/ppermute | solution.py:215

commit v2 on v1

v2 whole, which is shorter than its diff:
```python
import functools
import math

import jax
import jax.numpy as jnp
import numpy as np
from jax import lax
from jax.experimental import pallas as pl
from jax.experimental.pallas import tpu as pltpu
from jax.sharding import PartitionSpec as P

BLOCK = 2048
MODES = 8
RANK = 2 * MODES
COLS = 8
LANES = 128
PERIOD = 12288
PAIR = 2
NCODE = 4
TAIL = 256
F32 = jnp.float32
BF16 = jnp.bfloat16


def basis_table():
    turn = np.outer(np.arange(MODES), np.arange(BLOCK)) % PERIOD
    angle = turn * (2.0 * math.pi / PERIOD)
    return np.concatenate([np.cos(angle), np.sin(angle)], 0).astype(np.float32)


def turn_table():
    mode = (np.arange(LANES) // COLS) % MODES
    sign = np.where(np.arange(LANES) < LANES // 2, -1.0, 1.0)
    rows = []
    for o in (1, 2):
        angle = ((mode * o * BLOCK) % PERIOD) * (2.0 * math.pi / PERIOD)
        rows += [np.cos(angle), np.sin(angle) * sign]
    rows += [np.zeros(LANES)] * 4
    return np.stack(rows).astype(np.float32)


def split(value):
    high = value.astype(BF16)
    low = (value - high.astype(F32)).astype(BF16)
    return high, low


def turned(value, turns, o, back):
    c = turns[2 * o - 2 : 2 * o - 1, :]
    s = turns[2 * o - 1 : 2 * o, :]
    other = pltpu.roll(value, LANES // 2, 1)
    return value * c - other * s if back else value * c + other * s


def message_kernel(code_ref, klass_ref, table_ref, v_ref, count_ref, out_ref, code, klass, table, tail, sems):
    n = v_ref.shape[1]
    body = pltpu.make_async_copy(v_ref, out_ref.at[:, :n], sems.at[0])
    body.start()
    pairs = ((code_ref, code), (klass_ref, klass), (table_ref, table))
    copies = [pltpu.make_async_copy(a, b, sems.at[i + 1]) for i, (a, b) in enumerate(pairs)]
    for c in copies:
        c.start()
    for c in copies:
        c.wait()
    row = lax.broadcasted_iota(jnp.int32, (8, LANES), 0)
    listed = jnp.broadcast_to(count_ref[...].reshape(1, 1), (8, LANES))
    w = jnp.zeros((8, LANES), F32)
    for slot in range(NCODE):
        hit = (row % NCODE == code[slot]) & (slot < listed)
        w = w + jnp.where(hit, table[klass[slot]], F32(0.0))
    high, low = split(w)
    rest = (w - high.astype(F32) - low.astype(F32)).astype(BF16)
    first = row < NCODE
    tail[:, :LANES] = jnp.where(first, high.astype(F32), low.astype(F32)).astype(BF16)
    tail[:, LANES:] = rest
    end = pltpu.make_async_copy(tail, out_ref.at[:, n:], sems.at[4])
    end.start()
    end.wait()
    body.wait()


def weights_of(msg_ref):
    n = msg_ref.shape[1] - TAIL
    both = msg_ref[:, n : n + LANES].astype(F32)
    rest = msg_ref[:, n + LANES :].astype(F32)
    return both[:NCODE] + both[NCODE:] + rest[:NCODE]


def project(x, v, basis):
    wide = (basis[:, None, :] * v[None, :, :].astype(F32)).reshape(RANK * COLS, v.shape[1])
    high, low = split(wide)
    both = jnp.concatenate([high, low], 0)
    out = lax.dot_general(x, both, (((1,), (1,)), ((), ())), preferred_element_type=F32)
    return out[:, :LANES] + out[:, LANES:]


def project_chunk(x_ref, v_ref, basis_ref, member, u_ref):
    for j in range(PAIR):
        k = member * PAIR + j
        x = x_ref[:, pl.ds(pl.multiple_of(k * BLOCK, BLOCK), BLOCK)]
        u_ref[j] = project(x, v_ref[:, j * BLOCK : (j + 1) * BLOCK], basis_ref[...])


def stage_kernel(modes, x_hbm, msg_ref, basis_ref, x_ref, l_ref, u_ref, w_ref, sem):
    copy = pltpu.make_async_copy(x_hbm, x_ref, sem)
    copy.start()
    w_ref[...] = weights_of(msg_ref)
    scale = F32(1.0 / 127.0)
    for r in range(RANK):
        l_ref[r : r + 1, :] = basis_ref[r : r + 1, :] * (modes[r % MODES] * scale)
    copy.wait()
    project_chunk(x_ref, msg_ref, basis_ref, lax.axis_index("mem"), u_ref)


def project_kernel(distance, x_ref, msg_ref, basis_ref, u_ref, w_ref):
    w_ref[...] = weights_of(msg_ref)
    project_chunk(x_ref, msg_ref, basis_ref, lax.axis_index("mem") ^ distance, u_ref)


def combine_kernel(x_ref, msg_ref, u0, u1, u2, w0, w1, w2, basis_ref, turns_ref, z_ref, e_ref, o_ref, w_ref, u_sc, w_sc):
    me = lax.axis_index("mem")
    nblk = z_ref.shape[0]
    for d, (u, w) in enumerate(((u0, w0), (u1, w1), (u2, w2))):
        for j in range(PAIR):
            u_sc[(me ^ d) * PAIR + j] = u[j]
        w_sc[me ^ d] = w[...]
    w_sc[me ^ 3] = weights_of(msg_ref)
    project_chunk(x_ref, msg_ref, basis_ref, me ^ 3, u_sc.at[pl.ds((me ^ 3) * PAIR, PAIR)])
    turns = turns_ref[...]

    def rho(k, o):
        c = (k % PAIR) * PAIR + o - 1
        return w_sc[k // PAIR][c : c + 1, :]

    last = nblk - 1
    even = lax.axis_index("blk") % 2 == 0
    ahead = (
        turned(u_sc[last - 1], turns, 2, True) * rho(last - 1, 2) + turned(u_sc[last], turns, 1, True) * rho(last, 1),
        turned(u_sc[last], turns, 2, True) * rho(last, 2),
    )
    for j in range(PAIR):
        e_ref[j] = jnp.where(even, ahead[j], u_sc[j])
        o_ref[j] = jnp.where(even, u_sc[j], ahead[j])
    for k in range(nblk):
        z = u_sc[k]
        for o in (1, 2):
            if k + o < nblk:
                z = z + turned(u_sc[k + o], turns, o, False) * rho(k, o)
            if k - o >= 0:
                z = z + turned(u_sc[k - o], turns, o, True) * rho(k - o, o)
        z_ref[k] = z
    w_ref[...] = w_sc[nblk // PAIR - 1]


def expand_kernel(x_ref, z_ref, ein_ref, oin_ref, w_ref, l_ref, turns_ref, *rest):
    outs, z_sc = rest[:-1], rest[-1]
    me = lax.axis_index("mem")
    turns = turns_ref[...]
    nblk = z_ref.shape[0]
    even = lax.axis_index("blk") % 2 == 0
    zin = [jnp.where(even, oin_ref[j], ein_ref[j]) for j in range(PAIR)]
    uin = [jnp.where(even, ein_ref[j], oin_ref[j]) for j in range(PAIR)]
    z_sc[...] = z_ref[...]
    z_sc[0] = z_sc[0] + zin[0]
    z_sc[1] = z_sc[1] + zin[1]
    last = nblk - 1
    z_sc[last - 1] = z_sc[last - 1] + turned(uin[0], turns, 2, False) * w_ref[1:2, :]
    z_sc[last] = (
        z_sc[last]
        + turned(uin[0], turns, 1, False) * w_ref[2:3, :]
        + turned(uin[1], turns, 2, False) * w_ref[3:4, :]
    )
    left = l_ref[...]
    for d, out in enumerate(outs):
        for j in range(PAIR):
            k = (me ^ d) * PAIR + j
            x = x_ref[:, pl.ds(pl.multiple_of(k * BLOCK, BLOCK), BLOCK)]
            high, low = split(z_sc[k])
            t = lax.dot_general(
                jnp.concatenate([high, low], 0),
                jnp.concatenate([x, x], 0),
                (((0,), (0,)), ((), ())),
                preferred_element_type=F32,
            )
            total = jnp.sum(t.reshape(RANK, COLS, BLOCK) * left[:, None, :], axis=0)
            out[:, j * BLOCK : (j + 1) * BLOCK] = total.astype(out.dtype)


def crossed(n, distance):
    return [(i ^ distance, i) for i in range(n)]


def partner(n, odd):
    pairs = [((2 * i + odd) % n, (2 * i + 1 + odd) % n) for i in range(n // 2)]
    return pairs + [(b, a) for a, b in pairs]


VM = pl.BlockSpec(memory_space=pltpu.VMEM)
SM = pl.BlockSpec(memory_space=pltpu.SMEM)
ANY = pl.BlockSpec(memory_space=pl.ANY)
LIMIT = pltpu.CompilerParams(vmem_limit_bytes=40 * 1024 * 1024)


def body(anomalies, increments, taper_table, taper_modes, pair_code, pair_class, pair_count):
    members, wide = anomalies.shape
    cols, width = increments.shape
    nmem = lax.axis_size("mem")
    nblk = wide // BLOCK
    basis = jnp.asarray(basis_table())
    turns = jnp.asarray(turn_table())
    shape = jax.ShapeDtypeStruct
    scalars = (pair_code, pair_class, taper_table)
    msg = pl.pallas_call(
        message_kernel,
        out_shape=shape((cols, width + TAIL), BF16),
        in_specs=[ANY] * 4 + [VM],
        out_specs=ANY,
        scratch_shapes=[pltpu.SMEM(a.shape, a.dtype) for a in scalars]
        + [pltpu.VMEM((cols, TAIL), BF16), pltpu.SemaphoreType.DMA((5,))],
        compiler_params=pltpu.CompilerParams(vmem_limit_bytes=62 * 1024 * 1024),
        name="message",
    )(*scalars, increments, pair_count)
    msgs = {d: lax.ppermute(msg, "mem", crossed(nmem, d)) for d in (3, 2, 1)}
    chunk = shape((PAIR, members, LANES), F32)
    weights = shape((NCODE, LANES), F32)
    x, left, u0, w0 = pl.pallas_call(
        stage_kernel,
        out_shape=[shape(anomalies.shape, BF16), shape(basis.shape, F32), chunk, weights],
        in_specs=[SM, ANY, VM, VM],
        out_specs=[VM] * 4,
        scratch_shapes=[pltpu.SemaphoreType.DMA],
        compiler_params=LIMIT,
        name="stage",
    )(taper_modes, anomalies, msg, basis)
    u, w = {}, {}
    for d in (1, 2):
        u[d], w[d] = pl.pallas_call(
            functools.partial(project_kernel, d),
            out_shape=[chunk, weights],
            in_specs=[VM] * 3,
            out_specs=[VM] * 2,
            compiler_params=LIMIT,
            name=f"project_{d}",
        )(x, msgs[d], basis)
    z, e, o, w3 = pl.pallas_call(
        combine_kernel,
        out_shape=[shape((nblk, members, LANES), F32), chunk, chunk, weights],
        in_specs=[VM] * 10,
        out_specs=[VM] * 4,
        scratch_shapes=[pltpu.VMEM((nblk, members, LANES), F32), pltpu.VMEM((nmem, NCODE, LANES), F32)],
        compiler_params=LIMIT,
        name="combine",
    )(x, msgs[3], u0, u[1], u[2], w0, w[1], w[2], basis, turns)
    nb = lax.axis_size("blk")
    oin = lax.ppermute(o, "blk", partner(nb, 1))
    ein = lax.ppermute(e, "blk", partner(nb, 0))
    outs = pl.pallas_call(
        expand_kernel,
        out_shape=[shape((cols, width), F32)] + [shape((cols, width), BF16)] * (nmem - 1),
        in_specs=[VM] * 7,
        out_specs=[VM] * nmem,
        scratch_shapes=[pltpu.VMEM((nblk, members, LANES), F32)],
        compiler_params=LIMIT,
        name="expand",
    )(x, z, ein, oin, w3, left, turns)
    total = outs[0]
    for d in (3, 2, 1):
        total = total + lax.ppermute(outs[d], "mem", crossed(nmem, d)).astype(F32)
    return total


def solution(mesh):
    in_specs = (
        P("mem", "blk"),
        P(None, ("blk", "mem")),
        P(),
        P(),
        P(("blk", "mem")),
        P(("blk", "mem")),
        P(("blk", "mem")),
    )
    out_specs = P(None, ("blk", "mem"))
    return jax.shard_map(body, mesh=mesh, in_specs=in_specs, out_specs=out_specs, check_vma=False)
```

time: 36.4 us -> 34 us (0.934)
  waiting for transfers between devices: 12 us -> 6.17 us
  Pallas kernels: 6.23 us -> 8.31 us
  starting transfers between devices: 13.7 us -> 15 us
    ppermute x8, waiting for transfers between devices: 12 us -> 6.17 us  [the longest x3 4.23 us: body(): total = total + lax.ppermute(outs[d], 'mem', crossed(nmem, d)).astype(F32)]
    pallas_call x3 -> x6, Pallas kernels: 6.23 us -> 8.31 us  [the longest x1 3.13 us: body(): pl.pallas_call(message_kernel, out_shape=shape((cols, width + TAIL), BF16...]
    ppermute x8, starting transfers between devices: 13.7 us -> 15 us  [the longest x1 6.33 us: body(): oin = lax.ppermute(o, 'blk', partner(nb, 1))]
    unnamed x12 -> x10, local copies, waits for them, and re-layouts: 2.77 us -> 2.8 us
  transfers between devices with their start and end apart: 8 -> 8, of which waited for: 6 -> 4; matrix products, arithmetic and copies ran while one was open for 0% -> 0% of each run, Pallas kernels for 0% -> 9%
where the time goes in v2:
time: 34 us; the launch traced here: 33.7 us
  starting transfers between devices  15 us (44%)
  Pallas kernels  8.31 us (24%)
  waiting for transfers between devices  6.17 us (18%)
  local copies, waits for them, and re-layouts  2.8 us (8%)
  between operations  0.76 us (2%)
  other arithmetic  0.69 us (2%)
    ppermute x1, starting transfers between devices, body(): oin = lax.ppermute(o, 'blk', partner(nb, 1))  6.33 us
    ppermute x3, starting transfers between devices, body(): msgs = {d: lax.ppermute(msg, 'mem', crossed(nmem, d)) for d in (3, 2, 1)}  4.41 us
    ppermute x3, waiting for transfers between devices, body(): total = total + lax.ppermute(outs[d], 'mem', crossed(nmem, d)).astype(F32)  4.23 us
    ppermute x3, starting transfers between devices, body(): total = total + lax.ppermute(outs[d], 'mem', crossed(nmem, d)).astype(F32)  4.17 us
    pallas_call x1, Pallas kernels, body(): pl.pallas_call(message_kernel, out_shape=shape((cols, width + TAIL), BF16...  3.13 us
    unnamed x10, local copies, waits for them, and re-layouts  2.8 us
    ppermute x1, waiting for transfers between devices, body(): oin = lax.ppermute(o, 'blk', partner(nb, 1))  1.59 us
    pallas_call x2, Pallas kernels, body(): pl.pallas_call(functools.partial(project_kernel, d), out_shape=[chunk, we...  1.46 us
  transfers between devices with their start and end apart: 8, of which 4 were waited for; matrix products, arithmetic and copies ran while one was open for 0% of the time, Pallas kernels for 9%

profile of v2, /device:TPU:0, one launch (start us, length us, event | category | flops | bytes accessed | tf_op | source)
XLA Modules:
  0.0 33.7 jit_solution(11041471041537032899)
XLA Ops:
  0.0 0.0 copy-start
  0.7 0.0 copy-start.4
  0.7 3.1 %message.1.msg_ref = bf16[8,4352]{1,0:T(8,128)(2,1)} custom-call(s32[4]{0:T(128)} %code_ref.1, s32[4]{0:T(128)} %klass_ref.1, f32[8]{0:T(128)} %table_ref.1, bf16[8,4096]{1,0:T(8,128)(2,1)} %v_ref.1, s32[1]{0:T(128)S(6)} %copy.10.count_ref), custom_call_target="tpu_custom_call" | custom-call | tf_op jit(solution)/shard_map/message/pallas_call | solution.py:213
  3.8 3.4 %collective-permute-start.2 = (bf16[8,4352]{1,0:T(8,128)(2,1)}, bf16[8,4352]{1,0:T(8,128)(2,1)S(1)}, u32[]{:S(2)}, u32[]{:S(2)}) collective-permute-start(bf16[8,4352]{1,0:T(8,128)(2,1)} %message.1.msg_ref), channel_id=1, source_target_pairs={{2,0},{3,1},{0,2},{1,3},{6,4},{7,5},{4,6},{5,7},{10,8},{11,9},{8,1... | collective-permute-start | bytes 208904 | tf_op jit(solution)/shard_map/ppermute | solution.py:223
  7.2 0.7 %collective-permute-start.1 = (bf16[8,4352]{1,0:T(8,128)(2,1)}, bf16[8,4352]{1,0:T(8,128)(2,1)S(1)}, u32[]{:S(2)}, u32[]{:S(2)}) collective-permute-start(bf16[8,4352]{1,0:T(8,128)(2,1)} %message.1.msg_ref), channel_id=1, source_target_pairs={{1,0},{0,1},{3,2},{2,3},{5,4},{4,5},{7,6},{6,7},{9,8},{8,9},{11,10... | collective-permute-start | bytes 208904 | tf_op jit(solution)/shard_map/ppermute | solution.py:223
  7.9 0.4 %collective-permute-start = (bf16[8,4352]{1,0:T(8,128)(2,1)}, bf16[8,4352]{1,0:T(8,128)(2,1)S(1)}, u32[]{:S(2)}, u32[]{:S(2)}) collective-permute-start(bf16[8,4352]{1,0:T(8,128)(2,1)} %message.1.msg_ref), channel_id=1, source_target_pairs={{3,0},{2,1},{1,2},{0,3},{7,4},{6,5},{5,6},{4,7},{11,8},{10,9},{9,1... | collective-permute-start | bytes 208904 | tf_op jit(solution)/shard_map/ppermute | solution.py:223
  8.3 0.0 copy-done
  8.3 0.0 copy-done.4
  8.3 0.0 copy-start.1
  8.3 1.2 %copy-done.1 = bf16[32,16384]{1,0:T(8,128)(2,1)S(1)} copy-done((bf16[32,16384]{1,0:T(8,128)(2,1)S(1)}, bf16[32,16384]{1,0:T(8,128)(2,1)}, u32[]{:S(2)}) %copy-start.1) | copy-done | bytes 1048600
  9.5 0.0 copy-start.2
  9.5 0.9 %copy-done.2 = bf16[8,4352]{1,0:T(8,128)(2,1)S(1)} copy-done((bf16[8,4352]{1,0:T(8,128)(2,1)S(1)}, bf16[8,4352]{1,0:T(8,128)(2,1)}, u32[]{:S(2)}) %copy-start.2) | copy-done | bytes 69656
  10.4 1.4 %stage.1 = (bf16[32,16384]{1,0:T(8,128)(2,1)S(1)}, f32[16,2048]{1,0:T(8,128)S(1)}, f32[2,32,128]{2,1,0:T(8,128)S(1)}, f32[4,128]{1,0:T(4,128)S(1)}) custom-call(f32[8]{0:T(128)S(1)} %copy-done.4, bf16[32,16384]{1,0:T(8,128)(2,1)S(1)} %copy-done.1, bf16[8,4352]{1,0:T(8,128)(2,1)S(1)} %copy-done.2, f32[16,2048]{1,0:T(8,128)S(1)} %copy-done), custom_call_target="tpu_custom_call" | custom-call | tf_op jit(solution)/shard_map/stage/pallas_call | solution.py:226
  11.8 0.0 collective-permute-done.2.msg_ref
  11.8 0.7 %project_2.1 = (f32[2,32,128]{2,1,0:T(8,128)S(1)}, f32[4,128]{1,0:T(4,128)S(1)}) custom-call(bf16[32,16384]{1,0:T(8,128)(2,1)S(1)} %get-tuple-element.21.x_ref, bf16[8,4352]{1,0:T(8,128)(2,1)S(1)} %collective-permute-done.2.msg_ref, f32[16,2048]{1,0:T(8,128)S(1)} %copy-done), custom_call_target="tpu_custom_call" | custom-call | tf_op jit(solution)/shard_map/project_2/pallas_call | solution.py:237
  12.5 0.0 collective-permute-done.1.msg_ref
  12.5 0.7 %project_1.1 = (f32[2,32,128]{2,1,0:T(8,128)S(1)}, f32[4,128]{1,0:T(4,128)S(1)}) custom-call(bf16[32,16384]{1,0:T(8,128)(2,1)S(1)} %get-tuple-element.21.x_ref, bf16[8,4352]{1,0:T(8,128)(2,1)S(1)} %collective-permute-done.1.msg_ref, f32[16,2048]{1,0:T(8,128)S(1)} %copy-done), custom_call_target="tpu_custom_call" | custom-call | tf_op jit(solution)/shard_map/project_1/pallas_call | solution.py:237
  13.3 0.3 collective-permute-done.msg_ref
  13.6 0.7 %copy-done.3 = f32[8,128]{1,0:T(8,128)S(1)} copy-done((f32[8,128]{1,0:T(8,128)S(1)}, f32[8,128]{1,0:T(8,128)}, u32[]{:S(2)}) %copy-start.3) | copy-done | bytes 4120
  14.3 0.9 %combine.1 = (f32[8,32,128]{2,1,0:T(8,128)S(1)}, f32[2,32,128]{2,1,0:T(8,128)S(1)}, f32[2,32,128]{2,1,0:T(8,128)S(1)}, f32[4,128]{1,0:T(4,128)S(1)}) custom-call(bf16[32,16384]{1,0:T(8,128)(2,1)S(1)} %get-tuple-element.21.x_ref, bf16[8,4352]{1,0:T(8,128)(2,1)S(1)} %collective-permute-done.msg_ref, f32[2,32,128]{2,1,0:T(8,128)S(1)} %get-tuple-element.22.u0, ...), custom_call_target="tpu_custom_call" | custom-call | tf_op jit(solution)/shard_map/combine/pallas_call | solution.py:245
  15.2 0.1 collective-permute-start.3
  15.3 6.3 %collective-permute-start.4 = (f32[2,32,128]{2,1,0:T(8,128)S(1)}, f32[2,32,128]{2,1,0:T(8,128)S(1)}, u32[]{:S(2)}, u32[]{:S(2)}) collective-permute-start(f32[2,32,128]{2,1,0:T(8,128)S(1)} %get-tuple-element.30), channel_id=1, source_target_pairs={{4,8},{12,16},{20,24},{28,32},{36,40},{44,48},{52,56},{60,64},{68,... | collective-permute-start | bytes 98312 | tf_op jit(solution)/shard_map/ppermute | solution.py:255
  21.7 0.0 collective-permute-done.3.ein_ref
  21.7 1.6 %collective-permute-done.4.oin_ref = f32[2,32,128]{2,1,0:T(8,128)S(1)} collective-permute-done((f32[2,32,128]{2,1,0:T(8,128)S(1)}, f32[2,32,128]{2,1,0:T(8,128)S(1)}, u32[]{:S(2)}, u32[]{:S(2)}) %collective-permute-start.4) | collective-permute-done | bytes 32800 | tf_op jit(solution)/shard_map/ppermute | solution.py:255
  23.3 1.4 %expand.1 = (f32[8,4096]{1,0:T(8,128)S(1)}, bf16[8,4096]{1,0:T(8,128)(2,1)S(1)}, bf16[8,4096]{1,0:T(8,128)(2,1)S(1)}, bf16[8,4096]{1,0:T(8,128)(2,1)S(1)}) custom-call(bf16[32,16384]{1,0:T(8,128)(2,1)S(1)} %get-tuple-element.21.x_ref, f32[8,32,128]{2,1,0:T(8,128)S(1)} %get-tuple-element.28.z_ref, f32[2,32,128]{2,1,0:T(8,128)S(1)} %collective-permute-done.3.ein_ref, ...), custom_call_target="tpu_custom_call" | custom-call | tf_op jit(solution)/shard_map/expand/pallas_call | solution.py:257
  24.6 2.6 %collective-permute-start.5 = (bf16[8,4096]{1,0:T(8,128)(2,1)S(1)}, bf16[8,4096]{1,0:T(8,128)(2,1)S(1)}, u32[]{:S(2)}, u32[]{:S(2)}) collective-permute-start(bf16[8,4096]{1,0:T(8,128)(2,1)S(1)} %get-tuple-element.34), channel_id=1, source_target_pairs={{3,0},{2,1},{1,2},{0,3},{7,4},{6,5},{5,6},{4,7},{11,8},{10,9},{9,1... | collective-permute-start | bytes 196616 | tf_op jit(solution)/shard_map/ppermute | solution.py:268
  27.3 0.6 %collective-permute-start.6 = (bf16[8,4096]{1,0:T(8,128)(2,1)S(1)}, bf16[8,4096]{1,0:T(8,128)(2,1)S(1)}, u32[]{:S(2)}, u32[]{:S(2)}) collective-permute-start(bf16[8,4096]{1,0:T(8,128)(2,1)S(1)} %get-tuple-element.35), channel_id=1, source_target_pairs={{2,0},{3,1},{0,2},{1,3},{6,4},{7,5},{4,6},{5,7},{10,8},{11,9},{8,1... | collective-permute-start | bytes 196616 | tf_op jit(solution)/shard_map/ppermute | solution.py:268
  27.9 0.9 %collective-permute-start.7 = (bf16[8,4096]{1,0:T(8,128)(2,1)S(1)}, bf16[8,4096]{1,0:T(8,128)(2,1)S(1)}, u32[]{:S(2)}, u32[]{:S(2)}) collective-permute-start(bf16[8,4096]{1,0:T(8,128)(2,1)S(1)} %get-tuple-element.36), channel_id=1, source_target_pairs={{1,0},{0,1},{3,2},{2,3},{5,4},{4,5},{7,6},{6,7},{9,8},{8,9},{11,10... | collective-permute-start | bytes 196616 | tf_op jit(solution)/shard_map/ppermute | solution.py:268
  28.8 1.4 %collective-permute-done.5 = bf16[8,4096]{1,0:T(8,128)(2,1)S(1)} collective-permute-done((bf16[8,4096]{1,0:T(8,128)(2,1)S(1)}, bf16[8,4096]{1,0:T(8,128)(2,1)S(1)}, u32[]{:S(2)}, u32[]{:S(2)}) %collective-permute-start.5) | collective-permute-done | bytes 65568 | tf_op jit(solution)/shard_map/ppermute | solution.py:268
  30.2 2.8 %collective-permute-done.6 = bf16[8,4096]{1,0:T(8,128)(2,1)S(1)} collective-permute-done((bf16[8,4096]{1,0:T(8,128)(2,1)S(1)}, bf16[8,4096]{1,0:T(8,128)(2,1)S(1)}, u32[]{:S(2)}, u32[]{:S(2)}) %collective-permute-start.6) | collective-permute-done | bytes 65568 | tf_op jit(solution)/shard_map/ppermute | solution.py:268
  33.0 0.0 collective-permute-done.7
  33.0 0.7 %convert_add_fusion = f32[8,4096]{1,0:T(8,128)} fusion(bf16[8,4096]{1,0:T(8,128)(2,1)S(1)} %collective-permute-done.7, bf16[8,4096]{1,0:T(8,128)(2,1)S(1)} %collective-permute-done.6, f32[8,4096]{1,0:T(8,128)S(1)} %get-tuple-element.33, bf16[8,4096]{1,0:T(8,128)(2,1)S(1)} %collective-permute-done.5), kind=kLoop, calls=%fused_computation | loop fusion | flops 196608 | bytes 458752 | tf_op jit(solution)/shard_map/add | solution.py:268
  (1 shorter events, 0.0 us)
Async XLA Ops:
  0.0 8.3 %copy-start = (f32[16,2048]{1,0:T(8,128)S(1)}, f32[16,2048]{1,0:T(8,128)}, u32[]{:S(2)}) copy-start(f32[16,2048]{1,0:T(8,128)} %constant.4.clone.basis_ref) | copy-start | bytes 393220
  0.7 7.6 %copy-start.4 = (f32[8]{0:T(128)S(1)}, f32[8]{0:T(128)}, u32[]{:S(2)}) copy-start(f32[8]{0:T(128)} %modes.1) | copy-start | bytes 100
  3.8 7.9 %collective-permute-start.2 = (bf16[8,4352]{1,0:T(8,128)(2,1)}, bf16[8,4352]{1,0:T(8,128)(2,1)S(1)}, u32[]{:S(2)}, u32[]{:S(2)}) collective-permute-start(bf16[8,4352]{1,0:T(8,128)(2,1)} %message.1.msg_ref), channel_id=1, source_target_pairs={{2,0},{3,1},{0,2},{1,3},{6,4},{7,5},{4,6},{5,7},{10,8},{11,9},{8,1... | collective-permute-start | bytes 208904 | tf_op jit(solution)/shard_map/ppermute | solution.py:223
  7.2 5.3 %collective-permute-start.1 = (bf16[8,4352]{1,0:T(8,128)(2,1)}, bf16[8,4352]{1,0:T(8,128)(2,1)S(1)}, u32[]{:S(2)}, u32[]{:S(2)}) collective-permute-start(bf16[8,4352]{1,0:T(8,128)(2,1)} %message.1.msg_ref), channel_id=1, source_target_pairs={{1,0},{0,1},{3,2},{2,3},{5,4},{4,5},{7,6},{6,7},{9,8},{8,9},{11,10... | collective-permute-start | bytes 208904 | tf_op jit(solution)/shard_map/ppermute | solution.py:223
  7.9 5.7 %collective-permute-start = (bf16[8,4352]{1,0:T(8,128)(2,1)}, bf16[8,4352]{1,0:T(8,128)(2,1)S(1)}, u32[]{:S(2)}, u32[]{:S(2)}) collective-permute-start(bf16[8,4352]{1,0:T(8,128)(2,1)} %message.1.msg_ref), channel_id=1, source_target_pairs={{3,0},{2,1},{1,2},{0,3},{7,4},{6,5},{5,6},{4,7},{11,8},{10,9},{9,1... | collective-permute-start | bytes 208904 | tf_op jit(solution)/shard_map/ppermute | solution.py:223
  8.3 1.2 %copy-start.1 = (bf16[32,16384]{1,0:T(8,128)(2,1)S(1)}, bf16[32,16384]{1,0:T(8,128)(2,1)}, u32[]{:S(2)}) copy-start(bf16[32,16384]{1,0:T(8,128)(2,1)} %x_hbm.1) | copy-start | bytes 3145732
  9.5 0.9 %copy-start.2 = (bf16[8,4352]{1,0:T(8,128)(2,1)S(1)}, bf16[8,4352]{1,0:T(8,128)(2,1)}, u32[]{:S(2)}) copy-start(bf16[8,4352]{1,0:T(8,128)(2,1)} %message.1.msg_ref) | copy-start | bytes 208900
  13.6 0.7 %copy-start.3 = (f32[8,128]{1,0:T(8,128)S(1)}, f32[8,128]{1,0:T(8,128)}, u32[]{:S(2)}) copy-start(f32[8,128]{1,0:T(8,128)} %constant.5.clone.turns_ref) | copy-start | bytes 12292
  15.2 6.4 %collective-permute-start.3 = (f32[2,32,128]{2,1,0:T(8,128)S(1)}, f32[2,32,128]{2,1,0:T(8,128)S(1)}, u32[]{:S(2)}, u32[]{:S(2)}) collective-permute-start(f32[2,32,128]{2,1,0:T(8,128)S(1)} %get-tuple-element.29), channel_id=1, source_target_pairs={{0,4},{8,12},{16,20},{24,28},{32,36},{40,44},{48,52},{56,60},{64,6... | collective-permute-start | bytes 98312 | tf_op jit(solution)/shard_map/ppermute | solution.py:256
  15.3 7.9 %collective-permute-start.4 = (f32[2,32,128]{2,1,0:T(8,128)S(1)}, f32[2,32,128]{2,1,0:T(8,128)S(1)}, u32[]{:S(2)}, u32[]{:S(2)}) collective-permute-start(f32[2,32,128]{2,1,0:T(8,128)S(1)} %get-tuple-element.30), channel_id=1, source_target_pairs={{4,8},{12,16},{20,24},{28,32},{36,40},{44,48},{52,56},{60,64},{68,... | collective-permute-start | bytes 98312 | tf_op jit(solution)/shard_map/ppermute | solution.py:255
  24.6 5.6 %collective-permute-start.5 = (bf16[8,4096]{1,0:T(8,128)(2,1)S(1)}, bf16[8,4096]{1,0:T(8,128)(2,1)S(1)}, u32[]{:S(2)}, u32[]{:S(2)}) collective-permute-start(bf16[8,4096]{1,0:T(8,128)(2,1)S(1)} %get-tuple-element.34), channel_id=1, source_target_pairs={{3,0},{2,1},{1,2},{0,3},{7,4},{6,5},{5,6},{4,7},{11,8},{10,9},{9,1... | collective-permute-start | bytes 196616 | tf_op jit(solution)/shard_map/ppermute | solution.py:268
  27.3 5.8 %collective-permute-start.6 = (bf16[8,4096]{1,0:T(8,128)(2,1)S(1)}, bf16[8,4096]{1,0:T(8,128)(2,1)S(1)}, u32[]{:S(2)}, u32[]{:S(2)}) collective-permute-start(bf16[8,4096]{1,0:T(8,128)(2,1)S(1)} %get-tuple-element.35), channel_id=1, source_target_pairs={{2,0},{3,1},{0,2},{1,3},{6,4},{7,5},{4,6},{5,7},{10,8},{11,9},{8,1... | collective-permute-start | bytes 196616 | tf_op jit(solution)/shard_map/ppermute | solution.py:268
  27.9 5.1 %collective-permute-start.7 = (bf16[8,4096]{1,0:T(8,128)(2,1)S(1)}, bf16[8,4096]{1,0:T(8,128)(2,1)S(1)}, u32[]{:S(2)}, u32[]{:S(2)}) collective-permute-start(bf16[8,4096]{1,0:T(8,128)(2,1)S(1)} %get-tuple-element.36), channel_id=1, source_target_pairs={{1,0},{0,1},{3,2},{2,3},{5,4},{4,5},{7,6},{6,7},{9,8},{8,9},{11,10... | collective-permute-start | bytes 196616 | tf_op jit(solution)/shard_map/ppermute | solution.py:268

commit v3 on v1

v3 whole, which is shorter than its diff:
```python
import functools
import math

import jax
import jax.numpy as jnp
from jax import lax
from jax.experimental import pallas as pl
from jax.experimental.pallas import tpu as pltpu
from jax.sharding import PartitionSpec as P

BLOCK = 2048
MODES = 8
RANK = 2 * MODES
COLS = 8
LANES = 128
PERIOD = 12288
PAIR = 2
NCODE = 4
TAIL = 256
F32 = jnp.float32
BF16 = jnp.bfloat16


def cosine(turn):
    turn = lax.rem(turn, jnp.int32(PERIOD))
    fold = jnp.abs(turn - PERIOD // 2) - PERIOD // 4
    x = fold.astype(F32) * F32(2.0 * math.pi / PERIOD)
    y = x * x
    total = F32(1.0 / 6227020800.0)
    for c in (-1.0 / 39916800.0, 1.0 / 362880.0, -1.0 / 5040.0, 1.0 / 120.0, -1.0 / 6.0, 1.0):
        total = total * y + F32(c)
    return x * total


def write_basis(ref):
    row = lax.broadcasted_iota(jnp.int32, (RANK, LANES), 0)
    lane = lax.broadcasted_iota(jnp.int32, (RANK, LANES), 1)
    shift = jnp.where(row < MODES, 0, PERIOD - PERIOD // 4)
    for c in range(0, BLOCK, LANES):
        ref[:, c : c + LANES] = cosine((row % MODES) * (lane + c) + shift)


def write_turns(ref):
    row = lax.broadcasted_iota(jnp.int32, (8, LANES), 0)
    lane = lax.broadcasted_iota(jnp.int32, (8, LANES), 1)
    shift = jnp.where(row % 2 == 0, 0, PERIOD - PERIOD // 4)
    value = cosine(((lane // COLS) % MODES) * ((row // 2 + 1) * BLOCK) + shift)
    ref[...] = jnp.where((row % 2 == 1) & (lane < LANES // 2), -value, value)


def split(value):
    high = value.astype(BF16)
    low = (value - high.astype(F32)).astype(BF16)
    return high, low


def turned(value, turns, o, back):
    c = turns[2 * o - 2 : 2 * o - 1, :]
    s = turns[2 * o - 1 : 2 * o, :]
    other = pltpu.roll(value, LANES // 2, 1)
    return value * c - other * s if back else value * c + other * s


def message_kernel(code, klass, count, table, modes, v_ref, out_ref, aux_ref):
    n = v_ref.shape[1]
    out_ref[:, :n] = v_ref[...]
    row = lax.broadcasted_iota(jnp.int32, (8, LANES), 0)
    w = jnp.zeros((8, LANES), F32)
    for slot in range(NCODE):
        rho = jnp.where(slot < count[0], table[klass[slot]], F32(0.0))
        w = w + jnp.where(row % NCODE == code[slot], rho, F32(0.0))
    high, low = split(w)
    rest = (w - high.astype(F32) - low.astype(F32)).astype(BF16)
    first = row < NCODE
    out_ref[:, n : n + LANES] = jnp.where(first, high.astype(F32), low.astype(F32)).astype(BF16)
    out_ref[:, n + LANES :] = rest
    aux_ref[:8, :] = w
    rank = lax.broadcasted_iota(jnp.int32, (RANK, LANES), 0) % MODES
    gain = jnp.zeros((RANK, LANES), F32)
    for m in range(MODES):
        gain = jnp.where(rank == m, modes[m] * F32(1.0 / 127.0), gain)
    aux_ref[8:, :] = gain


def weights_of(msg_ref):
    n = msg_ref.shape[1] - TAIL
    both = msg_ref[:, n : n + LANES].astype(F32)
    rest = msg_ref[:, n + LANES :].astype(F32)
    return both[:NCODE] + both[NCODE:] + rest[:NCODE]


def project(x, v, basis):
    wide = (basis[:, None, :] * v[None, :, :].astype(F32)).reshape(RANK * COLS, v.shape[1])
    high, low = split(wide)
    both = jnp.concatenate([high, low], 0)
    out = lax.dot_general(x, both, (((1,), (1,)), ((), ())), preferred_element_type=F32)
    return out[:, :LANES] + out[:, LANES:]


def project_chunk(x_ref, v_ref, basis_ref, member, u_ref):
    for j in range(PAIR):
        k = member * PAIR + j
        x = x_ref[:, pl.ds(pl.multiple_of(k * BLOCK, BLOCK), BLOCK)]
        u_ref[j] = project(x, v_ref[:, j * BLOCK : (j + 1) * BLOCK], basis_ref[...])


def own_kernel(x_ref, v_ref, u_ref, basis_ref, turns_ref):
    write_basis(basis_ref)
    write_turns(turns_ref)
    project_chunk(x_ref, v_ref, basis_ref, lax.axis_index("mem"), u_ref)


def project_kernel(distance, x_ref, msg_ref, basis_ref, u_ref):
    project_chunk(x_ref, msg_ref, basis_ref, lax.axis_index("mem") ^ distance, u_ref)


def combine_kernel(x_ref, u0, u2, u3, aux_ref, m1, m2, m3, basis_ref, turns_ref, u_ref, w_ref, e_ref, o_ref):
    me = lax.axis_index("mem")
    nblk = u_ref.shape[0]
    project_chunk(x_ref, m1, basis_ref, me ^ 1, u_ref.at[pl.ds((me ^ 1) * PAIR, PAIR)])
    for d, u in ((0, u0), (2, u2), (3, u3)):
        for j in range(PAIR):
            u_ref[(me ^ d) * PAIR + j] = u[j]
    w_ref[me] = aux_ref[:NCODE, :]
    for d, m in enumerate((m1, m2, m3), 1):
        w_ref[me ^ d] = weights_of(m)
    turns = turns_ref[...]
    last = nblk - 1
    w = w_ref[last // PAIR]
    even = lax.axis_index("blk") % 2 == 0
    ahead = (
        turned(u_ref[last - 1], turns, 2, True) * w[1:2] + turned(u_ref[last], turns, 1, True) * w[2:3],
        turned(u_ref[last], turns, 2, True) * w[3:4],
    )
    for j in range(PAIR):
        e_ref[j] = jnp.where(even, ahead[j], u_ref[j])
        o_ref[j] = jnp.where(even, u_ref[j], ahead[j])


def expand(x, z, l_ref):
    high, low = split(z)
    t = lax.dot_general(
        jnp.concatenate([high, low], 0),
        jnp.concatenate([x, x], 0),
        (((0,), (0,)), ((), ())),
        preferred_element_type=F32,
    )
    return jnp.sum(t.reshape(RANK, COLS, BLOCK) * l_ref[...][:, None, :], axis=0)


def inner_kernel(x_ref, u_ref, w_ref, aux_ref, basis_ref, turns_ref, z_ref, y_ref, l_ref):
    for c in range(0, BLOCK, LANES):
        l_ref[:, c : c + LANES] = basis_ref[:, c : c + LANES] * aux_ref[8:, :]
    nblk = u_ref.shape[0]
    turns = turns_ref[...]

    def rho(k, o):
        c = (k % PAIR) * PAIR + o - 1
        return w_ref[k // PAIR][c : c + 1, :]

    for k in range(nblk):
        z = u_ref[k]
        for o in (1, 2):
            if k + o < nblk:
                z = z + turned(u_ref[k + o], turns, o, False) * rho(k, o)
            if k - o >= 0:
                z = z + turned(u_ref[k - o], turns, o, True) * rho(k - o, o)
        if 2 <= k < nblk - 2:
            y_ref[k // PAIR - 1, :, (k % PAIR) * BLOCK : (k % PAIR + 1) * BLOCK] = expand(
                x_ref[:, k * BLOCK : (k + 1) * BLOCK], z, l_ref
            )
        else:
            z_ref[k % 4] = z


def close_kernel(x_ref, z_ref, zo_ref, ein_ref, oin_ref, w_ref, l_ref, turns_ref, yi_ref, *rest):
    outs, all_sc = rest[:-1], rest[-1]
    me = lax.axis_index("mem")
    turns = turns_ref[...]
    nblk = x_ref.shape[1] // BLOCK
    last = nblk - 1
    w = w_ref[last // PAIR]
    even = lax.axis_index("blk") % 2 == 0
    uin = [jnp.where(even, ein_ref[j], oin_ref[j]) for j in range(PAIR)]
    z = {j: jnp.where(even, zo_ref[j], z_ref[j] + ein_ref[j]) for j in range(PAIR)}
    z[last - 1] = z_ref[2] + turned(uin[0], turns, 2, False) * w[1:2]
    z[last] = z_ref[3] + turned(uin[0], turns, 1, False) * w[2:3] + turned(uin[1], turns, 2, False) * w[3:4]
    for k, value in z.items():
        where = slice((k % PAIR) * BLOCK, (k % PAIR + 1) * BLOCK)
        all_sc[k // PAIR, :, where] = expand(x_ref[:, k * BLOCK : (k + 1) * BLOCK], value, l_ref)
    all_sc[1] = yi_ref[0]
    all_sc[2] = yi_ref[1]
    for d, out in enumerate(outs):
        out[...] = all_sc[me ^ d].astype(out.dtype)


def crossed(n, distance):
    return [(i ^ distance, i) for i in range(n)]


def partner(n, odd):
    pairs = [((2 * i + odd) % n, (2 * i + 1 + odd) % n) for i in range(n // 2)]
    return pairs + [(b, a) for a, b in pairs]


VM = pl.BlockSpec(memory_space=pltpu.VMEM)
SM = pl.BlockSpec(memory_space=pltpu.SMEM)
LIMIT = pltpu.CompilerParams(vmem_limit_bytes=40 * 1024 * 1024)


def body(anomalies, increments, taper_table, taper_modes, pair_code, pair_class, pair_count):
    members, wide = anomalies.shape
    cols, width = increments.shape
    nmem = lax.axis_size("mem")
    nblk = wide // BLOCK
    shape = jax.ShapeDtypeStruct
    x = anomalies
    msg, aux = pl.pallas_call(
        message_kernel,
        out_shape=[shape((cols, width + TAIL), BF16), shape((8 + RANK, LANES), F32)],
        in_specs=[SM] * 5 + [VM],
        out_specs=[VM] * 2,
        name="message",
    )(pair_code, pair_class, pair_count, taper_table, taper_modes, increments)
    m1, m2, m3 = [lax.ppermute(msg, "mem", crossed(nmem, d)) for d in (1, 2, 3)]
    chunk = shape((PAIR, members, LANES), F32)
    table = shape((RANK, BLOCK), F32)
    u0, basis, turns = pl.pallas_call(
        own_kernel,
        out_shape=[chunk, table, shape((8, LANES), F32)],
        in_specs=[VM] * 2,
        out_specs=[VM] * 3,
        compiler_params=LIMIT,
        name="own",
    )(x, increments)
    u3, u2 = [
        pl.pallas_call(
            functools.partial(project_kernel, d),
            out_shape=chunk,
            in_specs=[VM] * 3,
            out_specs=VM,
            compiler_params=LIMIT,
            name=f"project_{d}",
        )(x, m, basis)
        for d, m in ((3, m3), (2, m2))
    ]
    uall, wall, e, o = pl.pallas_call(
        combine_kernel,
        out_shape=[shape((nblk, members, LANES), F32), shape((nmem, NCODE, LANES), F32), chunk, chunk],
        in_specs=[VM] * 10,
        out_specs=[VM] * 4,
        compiler_params=LIMIT,
        name="combine",
    )(x, u0, u2, u3, aux, m1, m2, m3, basis, turns)
    nb = lax.axis_size("blk")
    oin = lax.ppermute(o, "blk", partner(nb, 1))
    ein = lax.ppermute(e, "blk", partner(nb, 0))
    z, yi, left = pl.pallas_call(
        inner_kernel,
        out_shape=[shape((4, members, LANES), F32), shape((2, cols, width), F32), table],
        in_specs=[VM] * 6,
        out_specs=[VM] * 3,
        compiler_params=LIMIT,
        name="inner",
    )(x, uall, wall, aux, basis, turns)
    zo = z[:PAIR] + oin
    outs = pl.pallas_call(
        close_kernel,
        out_shape=[shape((cols, width), F32)] + [shape((cols, width), BF16)] * (nmem - 1),
        in_specs=[VM] * 9,
        out_specs=[VM] * nmem,
        scratch_shapes=[pltpu.VMEM((nmem, cols, width), F32)],
        compiler_params=LIMIT,
        name="close",
    )(x, z, zo, ein, oin, wall, left, turns, yi)
    total = outs[0]
    for d in (3, 2, 1):
        total = total + lax.ppermute(outs[d], "mem", crossed(nmem, d)).astype(F32)
    return total


def solution(mesh):
    in_specs = (
        P("mem", "blk"),
        P(None, ("blk", "mem")),
        P(),
        P(),
        P(("blk", "mem")),
        P(("blk", "mem")),
        P(("blk", "mem")),
    )
    out_specs = P(None, ("blk", "mem"))
    return jax.shard_map(body, mesh=mesh, in_specs=in_specs, out_specs=out_specs, check_vma=False)
```

time: 36.4 us -> 28.7 us (0.79)
  waiting for transfers between devices: 12 us -> 7.05 us
  local copies, waits for them, and re-layouts: 2.77 us -> 1.23 us
  starting transfers between devices: 13.7 us -> 12.5 us
    ppermute x8, waiting for transfers between devices: 12 us -> 7.05 us  [the longest x3 3.09 us: body(): total = total + lax.ppermute(outs[d], 'mem', crossed(nmem, d)).astype(F32)]
    unnamed x12 -> x6, local copies, waits for them, and re-layouts: 2.77 us -> 1.23 us
    ppermute x8, starting transfers between devices: 13.7 us -> 12.5 us  [the longest x1 4.24 us: body(): oin = lax.ppermute(o, 'blk', partner(nb, 1))]
    pallas_call x3 -> x7, Pallas kernels: 6.23 us -> 6.24 us  [the longest x1 1.51 us: body(): pl.pallas_call(message_kernel, out_shape=[shape((cols, width + TAIL), BF1...]
  transfers between devices with their start and end apart: 8 -> 8, of which waited for: 6 -> 4; matrix products, arithmetic and copies ran while one was open for 0% -> 0% of each run, Pallas kernels for 0% -> 11%
where the time goes in v3:
time: 28.7 us; the launch traced here: 28.5 us
  starting transfers between devices  12.5 us (44%)
  waiting for transfers between devices  7.05 us (25%)
  Pallas kernels  6.24 us (22%)
  local copies, waits for them, and re-layouts  1.23 us (4%)
  between operations  0.76 us (3%)
  other arithmetic  0.7 us (2%)
    ppermute x1, starting transfers between devices, body(): oin = lax.ppermute(o, 'blk', partner(nb, 1))  4.24 us
    ppermute x3, starting transfers between devices, body(): total = total + lax.ppermute(outs[d], 'mem', crossed(nmem, d)).astype(F32)  4.17 us
    ppermute x3, starting transfers between devices, body(): m1, m2, m3 = [lax.ppermute(msg, 'mem', crossed(nmem, d)) for d in (1, 2, 3)]  4.09 us
    ppermute x3, waiting for transfers between devices, body(): total = total + lax.ppermute(outs[d], 'mem', crossed(nmem, d)).astype(F32)  3.09 us
    ppermute x3, waiting for transfers between devices, body(): m1, m2, m3 = [lax.ppermute(msg, 'mem', crossed(nmem, d)) for d in (1, 2, 3)]  2.29 us
    ppermute x1, waiting for transfers between devices, body(): oin = lax.ppermute(o, 'blk', partner(nb, 1))  1.66 us
    pallas_call x1, Pallas kernels, body(): pl.pallas_call(message_kernel, out_shape=[shape((cols, width + TAIL), BF1...  1.51 us
    pallas_call x2, Pallas kernels, body(): pl.pallas_call(functools.partial(project_kernel, d), out_shape=chunk, in_...  1.46 us
  transfers between devices with their start and end apart: 8, of which 4 were waited for; matrix products, arithmetic and copies ran while one was open for 0% of the time, Pallas kernels for 11%

profile of v3, /device:TPU:0, one launch (start us, length us, event | category | flops | bytes accessed | tf_op | source)
XLA Modules:
  0.0 28.5 jit_solution(16770727679057039366)
XLA Ops:
  0.0 0.0 copy-start.1
  0.7 1.5 %message.1 = (bf16[8,4352]{1,0:T(8,128)(2,1)}, f32[24,128]{1,0:T(8,128)}) custom-call(s32[4]{0:T(128)} %code.1, s32[4]{0:T(128)} %klass.1, s32[1]{0:T(128)S(6)} %copy.8.count, f32[8]{0:T(128)} %table.1, f32[8]{0:T(128)} %modes.1, bf16[8,4096]{1,0:T(8,128)(2,1)} %v_ref.3), custom_call_target="tpu_custom_call" | custom-call | tf_op jit(solution)/shard_map/message/pallas_call | solution.py:218
  2.2 3.1 %collective-permute-start.1 = (bf16[8,4352]{1,0:T(8,128)(2,1)}, bf16[8,4352]{1,0:T(8,128)(2,1)S(1)}, u32[]{:S(2)}, u32[]{:S(2)}) collective-permute-start(bf16[8,4352]{1,0:T(8,128)(2,1)} %get-tuple-element.22), channel_id=1, source_target_pairs={{3,0},{2,1},{1,2},{0,3},{7,4},{6,5},{5,6},{4,7},{11,8},{10,9},{9,1... | collective-permute-start | bytes 208904 | tf_op jit(solution)/shard_map/ppermute | solution.py:225
  5.3 0.6 %collective-permute-start = (bf16[8,4352]{1,0:T(8,128)(2,1)}, bf16[8,4352]{1,0:T(8,128)(2,1)S(1)}, u32[]{:S(2)}, u32[]{:S(2)}) collective-permute-start(bf16[8,4352]{1,0:T(8,128)(2,1)} %get-tuple-element.22), channel_id=1, source_target_pairs={{2,0},{3,1},{0,2},{1,3},{6,4},{7,5},{4,6},{5,7},{10,8},{11,9},{8,1... | collective-permute-start | bytes 208904 | tf_op jit(solution)/shard_map/ppermute | solution.py:225
  5.9 0.4 %collective-permute-start.2 = (bf16[8,4352]{1,0:T(8,128)(2,1)}, bf16[8,4352]{1,0:T(8,128)(2,1)S(1)}, u32[]{:S(2)}, u32[]{:S(2)}) collective-permute-start(bf16[8,4352]{1,0:T(8,128)(2,1)} %get-tuple-element.22), channel_id=1, source_target_pairs={{1,0},{0,1},{3,2},{2,3},{5,4},{4,5},{7,6},{6,7},{9,8},{8,9},{11,10... | collective-permute-start | bytes 208904 | tf_op jit(solution)/shard_map/ppermute | solution.py:225
  6.3 0.0 copy-done.1
  6.3 0.0 copy-start
  6.3 1.2 %copy-done = bf16[32,16384]{1,0:T(8,128)(2,1)S(1)} copy-done((bf16[32,16384]{1,0:T(8,128)(2,1)S(1)}, bf16[32,16384]{1,0:T(8,128)(2,1)}, u32[]{:S(2)}) %copy-start) | copy-done | bytes 1048600
  7.5 0.8 %own.1 = (f32[2,32,128]{2,1,0:T(8,128)S(1)}, f32[16,2048]{1,0:T(8,128)S(1)}, f32[8,128]{1,0:T(8,128)S(1)}) custom-call(bf16[32,16384]{1,0:T(8,128)(2,1)S(1)} %copy-done, bf16[8,4096]{1,0:T(8,128)(2,1)S(1)} %copy-done.1), custom_call_target="tpu_custom_call" | custom-call | tf_op jit(solution)/shard_map/own/pallas_call | solution.py:228
  8.4 0.0 collective-permute-done.1.msg_ref.m3
  8.4 0.7 %project_3.1.u3 = f32[2,32,128]{2,1,0:T(8,128)S(1)} custom-call(bf16[32,16384]{1,0:T(8,128)(2,1)S(1)} %copy-done, bf16[8,4352]{1,0:T(8,128)(2,1)S(1)} %collective-permute-done.1.msg_ref.m3, f32[16,2048]{1,0:T(8,128)S(1)} %get-tuple-element.23.basis_ref), custom_call_target="tpu_custom_call" | custom-call | tf_op jit(solution)/shard_map/project_3/pallas_call | solution.py:237
  9.1 2.3 %collective-permute-done.msg_ref.m2 = bf16[8,4352]{1,0:T(8,128)(2,1)S(1)} collective-permute-done((bf16[8,4352]{1,0:T(8,128)(2,1)}, bf16[8,4352]{1,0:T(8,128)(2,1)S(1)}, u32[]{:S(2)}, u32[]{:S(2)}) %collective-permute-start) | collective-permute-done | bytes 69664 | tf_op jit(solution)/shard_map/ppermute | solution.py:225
  11.4 0.0 copy-start.2
  11.4 0.7 %project_2.1.u2 = f32[2,32,128]{2,1,0:T(8,128)S(1)} custom-call(bf16[32,16384]{1,0:T(8,128)(2,1)S(1)} %copy-done, bf16[8,4352]{1,0:T(8,128)(2,1)S(1)} %collective-permute-done.msg_ref.m2, f32[16,2048]{1,0:T(8,128)S(1)} %get-tuple-element.23.basis_ref), custom_call_target="tpu_custom_call" | custom-call | tf_op jit(solution)/shard_map/project_2/pallas_call | solution.py:237
  12.1 0.0 collective-permute-done.2.m1
  12.1 0.0 copy-done.2
  12.2 0.8 %combine.1 = (f32[8,32,128]{2,1,0:T(8,128)S(1)}, f32[4,4,128]{2,1,0:T(4,128)S(1)}, f32[2,32,128]{2,1,0:T(8,128)S(1)}, f32[2,32,128]{2,1,0:T(8,128)S(1)}) custom-call(bf16[32,16384]{1,0:T(8,128)(2,1)S(1)} %copy-done, f32[2,32,128]{2,1,0:T(8,128)S(1)} %get-tuple-element.21.u0, f32[2,32,128]{2,1,0:T(8,128)S(1)} %project_2.1.u2, f32[2,32,128]{2,1,0:T(8,128)S(1)} %project_3.1.u3, ...), custom_call_target="tpu_custom_call" | custom-call | tf_op jit(solution)/shard_map/combine/pallas_call | solution.py:247
  13.0 4.2 %collective-permute-start.3 = (f32[2,32,128]{2,1,0:T(8,128)S(1)}, f32[2,32,128]{2,1,0:T(8,128)S(1)}, u32[]{:S(2)}, u32[]{:S(2)}) collective-permute-start(f32[2,32,128]{2,1,0:T(8,128)S(1)} %get-tuple-element.29), channel_id=1, source_target_pairs={{4,8},{12,16},{20,24},{28,32},{36,40},{44,48},{52,56},{60,64},{68,... | collective-permute-start | bytes 98312 | tf_op jit(solution)/shard_map/ppermute | solution.py:256
  17.2 0.0 collective-permute-start.4
  17.2 0.8 %inner.1 = (f32[4,32,128]{2,1,0:T(8,128)S(1)}, f32[2,8,4096]{2,1,0:T(8,128)S(1)}, f32[16,2048]{1,0:T(8,128)S(1)}) custom-call(bf16[32,16384]{1,0:T(8,128)(2,1)S(1)} %copy-done, f32[8,32,128]{2,1,0:T(8,128)S(1)} %get-tuple-element.26.u_ref, f32[4,4,128]{2,1,0:T(4,128)S(1)} %get-tuple-element.27.w_ref, f32[24,128]{1,0:T(8,128)S(1)} %copy-done.2, ...), custom_call_target="tpu_custom_call" | custom-call | tf_op jit(solution)/shard_map/inner/pallas_call | solution.py:258
  18.1 1.7 %collective-permute-done.3.oin_ref = f32[2,32,128]{2,1,0:T(8,128)S(1)} collective-permute-done((f32[2,32,128]{2,1,0:T(8,128)S(1)}, f32[2,32,128]{2,1,0:T(8,128)S(1)}, u32[]{:S(2)}, u32[]{:S(2)}) %collective-permute-start.3) | collective-permute-done | bytes 32800 | tf_op jit(solution)/shard_map/ppermute | solution.py:256
  19.7 0.0 collective-permute-done.4.ein_ref
  19.8 0.8 %close.1 = (f32[8,4096]{1,0:T(8,128)S(1)}, bf16[8,4096]{1,0:T(8,128)(2,1)S(1)}, bf16[8,4096]{1,0:T(8,128)(2,1)S(1)}, bf16[8,4096]{1,0:T(8,128)(2,1)S(1)}) custom-call(bf16[32,16384]{1,0:T(8,128)(2,1)S(1)} %copy-done, f32[4,32,128]{2,1,0:T(8,128)S(1)} %get-tuple-element.28.z_ref, f32[2,32,128]{2,1,0:T(8,128)S(1)} %slice_add_fusion.zo_ref, ...), custom_call_target="tpu_custom_call" | custom-call | tf_op jit(solution)/shard_map/close/pallas_call | solution.py:267
  20.5 1.5 %collective-permute-start.5 = (bf16[8,4096]{1,0:T(8,128)(2,1)S(1)}, bf16[8,4096]{1,0:T(8,128)(2,1)S(1)}, u32[]{:S(2)}, u32[]{:S(2)}) collective-permute-start(bf16[8,4096]{1,0:T(8,128)(2,1)S(1)} %get-tuple-element.34), channel_id=1, source_target_pairs={{3,0},{2,1},{1,2},{0,3},{7,4},{6,5},{5,6},{4,7},{11,8},{10,9},{9,1... | collective-permute-start | bytes 196616 | tf_op jit(solution)/shard_map/ppermute | solution.py:278
  22.0 1.1 %collective-permute-start.6 = (bf16[8,4096]{1,0:T(8,128)(2,1)S(1)}, bf16[8,4096]{1,0:T(8,128)(2,1)S(1)}, u32[]{:S(2)}, u32[]{:S(2)}) collective-permute-start(bf16[8,4096]{1,0:T(8,128)(2,1)S(1)} %get-tuple-element.35), channel_id=1, source_target_pairs={{2,0},{3,1},{0,2},{1,3},{6,4},{7,5},{4,6},{5,7},{10,8},{11,9},{8,1... | collective-permute-start | bytes 196616 | tf_op jit(solution)/shard_map/ppermute | solution.py:278
  23.1 1.6 %collective-permute-start.7 = (bf16[8,4096]{1,0:T(8,128)(2,1)S(1)}, bf16[8,4096]{1,0:T(8,128)(2,1)S(1)}, u32[]{:S(2)}, u32[]{:S(2)}) collective-permute-start(bf16[8,4096]{1,0:T(8,128)(2,1)S(1)} %get-tuple-element.36), channel_id=1, source_target_pairs={{1,0},{0,1},{3,2},{2,3},{5,4},{4,5},{7,6},{6,7},{9,8},{8,9},{11,10... | collective-permute-start | bytes 196616 | tf_op jit(solution)/shard_map/ppermute | solution.py:278
  24.7 2.1 %collective-permute-done.5 = bf16[8,4096]{1,0:T(8,128)(2,1)S(1)} collective-permute-done((bf16[8,4096]{1,0:T(8,128)(2,1)S(1)}, bf16[8,4096]{1,0:T(8,128)(2,1)S(1)}, u32[]{:S(2)}, u32[]{:S(2)}) %collective-permute-start.5) | collective-permute-done | bytes 65568 | tf_op jit(solution)/shard_map/ppermute | solution.py:278
  26.8 1.0 %collective-permute-done.6 = bf16[8,4096]{1,0:T(8,128)(2,1)S(1)} collective-permute-done((bf16[8,4096]{1,0:T(8,128)(2,1)S(1)}, bf16[8,4096]{1,0:T(8,128)(2,1)S(1)}, u32[]{:S(2)}, u32[]{:S(2)}) %collective-permute-start.6) | collective-permute-done | bytes 65568 | tf_op jit(solution)/shard_map/ppermute | solution.py:278
  27.8 0.0 collective-permute-done.7
  27.8 0.7 %convert_add_fusion = f32[8,4096]{1,0:T(8,128)} fusion(bf16[8,4096]{1,0:T(8,128)(2,1)S(1)} %collective-permute-done.7, bf16[8,4096]{1,0:T(8,128)(2,1)S(1)} %collective-permute-done.6, f32[8,4096]{1,0:T(8,128)S(1)} %get-tuple-element.33, bf16[8,4096]{1,0:T(8,128)(2,1)S(1)} %collective-permute-done.5), kind=kLoop, calls=%fused_computation | loop fusion | flops 196608 | bytes 458752 | tf_op jit(solution)/shard_map/add | solution.py:278
  (1 shorter events, 0.0 us)
Async XLA Ops:
  0.0 6.3 %copy-start.1 = (bf16[8,4096]{1,0:T(8,128)(2,1)S(1)}, bf16[8,4096]{1,0:T(8,128)(2,1)}, u32[]{:S(2)}) copy-start(bf16[8,4096]{1,0:T(8,128)(2,1)} %v_ref.3) | copy-start | bytes 196612
  2.2 6.2 %collective-permute-start.1 = (bf16[8,4352]{1,0:T(8,128)(2,1)}, bf16[8,4352]{1,0:T(8,128)(2,1)S(1)}, u32[]{:S(2)}, u32[]{:S(2)}) collective-permute-start(bf16[8,4352]{1,0:T(8,128)(2,1)} %get-tuple-element.22), channel_id=1, source_target_pairs={{3,0},{2,1},{1,2},{0,3},{7,4},{6,5},{5,6},{4,7},{11,8},{10,9},{9,1... | collective-permute-start | bytes 208904 | tf_op jit(solution)/shard_map/ppermute | solution.py:225
  5.3 6.1 %collective-permute-start = (bf16[8,4352]{1,0:T(8,128)(2,1)}, bf16[8,4352]{1,0:T(8,128)(2,1)S(1)}, u32[]{:S(2)}, u32[]{:S(2)}) collective-permute-start(bf16[8,4352]{1,0:T(8,128)(2,1)} %get-tuple-element.22), channel_id=1, source_target_pairs={{2,0},{3,1},{0,2},{1,3},{6,4},{7,5},{4,6},{5,7},{10,8},{11,9},{8,1... | collective-permute-start | bytes 208904 | tf_op jit(solution)/shard_map/ppermute | solution.py:225
  5.9 6.2 %collective-permute-start.2 = (bf16[8,4352]{1,0:T(8,128)(2,1)}, bf16[8,4352]{1,0:T(8,128)(2,1)S(1)}, u32[]{:S(2)}, u32[]{:S(2)}) collective-permute-start(bf16[8,4352]{1,0:T(8,128)(2,1)} %get-tuple-element.22), channel_id=1, source_target_pairs={{1,0},{0,1},{3,2},{2,3},{5,4},{4,5},{7,6},{6,7},{9,8},{8,9},{11,10... | collective-permute-start | bytes 208904 | tf_op jit(solution)/shard_map/ppermute | solution.py:225
  6.3 1.2 %copy-start = (bf16[32,16384]{1,0:T(8,128)(2,1)S(1)}, bf16[32,16384]{1,0:T(8,128)(2,1)}, u32[]{:S(2)}) copy-start(bf16[32,16384]{1,0:T(8,128)(2,1)} %x_ref.11) | copy-start | bytes 3145732
  11.4 0.8 %copy-start.2 = (f32[24,128]{1,0:T(8,128)S(1)}, f32[24,128]{1,0:T(8,128)}, u32[]{:S(2)}) copy-start(f32[24,128]{1,0:T(8,128)} %get-tuple-element.24.aux_ref) | copy-start | bytes 36868
  13.0 6.7 %collective-permute-start.3 = (f32[2,32,128]{2,1,0:T(8,128)S(1)}, f32[2,32,128]{2,1,0:T(8,128)S(1)}, u32[]{:S(2)}, u32[]{:S(2)}) collective-permute-start(f32[2,32,128]{2,1,0:T(8,128)S(1)} %get-tuple-element.29), channel_id=1, source_target_pairs={{4,8},{12,16},{20,24},{28,32},{36,40},{44,48},{52,56},{60,64},{68,... | collective-permute-start | bytes 98312 | tf_op jit(solution)/shard_map/ppermute | solution.py:256
  17.2 2.5 %collective-permute-start.4 = (f32[2,32,128]{2,1,0:T(8,128)S(1)}, f32[2,32,128]{2,1,0:T(8,128)S(1)}, u32[]{:S(2)}, u32[]{:S(2)}) collective-permute-start(f32[2,32,128]{2,1,0:T(8,128)S(1)} %get-tuple-element.30), channel_id=1, source_target_pairs={{0,4},{8,12},{16,20},{24,28},{32,36},{40,44},{48,52},{56,60},{64,6... | collective-permute-start | bytes 98312 | tf_op jit(solution)/shard_map/ppermute | solution.py:257
  20.5 6.3 %collective-permute-start.5 = (bf16[8,4096]{1,0:T(8,128)(2,1)S(1)}, bf16[8,4096]{1,0:T(8,128)(2,1)S(1)}, u32[]{:S(2)}, u32[]{:S(2)}) collective-permute-start(bf16[8,4096]{1,0:T(8,128)(2,1)S(1)} %get-tuple-element.34), channel_id=1, source_target_pairs={{3,0},{2,1},{1,2},{0,3},{7,4},{6,5},{5,6},{4,7},{11,8},{10,9},{9,1... | collective-permute-start | bytes 196616 | tf_op jit(solution)/shard_map/ppermute | solution.py:278
  22.0 5.8 %collective-permute-start.6 = (bf16[8,4096]{1,0:T(8,128)(2,1)S(1)}, bf16[8,4096]{1,0:T(8,128)(2,1)S(1)}, u32[]{:S(2)}, u32[]{:S(2)}) collective-permute-start(bf16[8,4096]{1,0:T(8,128)(2,1)S(1)} %get-tuple-element.35), channel_id=1, source_target_pairs={{2,0},{3,1},{0,2},{1,3},{6,4},{7,5},{4,6},{5,7},{10,8},{11,9},{8,1... | collective-permute-start | bytes 196616 | tf_op jit(solution)/shard_map/ppermute | solution.py:278
  23.1 4.7 %collective-permute-start.7 = (bf16[8,4096]{1,0:T(8,128)(2,1)S(1)}, bf16[8,4096]{1,0:T(8,128)(2,1)S(1)}, u32[]{:S(2)}, u32[]{:S(2)}) collective-permute-start(bf16[8,4096]{1,0:T(8,128)(2,1)S(1)} %get-tuple-element.36), channel_id=1, source_target_pairs={{1,0},{0,1},{3,2},{2,3},{5,4},{4,5},{7,6},{6,7},{9,8},{8,9},{11,10... | collective-permute-start | bytes 196616 | tf_op jit(solution)/shard_map/ppermute | solution.py:278

commit v4 on v3

--- a/solution.py
+++ b/solution.py
@@ -61,7 +61,7 @@
     return value * c - other * s if back else value * c + other * s
 
 
-def message_kernel(code, klass, count, table, modes, v_ref, out_ref, aux_ref):
+def message_kernel(code, klass, count, table, v_ref, out_ref, w_ref):
     n = v_ref.shape[1]
     out_ref[:, :n] = v_ref[...]
     row = lax.broadcasted_iota(jnp.int32, (8, LANES), 0)
@@ -74,12 +74,7 @@
     first = row < NCODE
     out_ref[:, n : n + LANES] = jnp.where(first, high.astype(F32), low.astype(F32)).astype(BF16)
     out_ref[:, n + LANES :] = rest
-    aux_ref[:8, :] = w
-    rank = lax.broadcasted_iota(jnp.int32, (RANK, LANES), 0) % MODES
-    gain = jnp.zeros((RANK, LANES), F32)
-    for m in range(MODES):
-        gain = jnp.where(rank == m, modes[m] * F32(1.0 / 127.0), gain)
-    aux_ref[8:, :] = gain
+    w_ref[...] = w
 
 
 def weights_of(msg_ref):
@@ -104,25 +99,60 @@
         u_ref[j] = project(x, v_ref[:, j * BLOCK : (j + 1) * BLOCK], basis_ref[...])
 
 
-def own_kernel(x_ref, v_ref, u_ref, basis_ref, turns_ref):
+def at_end():
+    me = lax.axis_index("mem")
+    return (me == 0) | (me == 3)
+
+
+def chunk_of(u_ref, distance):
+    return u_ref.at[pl.ds((lax.axis_index("mem") ^ distance) * PAIR, PAIR)]
+
+
+def own_kernel(modes_ref, x_ref, v_ref, u_ref, basis_ref, turns_ref, l_ref, keep_ref, sem):
+    copy = pltpu.make_async_copy(x_ref, keep_ref, sem)
+    copy.start()
     write_basis(basis_ref)
     write_turns(turns_ref)
-    project_chunk(x_ref, v_ref, basis_ref, lax.axis_index("mem"), u_ref)
-
-
-def project_kernel(distance, x_ref, msg_ref, basis_ref, u_ref):
-    project_chunk(x_ref, msg_ref, basis_ref, lax.axis_index("mem") ^ distance, u_ref)
-
-
-def combine_kernel(x_ref, u0, u2, u3, aux_ref, m1, m2, m3, basis_ref, turns_ref, u_ref, w_ref, e_ref, o_ref):
+    row = lax.broadcasted_iota(jnp.int32, (RANK, MODES), 0) % MODES
+    lane = lax.broadcasted_iota(jnp.int32, (RANK, MODES), 1)
+    modes = modes_ref[...].reshape(1, MODES) * F32(1.0 / 127.0)
+    gain = jnp.sum(jnp.where(row == lane, modes, F32(0.0)), axis=1, keepdims=True)
+    l_ref[...] = basis_ref[...] * gain
+
+    @pl.when(at_end())
+    def _():
+        project_chunk(x_ref, v_ref, basis_ref, lax.axis_index("mem"), u_ref)
+
+    copy.wait()
+
+
+def project_kernel(distance, ends, x_ref, msg_ref, basis_ref, u_ref):
+    @pl.when(at_end() if ends else jnp.logical_not(at_end()))
+    def _():
+        project_chunk(x_ref, msg_ref, basis_ref, lax.axis_index("mem") ^ distance, u_ref)
+
+
+def edges_kernel(x_ref, u0, u2, u3, own_ref, m1, m2, m3, basis_ref, turns_ref, u_ref, w_ref, e_ref, o_ref):
     me = lax.axis_index("mem")
-    nblk = u_ref.shape[0]
-    project_chunk(x_ref, m1, basis_ref, me ^ 1, u_ref.at[pl.ds((me ^ 1) * PAIR, PAIR)])
-    for d, u in ((0, u0), (2, u2), (3, u3)):
+    nblk = x_ref.shape[1] // BLOCK
+    u_ref[...] = jnp.zeros_like(u_ref)
+
+    def keep(d, u):
         for j in range(PAIR):
             u_ref[(me ^ d) * PAIR + j] = u[j]
-    w_ref[me] = aux_ref[:NCODE, :]
-    for d, m in enumerate((m1, m2, m3), 1):
+
+    @pl.when(at_end())
+    def _():
+        keep(0, u0)
+        keep(3, u3)
+
+    @pl.when(jnp.logical_not(at_end()))
+    def _():
+        project_chunk(x_ref, m1, basis_ref, me ^ 1, chunk_of(u_ref, 1))
+        keep(2, u2)
+
+    w_ref[me] = own_ref[:NCODE, :]
+    for d, m in ((1, m1), (2, m2), (3, m3)):
         w_ref[me ^ d] = weights_of(m)
     turns = turns_ref[...]
     last = nblk - 1
@@ -148,9 +178,22 @@
     return jnp.sum(t.reshape(RANK, COLS, BLOCK) * l_ref[...][:, None, :], axis=0)
 
 
-def inner_kernel(x_ref, u_ref, w_ref, aux_ref, basis_ref, turns_ref, z_ref, y_ref, l_ref):
-    for c in range(0, BLOCK, LANES):
-        l_ref[:, c : c + LANES] = basis_ref[:, c : c + LANES] * aux_ref[8:, :]
+def inner_kernel(
+    x_ref, uin_ref, v_ref, m1, m2, m3, w_ref, l_ref, basis_ref, turns_ref, z_ref, y_ref, u_ref
+):
+    me = lax.axis_index("mem")
+    u_ref[...] = uin_ref[...]
+
+    @pl.when(at_end())
+    def _():
+        for d, m in ((1, m1), (2, m2)):
+            project_chunk(x_ref, m, basis_ref, me ^ d, chunk_of(u_ref, d))
+
+    @pl.when(jnp.logical_not(at_end()))
+    def _():
+        for d, m in ((0, v_ref), (3, m3)):
+            project_chunk(x_ref, m, basis_ref, me ^ d, chunk_of(u_ref, d))
+
     nblk = u_ref.shape[0]
     turns = turns_ref[...]
 
@@ -215,54 +258,59 @@
     nblk = wide // BLOCK
     shape = jax.ShapeDtypeStruct
     x = anomalies
-    msg, aux = pl.pallas_call(
+    msg, wown = pl.pallas_call(
         message_kernel,
-        out_shape=[shape((cols, width + TAIL), BF16), shape((8 + RANK, LANES), F32)],
-        in_specs=[SM] * 5 + [VM],
+        out_shape=[shape((cols, width + TAIL), BF16), shape((8, LANES), F32)],
+        in_specs=[SM] * 4 + [VM],
         out_specs=[VM] * 2,
+        compiler_params=LIMIT,
         name="message",
-    )(pair_code, pair_class, pair_count, taper_table, taper_modes, increments)
-    m1, m2, m3 = [lax.ppermute(msg, "mem", crossed(nmem, d)) for d in (1, 2, 3)]
+    )(pair_code, pair_class, pair_count, taper_table, increments)
+    m2, m3, m1 = [lax.ppermute(msg, "mem", crossed(nmem, d)) for d in (2, 3, 1)]
     chunk = shape((PAIR, members, LANES), F32)
     table = shape((RANK, BLOCK), F32)
-    u0, basis, turns = pl.pallas_call(
+    u0, basis, turns, left, x = pl.pallas_call(
         own_kernel,
-        out_shape=[chunk, table, shape((8, LANES), F32)],
-        in_specs=[VM] * 2,
-        out_specs=[VM] * 3,
+        out_shape=[chunk, table, shape((8, LANES), F32), table, shape(x.shape, x.dtype)],
+        in_specs=[VM] * 3,
+        out_specs=[VM] * 5,
+        scratch_shapes=[pltpu.SemaphoreType.DMA],
         compiler_params=LIMIT,
         name="own",
-    )(x, increments)
-    u3, u2 = [
+    )(taper_modes, x, msg)
+    u2, u3 = [
         pl.pallas_call(
-            functools.partial(project_kernel, d),
+            functools.partial(project_kernel, d, d == 3),
             out_shape=chunk,
             in_specs=[VM] * 3,
             out_specs=VM,
             compiler_params=LIMIT,
             name=f"project_{d}",
         )(x, m, basis)
-        for d, m in ((3, m3), (2, m2))
+        for d, m in ((2, m2), (3, m3))
     ]
-    uall, wall, e, o = pl.pallas_call(
-        combine_kernel,
-        out_shape=[shape((nblk, members, LANES), F32), shape((nmem, NCODE, LANES), F32), chunk, chunk],
+    products = shape((nblk, members, LANES), F32)
+    weights = shape((nmem, NCODE, LANES), F32)
+    uend, wall, e, o = pl.pallas_call(
+        edges_kernel,
+        out_shape=[products, weights, chunk, chunk],
         in_specs=[VM] * 10,
         out_specs=[VM] * 4,
         compiler_params=LIMIT,
-        name="combine",
-    )(x, u0, u2, u3, aux, m1, m2, m3, basis, turns)
+        name="edges",
+    )(x, u0, u2, u3, wown, m1, m2, m3, basis, turns)
     nb = lax.axis_size("blk")
     oin = lax.ppermute(o, "blk", partner(nb, 1))
     ein = lax.ppermute(e, "blk", partner(nb, 0))
-    z, yi, left = pl.pallas_call(
+    z, yi = pl.pallas_call(
         inner_kernel,
-        out_shape=[shape((4, members, LANES), F32), shape((2, cols, width), F32), table],
-        in_specs=[VM] * 6,
-        out_specs=[VM] * 3,
+        out_shape=[shape((4, members, LANES), F32), shape((2, cols, width), F32)],
+        in_specs=[VM] * 10,
+        out_specs=[VM] * 2,
+        scratch_shapes=[pltpu.VMEM((nblk, members, LANES), F32)],
         compiler_params=LIMIT,
         name="inner",
-    )(x, uall, wall, aux, basis, turns)
+    )(x, uend, msg, m1, m2, m3, wall, left, basis, turns)
     zo = z[:PAIR] + oin
     outs = pl.pallas_call(
         close_kernel,

time: 28.7 us -> 28.1 us (0.979)
  local copies, waits for them, and re-layouts: 1.23 us -> 2.07 us
  Pallas kernels: 6.24 us -> 5.41 us
  waiting for transfers between devices: 7.05 us -> 6.31 us
    pallas_call x3, Pallas kernels: 2.3 us -> 0.84 us  [the longest x2 0.74 us: body(): pl.pallas_call(functools.partial(project_kernel, d, d == 3), out_shape=ch...]
    ppermute x1, waiting for transfers between devices: 1.66 us -> 0.27 us  [body(): oin = lax.ppermute(o, 'blk', partner(nb, 1))]
    pallas_call x1, Pallas kernels: 0.82 us -> 2.22 us  [body(): pl.pallas_call(inner_kernel, out_shape=[shape((4, members, LANES), F32),...]
    ppermute x3, waiting for transfers between devices: 3.09 us -> 4.13 us  [body(): total = total + lax.ppermute(outs[d], 'mem', crossed(nmem, d)).astype(F32)]
    pallas_call x1, Pallas kernels: 1.51 us -> 0.57 us  [body(): pl.pallas_call(message_kernel, out_shape=[shape((cols, width + TAIL), BF1...]
    unnamed x6 -> x12, local copies, waits for them, and re-layouts: 1.23 us -> 2.07 us
    ppermute x3, waiting for transfers between devices: 2.29 us -> 1.91 us  [body(): m2, m3, m1 = [lax.ppermute(msg, 'mem', crossed(nmem, d)) for d in (2, 3, 1)]]
  transfers between devices with their start and end apart: 8 -> 8, of which waited for: 4 -> 5; matrix products, arithmetic and copies ran while one was open for 0% -> 0% of each run, Pallas kernels for 11% -> 14%
where the time goes in v4:
time: 28.1 us; the launch traced here: 27.9 us
  starting transfers between devices  12.6 us (45%)
  waiting for transfers between devices  6.31 us (22%)
  Pallas kernels  5.41 us (19%)
  local copies, waits for them, and re-layouts  2.07 us (7%)
  between operations  0.79 us (3%)
  other arithmetic  0.69 us (2%)
    ppermute x1, starting transfers between devices, body(): oin = lax.ppermute(o, 'blk', partner(nb, 1))  4.24 us
    ppermute x3, starting transfers between devices, body(): m2, m3, m1 = [lax.ppermute(msg, 'mem', crossed(nmem, d)) for d in (2, 3, 1)]  4.17 us
    ppermute x3, starting transfers between devices, body(): total = total + lax.ppermute(outs[d], 'mem', crossed(nmem, d)).astype(F32)  4.17 us
    ppermute x3, waiting for transfers between devices, body(): total = total + lax.ppermute(outs[d], 'mem', crossed(nmem, d)).astype(F32)  4.13 us
    pallas_call x1, Pallas kernels, body(): pl.pallas_call(inner_kernel, out_shape=[shape((4, members, LANES), F32),...  2.22 us
    unnamed x12, local copies, waits for them, and re-layouts  2.07 us
    ppermute x3, waiting for transfers between devices, body(): m2, m3, m1 = [lax.ppermute(msg, 'mem', crossed(nmem, d)) for d in (2, 3, 1)]  1.91 us
    pallas_call x1, Pallas kernels, body(): pl.pallas_call(own_kernel, out_shape=[chunk, table, shape((8, LANES), F32...  1 us
  transfers between devices with their start and end apart: 8, of which 5 were waited for; matrix products, arithmetic and copies ran while one was open for 0% of the time, Pallas kernels for 14%

profile of v4, /device:TPU:0, one launch (start us, length us, event | category | flops | bytes accessed | tf_op | source)
XLA Modules:
  0.0 27.9 jit_solution(17709407413915284675)
XLA Ops:
  0.0 0.0 copy-start.3
  0.7 0.0 copy-done.3
  0.7 0.0 copy-done.2
  0.7 0.0 copy-done.4
  0.7 0.0 copy-start.1
  0.7 0.8 %copy-done.1 = bf16[8,4096]{1,0:T(8,128)(2,1)S(1)} copy-done((bf16[8,4096]{1,0:T(8,128)(2,1)S(1)}, bf16[8,4096]{1,0:T(8,128)(2,1)}, u32[]{:S(2)}) %copy-start.1) | copy-done | bytes 65560
  1.6 0.6 %message.1 = (bf16[8,4352]{1,0:T(8,128)(2,1)S(1)}, f32[8,128]{1,0:T(8,128)S(1)}) custom-call(s32[4]{0:T(128)S(1)} %copy-done.2, s32[4]{0:T(128)S(1)} %copy-done.3, s32[1]{0:T(128)S(6)} %copy.8.count, f32[8]{0:T(128)S(1)} %copy-done.4, bf16[8,4096]{1,0:T(8,128)(2,1)S(1)} %copy-done.1), custom_call_target="tpu_custom_call" | custom-call | tf_op jit(solution)/shard_map/message/pallas_call | solution.py:261
  2.1 0.0 copy-start.5
  2.2 3.2 %collective-permute-start.1 = (bf16[8,4352]{1,0:T(8,128)(2,1)S(1)}, bf16[8,4352]{1,0:T(8,128)(2,1)S(1)}, u32[]{:S(2)}, u32[]{:S(2)}) collective-permute-start(bf16[8,4352]{1,0:T(8,128)(2,1)S(1)} %get-tuple-element.22.v_ref), channel_id=1, source_target_pairs={{3,0},{2,1},{1,2},{0,3},{7,4},{6,5},{5,6},{4,7},{11,8},{10,9},{9,1... | collective-permute-start | bytes 208904 | tf_op jit(solution)/shard_map/ppermute | solution.py:269
  5.3 0.6 %collective-permute-start = (bf16[8,4352]{1,0:T(8,128)(2,1)S(1)}, bf16[8,4352]{1,0:T(8,128)(2,1)S(1)}, u32[]{:S(2)}, u32[]{:S(2)}) collective-permute-start(bf16[8,4352]{1,0:T(8,128)(2,1)S(1)} %get-tuple-element.22.v_ref), channel_id=1, source_target_pairs={{2,0},{3,1},{0,2},{1,3},{6,4},{7,5},{4,6},{5,7},{10,8},{11,9},{8,1... | collective-permute-start | bytes 208904 | tf_op jit(solution)/shard_map/ppermute | solution.py:269
  6.0 0.4 %collective-permute-start.2 = (bf16[8,4352]{1,0:T(8,128)(2,1)S(1)}, bf16[8,4352]{1,0:T(8,128)(2,1)S(1)}, u32[]{:S(2)}, u32[]{:S(2)}) collective-permute-start(bf16[8,4352]{1,0:T(8,128)(2,1)S(1)} %get-tuple-element.22.v_ref), channel_id=1, source_target_pairs={{1,0},{0,1},{3,2},{2,3},{5,4},{4,5},{7,6},{6,7},{9,8},{8,9},{11,10... | collective-permute-start | bytes 208904 | tf_op jit(solution)/shard_map/ppermute | solution.py:269
  6.3 0.0 copy-done.5
  6.3 1.2 %copy-done = bf16[32,16384]{1,0:T(8,128)(2,1)S(1)} copy-done((bf16[32,16384]{1,0:T(8,128)(2,1)S(1)}, bf16[32,16384]{1,0:T(8,128)(2,1)}, u32[]{:S(2)}) %copy-start) | copy-done | bytes 1048600
  7.6 1.0 %own.1 = (f32[2,32,128]{2,1,0:T(8,128)S(1)}, f32[16,2048]{1,0:T(8,128)S(1)}, f32[8,128]{1,0:T(8,128)S(1)}, f32[16,2048]{1,0:T(8,128)S(1)}, bf16[32,16384]{1,0:T(8,128)(2,1)S(1)}) custom-call(f32[8]{0:T(128)S(1)} %copy-done.5, bf16[32,16384]{1,0:T(8,128)(2,1)S(1)} %copy-done, bf16[8,4352]{1,0:T(8,128)(2,1)S(1)} %get-tuple-element.22.v_ref), custom_call_target="tpu_custom_call" | custom-call | tf_op jit(solution)/shard_map/own/pallas_call | solution.py:272
  8.6 0.0 collective-permute-done.1.msg_ref.m3
  8.6 0.7 %project_3.1.u3 = f32[2,32,128]{2,1,0:T(8,128)S(1)} custom-call(bf16[32,16384]{1,0:T(8,128)(2,1)S(1)} %get-tuple-element.23.x_ref, bf16[8,4352]{1,0:T(8,128)(2,1)S(1)} %collective-permute-done.1.msg_ref.m3, f32[16,2048]{1,0:T(8,128)S(1)} %get-tuple-element.25.basis_ref), custom_call_target="tpu_custom_call" | custom-call | tf_op jit(solution)/shard_map/project_3/pallas_call | solution.py:282
  9.3 1.9 %collective-permute-done.msg_ref.m2 = bf16[8,4352]{1,0:T(8,128)(2,1)S(1)} collective-permute-done((bf16[8,4352]{1,0:T(8,128)(2,1)S(1)}, bf16[8,4352]{1,0:T(8,128)(2,1)S(1)}, u32[]{:S(2)}, u32[]{:S(2)}) %collective-permute-start) | collective-permute-done | bytes 69664 | tf_op jit(solution)/shard_map/ppermute | solution.py:269
  11.2 0.0 collective-permute-done.2.m1
  11.2 0.1 edges.1
  11.3 4.2 %collective-permute-start.3 = (f32[2,32,128]{2,1,0:T(8,128)S(1)}, f32[2,32,128]{2,1,0:T(8,128)S(1)}, u32[]{:S(2)}, u32[]{:S(2)}) collective-permute-start(f32[2,32,128]{2,1,0:T(8,128)S(1)} %get-tuple-element.32), channel_id=1, source_target_pairs={{4,8},{12,16},{20,24},{28,32},{36,40},{44,48},{52,56},{60,64},{68,... | collective-permute-start | bytes 98312 | tf_op jit(solution)/shard_map/ppermute | solution.py:303
  15.6 0.0 collective-permute-start.4
  15.6 2.2 %inner.1 = (f32[4,32,128]{2,1,0:T(8,128)S(1)}, f32[2,8,4096]{2,1,0:T(8,128)S(1)}) custom-call(bf16[32,16384]{1,0:T(8,128)(2,1)S(1)} %get-tuple-element.23.x_ref, f32[8,32,128]{2,1,0:T(8,128)S(1)} %get-tuple-element.28.uin_ref, bf16[8,4352]{1,0:T(8,128)(2,1)S(1)} %get-tuple-element.22.v_ref, bf16[8,4352]{1,0:T(8,128)(2,1)S(1)} %collective-permute-done.2.m1, ...), custom_call_target="tpu_custom_call" | custom-call | tf_op jit(solution)/shard_map/inner/pallas_call | solution.py:305
  17.8 0.3 collective-permute-done.3.oin_ref
  18.1 0.0 collective-permute-done.4.ein_ref
  18.1 0.8 %close.1 = (f32[8,4096]{1,0:T(8,128)S(1)}, bf16[8,4096]{1,0:T(8,128)(2,1)S(1)}, bf16[8,4096]{1,0:T(8,128)(2,1)S(1)}, bf16[8,4096]{1,0:T(8,128)(2,1)S(1)}) custom-call(bf16[32,16384]{1,0:T(8,128)(2,1)S(1)} %get-tuple-element.23.x_ref, f32[4,32,128]{2,1,0:T(8,128)S(1)} %get-tuple-element.31.z_ref, f32[2,32,128]{2,1,0:T(8,128)S(1)} %slice_add_fusion.zo_ref, ...), custom_call_target="tpu_custom_call" | custom-call | tf_op jit(solution)/shard_map/close/pallas_call | solution.py:315
  18.9 2.0 %collective-permute-start.5 = (bf16[8,4096]{1,0:T(8,128)(2,1)S(1)}, bf16[8,4096]{1,0:T(8,128)(2,1)S(1)}, u32[]{:S(2)}, u32[]{:S(2)}) collective-permute-start(bf16[8,4096]{1,0:T(8,128)(2,1)S(1)} %get-tuple-element.36), channel_id=1, source_target_pairs={{3,0},{2,1},{1,2},{0,3},{7,4},{6,5},{5,6},{4,7},{11,8},{10,9},{9,1... | collective-permute-start | bytes 196616 | tf_op jit(solution)/shard_map/ppermute | solution.py:326
  20.8 2.1 %collective-permute-start.6 = (bf16[8,4096]{1,0:T(8,128)(2,1)S(1)}, bf16[8,4096]{1,0:T(8,128)(2,1)S(1)}, u32[]{:S(2)}, u32[]{:S(2)}) collective-permute-start(bf16[8,4096]{1,0:T(8,128)(2,1)S(1)} %get-tuple-element.37), channel_id=1, source_target_pairs={{2,0},{3,1},{0,2},{1,3},{6,4},{7,5},{4,6},{5,7},{10,8},{11,9},{8,1... | collective-permute-start | bytes 196616 | tf_op jit(solution)/shard_map/ppermute | solution.py:326
  22.9 0.1 collective-permute-start.7
  23.0 1.4 %collective-permute-done.5 = bf16[8,4096]{1,0:T(8,128)(2,1)S(1)} collective-permute-done((bf16[8,4096]{1,0:T(8,128)(2,1)S(1)}, bf16[8,4096]{1,0:T(8,128)(2,1)S(1)}, u32[]{:S(2)}, u32[]{:S(2)}) %collective-permute-start.5) | collective-permute-done | bytes 65568 | tf_op jit(solution)/shard_map/ppermute | solution.py:326
  24.4 2.4 %collective-permute-done.6 = bf16[8,4096]{1,0:T(8,128)(2,1)S(1)} collective-permute-done((bf16[8,4096]{1,0:T(8,128)(2,1)S(1)}, bf16[8,4096]{1,0:T(8,128)(2,1)S(1)}, u32[]{:S(2)}, u32[]{:S(2)}) %collective-permute-start.6) | collective-permute-done | bytes 65568 | tf_op jit(solution)/shard_map/ppermute | solution.py:326
  26.8 0.4 %collective-permute-done.7 = bf16[8,4096]{1,0:T(8,128)(2,1)S(1)} collective-permute-done((bf16[8,4096]{1,0:T(8,128)(2,1)S(1)}, bf16[8,4096]{1,0:T(8,128)(2,1)S(1)}, u32[]{:S(2)}, u32[]{:S(2)}) %collective-permute-start.7) | collective-permute-done | bytes 65568 | tf_op jit(solution)/shard_map/ppermute | solution.py:326
  27.2 0.7 %convert_add_fusion = f32[8,4096]{1,0:T(8,128)} fusion(bf16[8,4096]{1,0:T(8,128)(2,1)S(1)} %collective-permute-done.7, bf16[8,4096]{1,0:T(8,128)(2,1)S(1)} %collective-permute-done.6, f32[8,4096]{1,0:T(8,128)S(1)} %get-tuple-element.35, bf16[8,4096]{1,0:T(8,128)(2,1)S(1)} %collective-permute-done.5), kind=kLoop, calls=%fused_computation | loop fusion | flops 196608 | bytes 458752 | tf_op jit(solution)/shard_map/add | solution.py:326
  (5 shorter events, 0.0 us)
Async XLA Ops:
  0.0 0.7 %copy-start.3 = (s32[4]{0:T(128)S(1)}, s32[4]{0:T(128)}, u32[]{:S(2)}) copy-start(s32[4]{0:T(128)} %klass.1) | copy-start | bytes 52
  0.0 0.7 %copy-start.2 = (s32[4]{0:T(128)S(1)}, s32[4]{0:T(128)}, u32[]{:S(2)}) copy-start(s32[4]{0:T(128)} %code.1) | copy-start | bytes 52
  0.0 0.7 %copy-start.4 = (f32[8]{0:T(128)S(1)}, f32[8]{0:T(128)}, u32[]{:S(2)}) copy-start(f32[8]{0:T(128)} %table.1) | copy-start | bytes 100
  0.7 0.8 %copy-start.1 = (bf16[8,4096]{1,0:T(8,128)(2,1)S(1)}, bf16[8,4096]{1,0:T(8,128)(2,1)}, u32[]{:S(2)}) copy-start(bf16[8,4096]{1,0:T(8,128)(2,1)} %v_ref.1) | copy-start | bytes 196612
  2.1 4.2 %copy-start.5 = (f32[8]{0:T(128)S(1)}, f32[8]{0:T(128)}, u32[]{:S(2)}) copy-start(f32[8]{0:T(128)} %modes_ref.1) | copy-start | bytes 100
  2.2 6.4 %collective-permute-start.1 = (bf16[8,4352]{1,0:T(8,128)(2,1)S(1)}, bf16[8,4352]{1,0:T(8,128)(2,1)S(1)}, u32[]{:S(2)}, u32[]{:S(2)}) collective-permute-start(bf16[8,4352]{1,0:T(8,128)(2,1)S(1)} %get-tuple-element.22.v_ref), channel_id=1, source_target_pairs={{3,0},{2,1},{1,2},{0,3},{7,4},{6,5},{5,6},{4,7},{11,8},{10,9},{9,1... | collective-permute-start | bytes 208904 | tf_op jit(solution)/shard_map/ppermute | solution.py:269
  5.3 5.9 %collective-permute-start = (bf16[8,4352]{1,0:T(8,128)(2,1)S(1)}, bf16[8,4352]{1,0:T(8,128)(2,1)S(1)}, u32[]{:S(2)}, u32[]{:S(2)}) collective-permute-start(bf16[8,4352]{1,0:T(8,128)(2,1)S(1)} %get-tuple-element.22.v_ref), channel_id=1, source_target_pairs={{2,0},{3,1},{0,2},{1,3},{6,4},{7,5},{4,6},{5,7},{10,8},{11,9},{8,1... | collective-permute-start | bytes 208904 | tf_op jit(solution)/shard_map/ppermute | solution.py:269
  6.0 5.3 %collective-permute-start.2 = (bf16[8,4352]{1,0:T(8,128)(2,1)S(1)}, bf16[8,4352]{1,0:T(8,128)(2,1)S(1)}, u32[]{:S(2)}, u32[]{:S(2)}) collective-permute-start(bf16[8,4352]{1,0:T(8,128)(2,1)S(1)} %get-tuple-element.22.v_ref), channel_id=1, source_target_pairs={{1,0},{0,1},{3,2},{2,3},{5,4},{4,5},{7,6},{6,7},{9,8},{8,9},{11,10... | collective-permute-start | bytes 208904 | tf_op jit(solution)/shard_map/ppermute | solution.py:269
  6.3 1.2 %copy-start = (bf16[32,16384]{1,0:T(8,128)(2,1)S(1)}, bf16[32,16384]{1,0:T(8,128)(2,1)}, u32[]{:S(2)}) copy-start(bf16[32,16384]{1,0:T(8,128)(2,1)} %x_ref.1) | copy-start | bytes 3145732
  11.3 6.7 %collective-permute-start.3 = (f32[2,32,128]{2,1,0:T(8,128)S(1)}, f32[2,32,128]{2,1,0:T(8,128)S(1)}, u32[]{:S(2)}, u32[]{:S(2)}) collective-permute-start(f32[2,32,128]{2,1,0:T(8,128)S(1)} %get-tuple-element.32), channel_id=1, source_target_pairs={{4,8},{12,16},{20,24},{28,32},{36,40},{44,48},{52,56},{60,64},{68,... | collective-permute-start | bytes 98312 | tf_op jit(solution)/shard_map/ppermute | solution.py:303
  15.6 2.5 %collective-permute-start.4 = (f32[2,32,128]{2,1,0:T(8,128)S(1)}, f32[2,32,128]{2,1,0:T(8,128)S(1)}, u32[]{:S(2)}, u32[]{:S(2)}) collective-permute-start(f32[2,32,128]{2,1,0:T(8,128)S(1)} %get-tuple-element.33), channel_id=1, source_target_pairs={{0,4},{8,12},{16,20},{24,28},{32,36},{40,44},{48,52},{56,60},{64,6... | collective-permute-start | bytes 98312 | tf_op jit(solution)/shard_map/ppermute | solution.py:304
  18.9 5.6 %collective-permute-start.5 = (bf16[8,4096]{1,0:T(8,128)(2,1)S(1)}, bf16[8,4096]{1,0:T(8,128)(2,1)S(1)}, u32[]{:S(2)}, u32[]{:S(2)}) collective-permute-start(bf16[8,4096]{1,0:T(8,128)(2,1)S(1)} %get-tuple-element.36), channel_id=1, source_target_pairs={{3,0},{2,1},{1,2},{0,3},{7,4},{6,5},{5,6},{4,7},{11,8},{10,9},{9,1... | collective-permute-start | bytes 196616 | tf_op jit(solution)/shard_map/ppermute | solution.py:326
  20.8 6.0 %collective-permute-start.6 = (bf16[8,4096]{1,0:T(8,128)(2,1)S(1)}, bf16[8,4096]{1,0:T(8,128)(2,1)S(1)}, u32[]{:S(2)}, u32[]{:S(2)}) collective-permute-start(bf16[8,4096]{1,0:T(8,128)(2,1)S(1)} %get-tuple-element.37), channel_id=1, source_target_pairs={{2,0},{3,1},{0,2},{1,3},{6,4},{7,5},{4,6},{5,7},{10,8},{11,9},{8,1... | collective-permute-start | bytes 196616 | tf_op jit(solution)/shard_map/ppermute | solution.py:326
  22.9 4.3 %collective-permute-start.7 = (bf16[8,4096]{1,0:T(8,128)(2,1)S(1)}, bf16[8,4096]{1,0:T(8,128)(2,1)S(1)}, u32[]{:S(2)}, u32[]{:S(2)}) collective-permute-start(bf16[8,4096]{1,0:T(8,128)(2,1)S(1)} %get-tuple-element.38), channel_id=1, source_target_pairs={{1,0},{0,1},{3,2},{2,3},{5,4},{4,5},{7,6},{6,7},{9,8},{8,9},{11,10... | collective-permute-start | bytes 196616 | tf_op jit(solution)/shard_map/ppermute | solution.py:326

commit v5 on v4

--- a/solution.py
+++ b/solution.py
@@ -61,9 +61,7 @@
     return value * c - other * s if back else value * c + other * s
 
 
-def message_kernel(code, klass, count, table, v_ref, out_ref, w_ref):
-    n = v_ref.shape[1]
-    out_ref[:, :n] = v_ref[...]
+def tables_kernel(code, klass, count, table, basis_ref, turns_ref, w_ref, tail_ref):
     row = lax.broadcasted_iota(jnp.int32, (8, LANES), 0)
     w = jnp.zeros((8, LANES), F32)
     for slot in range(NCODE):
@@ -71,10 +69,17 @@
         w = w + jnp.where(row % NCODE == code[slot], rho, F32(0.0))
     high, low = split(w)
     rest = (w - high.astype(F32) - low.astype(F32)).astype(BF16)
-    first = row < NCODE
-    out_ref[:, n : n + LANES] = jnp.where(first, high.astype(F32), low.astype(F32)).astype(BF16)
-    out_ref[:, n + LANES :] = rest
+    tail_ref[:, :LANES] = jnp.where(row < NCODE, high.astype(F32), low.astype(F32)).astype(BF16)
+    tail_ref[:, LANES:] = rest
     w_ref[...] = w
+    write_basis(basis_ref)
+    write_turns(turns_ref)
+
+
+def message_kernel(v_ref, tail_ref, out_ref):
+    n = v_ref.shape[1]
+    out_ref[:, :n] = v_ref[...]
+    out_ref[:, n:] = tail_ref[...]
 
 
 def weights_of(msg_ref):
@@ -108,11 +113,9 @@
     return u_ref.at[pl.ds((lax.axis_index("mem") ^ distance) * PAIR, PAIR)]
 
 
-def own_kernel(modes_ref, x_ref, v_ref, u_ref, basis_ref, turns_ref, l_ref, keep_ref, sem):
+def own_kernel(modes_ref, x_ref, v_ref, basis_ref, u_ref, l_ref, keep_ref, sem):
     copy = pltpu.make_async_copy(x_ref, keep_ref, sem)
     copy.start()
-    write_basis(basis_ref)
-    write_turns(turns_ref)
     row = lax.broadcasted_iota(jnp.int32, (RANK, MODES), 0) % MODES
     lane = lax.broadcasted_iota(jnp.int32, (RANK, MODES), 1)
     modes = modes_ref[...].reshape(1, MODES) * F32(1.0 / 127.0)
@@ -258,26 +261,35 @@
     nblk = wide // BLOCK
     shape = jax.ShapeDtypeStruct
     x = anomalies
-    msg, wown = pl.pallas_call(
+    table = shape((RANK, BLOCK), F32)
+    basis, turns, wown, tail = pl.pallas_call(
+        tables_kernel,
+        out_shape=[table, shape((8, LANES), F32), shape((8, LANES), F32), shape((cols, TAIL), BF16)],
+        in_specs=[SM] * 4,
+        out_specs=[VM] * 4,
+        compiler_params=LIMIT,
+        cost_estimate=pl.CostEstimate(flops=1000000000, bytes_accessed=4000000, transcendentals=0),
+        name="tables",
+    )(pair_code, pair_class, pair_count, taper_table)
+    msg = pl.pallas_call(
         message_kernel,
-        out_shape=[shape((cols, width + TAIL), BF16), shape((8, LANES), F32)],
-        in_specs=[SM] * 4 + [VM],
-        out_specs=[VM] * 2,
+        out_shape=shape((cols, width + TAIL), BF16),
+        in_specs=[VM] * 2,
+        out_specs=VM,
         compiler_params=LIMIT,
         name="message",
-    )(pair_code, pair_class, pair_count, taper_table, increments)
+    )(increments, tail)
     m2, m3, m1 = [lax.ppermute(msg, "mem", crossed(nmem, d)) for d in (2, 3, 1)]
     chunk = shape((PAIR, members, LANES), F32)
-    table = shape((RANK, BLOCK), F32)
-    u0, basis, turns, left, x = pl.pallas_call(
+    u0, left, x = pl.pallas_call(
         own_kernel,
-        out_shape=[chunk, table, shape((8, LANES), F32), table, shape(x.shape, x.dtype)],
-        in_specs=[VM] * 3,
-        out_specs=[VM] * 5,
+        out_shape=[chunk, table, shape(x.shape, x.dtype)],
+        in_specs=[VM] * 4,
+        out_specs=[VM] * 3,
         scratch_shapes=[pltpu.SemaphoreType.DMA],
         compiler_params=LIMIT,
         name="own",
-    )(taper_modes, x, msg)
+    )(taper_modes, x, msg, basis)
     u2, u3 = [
         pl.pallas_call(
             functools.partial(project_kernel, d, d == 3),

time: 28.1 us -> 27.4 us (0.975)
  local copies, waits for them, and re-layouts: 2.07 us -> 0.11 us
  waiting for transfers between devices: 6.31 us -> 7.64 us
    unnamed x12, local copies, waits for them, and re-layouts: 2.07 us -> 0.11 us
    ppermute x3, waiting for transfers between devices: 1.91 us -> 3.24 us  [body(): m2, m3, m1 = [lax.ppermute(msg, 'mem', crossed(nmem, d)) for d in (2, 3, 1)]]
    pallas_call x2 -> x3, Pallas kernels: 1.57 us -> 1.65 us  [the longest x1 0.92 us: body(): pl.pallas_call(own_kernel, out_shape=[chunk, table, shape(x.shape, x.dtyp...]
  transfers between devices with their start and end apart: 8 -> 8, of which waited for: 5 -> 6; matrix products, arithmetic and copies ran while one was open for 0% -> 0% of each run, Pallas kernels for 14% -> 14%
where the time goes in v5:
time: 27.4 us; the launch traced here: 27.3 us
  starting transfers between devices  12.6 us (46%)
  waiting for transfers between devices  7.64 us (28%)
  Pallas kernels  5.48 us (20%)
  between operations  0.78 us (3%)
  other arithmetic  0.7 us (3%)
    ppermute x1, starting transfers between devices, body(): oin = lax.ppermute(o, 'blk', partner(nb, 1))  4.24 us
    ppermute x3, starting transfers between devices, body(): m2, m3, m1 = [lax.ppermute(msg, 'mem', crossed(nmem, d)) for d in (2, 3, 1)]  4.17 us
    ppermute x3, starting transfers between devices, body(): total = total + lax.ppermute(outs[d], 'mem', crossed(nmem, d)).astype(F32)  4.17 us
    ppermute x3, waiting for transfers between devices, body(): total = total + lax.ppermute(outs[d], 'mem', crossed(nmem, d)).astype(F32)  4.13 us
    ppermute x3, waiting for transfers between devices, body(): m2, m3, m1 = [lax.ppermute(msg, 'mem', crossed(nmem, d)) for d in (2, 3, 1)]  3.24 us
    pallas_call x1, Pallas kernels, body(): pl.pallas_call(inner_kernel, out_shape=[shape((4, members, LANES), F32),...  2.22 us
    pallas_call x1, Pallas kernels, body(): pl.pallas_call(own_kernel, out_shape=[chunk, table, shape(x.shape, x.dtyp...  0.92 us
    pallas_call x1, Pallas kernels, body(): pl.pallas_call(close_kernel, out_shape=[shape((cols, width), F32)] + [sha...  0.78 us
  transfers between devices with their start and end apart: 8, of which 6 were waited for; matrix products, arithmetic and copies ran while one was open for 0% of the time, Pallas kernels for 14%

profile of v5, /device:TPU:0, one launch (start us, length us, event | category | flops | bytes accessed | tf_op | source)
XLA Modules:
  0.0 27.3 jit_solution(14184615476931171285)
XLA Ops:
  0.0 0.0 copy-start.4
  0.7 0.0 copy-done.4
  0.7 0.0 copy-done.3
  0.7 0.0 copy-done.5
  0.7 0.0 copy-start.1
  0.7 0.0 copy-start
  0.7 0.7 %tables.1 = (f32[16,2048]{1,0:T(8,128)S(1)}, f32[8,128]{1,0:T(8,128)S(1)}, f32[8,128]{1,0:T(8,128)S(1)}, bf16[8,256]{1,0:T(8,128)(2,1)S(1)}) custom-call(s32[4]{0:T(128)S(1)} %copy-done.3, s32[4]{0:T(128)S(1)} %copy-done.4, s32[1]{0:T(128)S(6)} %copy.8.count, f32[8]{0:T(128)S(1)} %copy-done.5), custom_call_target="tpu_custom_call" | custom-call | flops 1000000000 | bytes 4000000 | tf_op jit(solution)/shard_map/tables/pallas_call | solution.py:265
  1.5 0.1 copy-done.1
  1.6 3.2 %collective-permute-start.1 = (bf16[8,4352]{1,0:T(8,128)(2,1)S(1)}, bf16[8,4352]{1,0:T(8,128)(2,1)S(1)}, u32[]{:S(2)}, u32[]{:S(2)}) collective-permute-start(bf16[8,4352]{1,0:T(8,128)(2,1)S(1)} %message.1.v_ref), channel_id=1, source_target_pairs={{3,0},{2,1},{1,2},{0,3},{7,4},{6,5},{5,6},{4,7},{11,8},{10,9},{9,1... | collective-permute-start | bytes 208904 | tf_op jit(solution)/shard_map/ppermute | solution.py:282
  4.8 0.6 %collective-permute-start = (bf16[8,4352]{1,0:T(8,128)(2,1)S(1)}, bf16[8,4352]{1,0:T(8,128)(2,1)S(1)}, u32[]{:S(2)}, u32[]{:S(2)}) collective-permute-start(bf16[8,4352]{1,0:T(8,128)(2,1)S(1)} %message.1.v_ref), channel_id=1, source_target_pairs={{2,0},{3,1},{0,2},{1,3},{6,4},{7,5},{4,6},{5,7},{10,8},{11,9},{8,1... | collective-permute-start | bytes 208904 | tf_op jit(solution)/shard_map/ppermute | solution.py:282
  5.4 0.4 %collective-permute-start.2 = (bf16[8,4352]{1,0:T(8,128)(2,1)S(1)}, bf16[8,4352]{1,0:T(8,128)(2,1)S(1)}, u32[]{:S(2)}, u32[]{:S(2)}) collective-permute-start(bf16[8,4352]{1,0:T(8,128)(2,1)S(1)} %message.1.v_ref), channel_id=1, source_target_pairs={{1,0},{0,1},{3,2},{2,3},{5,4},{4,5},{7,6},{6,7},{9,8},{8,9},{11,10... | collective-permute-start | bytes 208904 | tf_op jit(solution)/shard_map/ppermute | solution.py:282
  5.8 0.0 copy-done
  5.8 0.0 copy-done.2
  5.8 0.9 %own.1 = (f32[2,32,128]{2,1,0:T(8,128)S(1)}, f32[16,2048]{1,0:T(8,128)S(1)}, bf16[32,16384]{1,0:T(8,128)(2,1)S(1)}) custom-call(f32[8]{0:T(128)S(1)} %copy-done.2, bf16[32,16384]{1,0:T(8,128)(2,1)S(1)} %copy-done, bf16[8,4352]{1,0:T(8,128)(2,1)S(1)} %message.1.v_ref, f32[16,2048]{1,0:T(8,128)S(1)} %get-tuple-element.23.basis_ref), custom_call_target="tpu_custom_call" | custom-call | tf_op jit(solution)/shard_map/own/pallas_call | solution.py:284
  6.7 0.8 %collective-permute-done.1.msg_ref.m3 = bf16[8,4352]{1,0:T(8,128)(2,1)S(1)} collective-permute-done((bf16[8,4352]{1,0:T(8,128)(2,1)S(1)}, bf16[8,4352]{1,0:T(8,128)(2,1)S(1)}, u32[]{:S(2)}, u32[]{:S(2)}) %collective-permute-start.1) | collective-permute-done | bytes 69664 | tf_op jit(solution)/shard_map/ppermute | solution.py:282
  7.5 0.7 %project_3.1.u3 = f32[2,32,128]{2,1,0:T(8,128)S(1)} custom-call(bf16[32,16384]{1,0:T(8,128)(2,1)S(1)} %get-tuple-element.24.x_ref, bf16[8,4352]{1,0:T(8,128)(2,1)S(1)} %collective-permute-done.1.msg_ref.m3, f32[16,2048]{1,0:T(8,128)S(1)} %get-tuple-element.23.basis_ref), custom_call_target="tpu_custom_call" | custom-call | tf_op jit(solution)/shard_map/project_3/pallas_call | solution.py:294
  8.2 2.5 %collective-permute-done.msg_ref.m2 = bf16[8,4352]{1,0:T(8,128)(2,1)S(1)} collective-permute-done((bf16[8,4352]{1,0:T(8,128)(2,1)S(1)}, bf16[8,4352]{1,0:T(8,128)(2,1)S(1)}, u32[]{:S(2)}, u32[]{:S(2)}) %collective-permute-start) | collective-permute-done | bytes 69664 | tf_op jit(solution)/shard_map/ppermute | solution.py:282
  10.7 0.0 collective-permute-done.2.m1
  10.7 0.1 edges.1
  10.8 4.2 %collective-permute-start.3 = (f32[2,32,128]{2,1,0:T(8,128)S(1)}, f32[2,32,128]{2,1,0:T(8,128)S(1)}, u32[]{:S(2)}, u32[]{:S(2)}) collective-permute-start(f32[2,32,128]{2,1,0:T(8,128)S(1)} %get-tuple-element.32), channel_id=1, source_target_pairs={{4,8},{12,16},{20,24},{28,32},{36,40},{44,48},{52,56},{60,64},{68,... | collective-permute-start | bytes 98312 | tf_op jit(solution)/shard_map/ppermute | solution.py:315
  15.0 0.0 collective-permute-start.4
  15.0 2.2 %inner.1 = (f32[4,32,128]{2,1,0:T(8,128)S(1)}, f32[2,8,4096]{2,1,0:T(8,128)S(1)}) custom-call(bf16[32,16384]{1,0:T(8,128)(2,1)S(1)} %get-tuple-element.24.x_ref, f32[8,32,128]{2,1,0:T(8,128)S(1)} %get-tuple-element.28.uin_ref, bf16[8,4352]{1,0:T(8,128)(2,1)S(1)} %message.1.v_ref, bf16[8,4352]{1,0:T(8,128)(2,1)S(1)} %collective-permute-done.2.m1, ...), custom_call_target="tpu_custom_call" | custom-call | tf_op jit(solution)/shard_map/inner/pallas_call | solution.py:317
  17.2 0.3 collective-permute-done.3.oin_ref
  17.5 0.0 collective-permute-done.4.ein_ref
  17.5 0.8 %close.1 = (f32[8,4096]{1,0:T(8,128)S(1)}, bf16[8,4096]{1,0:T(8,128)(2,1)S(1)}, bf16[8,4096]{1,0:T(8,128)(2,1)S(1)}, bf16[8,4096]{1,0:T(8,128)(2,1)S(1)}) custom-call(bf16[32,16384]{1,0:T(8,128)(2,1)S(1)} %get-tuple-element.24.x_ref, f32[4,32,128]{2,1,0:T(8,128)S(1)} %get-tuple-element.31.z_ref, f32[2,32,128]{2,1,0:T(8,128)S(1)} %slice_add_fusion.zo_ref, ...), custom_call_target="tpu_custom_call" | custom-call | tf_op jit(solution)/shard_map/close/pallas_call | solution.py:327
  18.3 2.0 %collective-permute-start.5 = (bf16[8,4096]{1,0:T(8,128)(2,1)S(1)}, bf16[8,4096]{1,0:T(8,128)(2,1)S(1)}, u32[]{:S(2)}, u32[]{:S(2)}) collective-permute-start(bf16[8,4096]{1,0:T(8,128)(2,1)S(1)} %get-tuple-element.36), channel_id=1, source_target_pairs={{3,0},{2,1},{1,2},{0,3},{7,4},{6,5},{5,6},{4,7},{11,8},{10,9},{9,1... | collective-permute-start | bytes 196616 | tf_op jit(solution)/shard_map/ppermute | solution.py:338
  20.3 2.1 %collective-permute-start.6 = (bf16[8,4096]{1,0:T(8,128)(2,1)S(1)}, bf16[8,4096]{1,0:T(8,128)(2,1)S(1)}, u32[]{:S(2)}, u32[]{:S(2)}) collective-permute-start(bf16[8,4096]{1,0:T(8,128)(2,1)S(1)} %get-tuple-element.37), channel_id=1, source_target_pairs={{2,0},{3,1},{0,2},{1,3},{6,4},{7,5},{4,6},{5,7},{10,8},{11,9},{8,1... | collective-permute-start | bytes 196616 | tf_op jit(solution)/shard_map/ppermute | solution.py:338
  22.3 0.1 collective-permute-start.7
  22.5 1.4 %collective-permute-done.5 = bf16[8,4096]{1,0:T(8,128)(2,1)S(1)} collective-permute-done((bf16[8,4096]{1,0:T(8,128)(2,1)S(1)}, bf16[8,4096]{1,0:T(8,128)(2,1)S(1)}, u32[]{:S(2)}, u32[]{:S(2)}) %collective-permute-start.5) | collective-permute-done | bytes 65568 | tf_op jit(solution)/shard_map/ppermute | solution.py:338
  23.9 2.4 %collective-permute-done.6 = bf16[8,4096]{1,0:T(8,128)(2,1)S(1)} collective-permute-done((bf16[8,4096]{1,0:T(8,128)(2,1)S(1)}, bf16[8,4096]{1,0:T(8,128)(2,1)S(1)}, u32[]{:S(2)}, u32[]{:S(2)}) %collective-permute-start.6) | collective-permute-done | bytes 65568 | tf_op jit(solution)/shard_map/ppermute | solution.py:338
  26.3 0.3 %collective-permute-done.7 = bf16[8,4096]{1,0:T(8,128)(2,1)S(1)} collective-permute-done((bf16[8,4096]{1,0:T(8,128)(2,1)S(1)}, bf16[8,4096]{1,0:T(8,128)(2,1)S(1)}, u32[]{:S(2)}, u32[]{:S(2)}) %collective-permute-start.7) | collective-permute-done | bytes 65568 | tf_op jit(solution)/shard_map/ppermute | solution.py:338
  26.6 0.7 %convert_add_fusion = f32[8,4096]{1,0:T(8,128)} fusion(bf16[8,4096]{1,0:T(8,128)(2,1)S(1)} %collective-permute-done.7, bf16[8,4096]{1,0:T(8,128)(2,1)S(1)} %collective-permute-done.6, f32[8,4096]{1,0:T(8,128)S(1)} %get-tuple-element.35, bf16[8,4096]{1,0:T(8,128)(2,1)S(1)} %collective-permute-done.5), kind=kLoop, calls=%fused_computation | loop fusion | flops 196608 | bytes 458752 | tf_op jit(solution)/shard_map/add | solution.py:338
  (6 shorter events, 0.0 us)
Async XLA Ops:
  0.0 0.7 %copy-start.4 = (s32[4]{0:T(128)S(1)}, s32[4]{0:T(128)}, u32[]{:S(2)}) copy-start(s32[4]{0:T(128)} %klass.1) | copy-start | bytes 52
  0.0 0.7 %copy-start.3 = (s32[4]{0:T(128)S(1)}, s32[4]{0:T(128)}, u32[]{:S(2)}) copy-start(s32[4]{0:T(128)} %code.1) | copy-start | bytes 52
  0.0 0.7 %copy-start.5 = (f32[8]{0:T(128)S(1)}, f32[8]{0:T(128)}, u32[]{:S(2)}) copy-start(f32[8]{0:T(128)} %table.1) | copy-start | bytes 100
  0.7 0.8 %copy-start.1 = (bf16[8,4096]{1,0:T(8,128)(2,1)S(1)}, bf16[8,4096]{1,0:T(8,128)(2,1)}, u32[]{:S(2)}) copy-start(bf16[8,4096]{1,0:T(8,128)(2,1)} %v_ref.1) | copy-start | bytes 196612
  0.7 5.0 %copy-start = (bf16[32,16384]{1,0:T(8,128)(2,1)S(1)}, bf16[32,16384]{1,0:T(8,128)(2,1)}, u32[]{:S(2)}) copy-start(bf16[32,16384]{1,0:T(8,128)(2,1)} %x_ref.1) | copy-start | bytes 3145732
  1.6 4.2 %copy-start.2 = (f32[8]{0:T(128)S(1)}, f32[8]{0:T(128)}, u32[]{:S(2)}) copy-start(f32[8]{0:T(128)} %modes_ref.1) | copy-start | bytes 100
  1.6 5.9 %collective-permute-start.1 = (bf16[8,4352]{1,0:T(8,128)(2,1)S(1)}, bf16[8,4352]{1,0:T(8,128)(2,1)S(1)}, u32[]{:S(2)}, u32[]{:S(2)}) collective-permute-start(bf16[8,4352]{1,0:T(8,128)(2,1)S(1)} %message.1.v_ref), channel_id=1, source_target_pairs={{3,0},{2,1},{1,2},{0,3},{7,4},{6,5},{5,6},{4,7},{11,8},{10,9},{9,1... | collective-permute-start | bytes 208904 | tf_op jit(solution)/shard_map/ppermute | solution.py:282
  4.8 5.9 %collective-permute-start = (bf16[8,4352]{1,0:T(8,128)(2,1)S(1)}, bf16[8,4352]{1,0:T(8,128)(2,1)S(1)}, u32[]{:S(2)}, u32[]{:S(2)}) collective-permute-start(bf16[8,4352]{1,0:T(8,128)(2,1)S(1)} %message.1.v_ref), channel_id=1, source_target_pairs={{2,0},{3,1},{0,2},{1,3},{6,4},{7,5},{4,6},{5,7},{10,8},{11,9},{8,1... | collective-permute-start | bytes 208904 | tf_op jit(solution)/shard_map/ppermute | solution.py:282
  5.4 5.3 %collective-permute-start.2 = (bf16[8,4352]{1,0:T(8,128)(2,1)S(1)}, bf16[8,4352]{1,0:T(8,128)(2,1)S(1)}, u32[]{:S(2)}, u32[]{:S(2)}) collective-permute-start(bf16[8,4352]{1,0:T(8,128)(2,1)S(1)} %message.1.v_ref), channel_id=1, source_target_pairs={{1,0},{0,1},{3,2},{2,3},{5,4},{4,5},{7,6},{6,7},{9,8},{8,9},{11,10... | collective-permute-start | bytes 208904 | tf_op jit(solution)/shard_map/ppermute | solution.py:282
  10.8 6.7 %collective-permute-start.3 = (f32[2,32,128]{2,1,0:T(8,128)S(1)}, f32[2,32,128]{2,1,0:T(8,128)S(1)}, u32[]{:S(2)}, u32[]{:S(2)}) collective-permute-start(f32[2,32,128]{2,1,0:T(8,128)S(1)} %get-tuple-element.32), channel_id=1, source_target_pairs={{4,8},{12,16},{20,24},{28,32},{36,40},{44,48},{52,56},{60,64},{68,... | collective-permute-start | bytes 98312 | tf_op jit(solution)/shard_map/ppermute | solution.py:315
  15.0 2.5 %collective-permute-start.4 = (f32[2,32,128]{2,1,0:T(8,128)S(1)}, f32[2,32,128]{2,1,0:T(8,128)S(1)}, u32[]{:S(2)}, u32[]{:S(2)}) collective-permute-start(f32[2,32,128]{2,1,0:T(8,128)S(1)} %get-tuple-element.33), channel_id=1, source_target_pairs={{0,4},{8,12},{16,20},{24,28},{32,36},{40,44},{48,52},{56,60},{64,6... | collective-permute-start | bytes 98312 | tf_op jit(solution)/shard_map/ppermute | solution.py:316
  18.3 5.6 %collective-permute-start.5 = (bf16[8,4096]{1,0:T(8,128)(2,1)S(1)}, bf16[8,4096]{1,0:T(8,128)(2,1)S(1)}, u32[]{:S(2)}, u32[]{:S(2)}) collective-permute-start(bf16[8,4096]{1,0:T(8,128)(2,1)S(1)} %get-tuple-element.36), channel_id=1, source_target_pairs={{3,0},{2,1},{1,2},{0,3},{7,4},{6,5},{5,6},{4,7},{11,8},{10,9},{9,1... | collective-permute-start | bytes 196616 | tf_op jit(solution)/shard_map/ppermute | solution.py:338
  20.3 6.0 %collective-permute-start.6 = (bf16[8,4096]{1,0:T(8,128)(2,1)S(1)}, bf16[8,4096]{1,0:T(8,128)(2,1)S(1)}, u32[]{:S(2)}, u32[]{:S(2)}) collective-permute-start(bf16[8,4096]{1,0:T(8,128)(2,1)S(1)} %get-tuple-element.37), channel_id=1, source_target_pairs={{2,0},{3,1},{0,2},{1,3},{6,4},{7,5},{4,6},{5,7},{10,8},{11,9},{8,1... | collective-permute-start | bytes 196616 | tf_op jit(solution)/shard_map/ppermute | solution.py:338
  22.3 4.3 %collective-permute-start.7 = (bf16[8,4096]{1,0:T(8,128)(2,1)S(1)}, bf16[8,4096]{1,0:T(8,128)(2,1)S(1)}, u32[]{:S(2)}, u32[]{:S(2)}) collective-permute-start(bf16[8,4096]{1,0:T(8,128)(2,1)S(1)} %get-tuple-element.38), channel_id=1, source_target_pairs={{1,0},{0,1},{3,2},{2,3},{5,4},{4,5},{7,6},{6,7},{9,8},{8,9},{11,10... | collective-permute-start | bytes 196616 | tf_op jit(solution)/shard_map/ppermute | solution.py:338

commit v6 on v5

--- a/solution.py
+++ b/solution.py
@@ -122,52 +122,70 @@
     gain = jnp.sum(jnp.where(row == lane, modes, F32(0.0)), axis=1, keepdims=True)
     l_ref[...] = basis_ref[...] * gain
 
-    @pl.when(at_end())
-    def _():
-        project_chunk(x_ref, v_ref, basis_ref, lax.axis_index("mem"), u_ref)
-
+    project_chunk(x_ref, v_ref, basis_ref, lax.axis_index("mem"), u_ref)
     copy.wait()
 
 
-def project_kernel(distance, ends, x_ref, msg_ref, basis_ref, u_ref):
-    @pl.when(at_end() if ends else jnp.logical_not(at_end()))
+def project_kernel(distance, every, x_ref, msg_ref, basis_ref, u_ref):
+    @pl.when(every | jnp.logical_not(at_end()))
     def _():
         project_chunk(x_ref, msg_ref, basis_ref, lax.axis_index("mem") ^ distance, u_ref)
 
 
-def edges_kernel(x_ref, u0, u2, u3, own_ref, m1, m2, m3, basis_ref, turns_ref, u_ref, w_ref, e_ref, o_ref):
-    me = lax.axis_index("mem")
-    nblk = x_ref.shape[1] // BLOCK
-    u_ref[...] = jnp.zeros_like(u_ref)
-
-    def keep(d, u):
-        for j in range(PAIR):
-            u_ref[(me ^ d) * PAIR + j] = u[j]
-
-    @pl.when(at_end())
+def one_needed():
+    even = lax.axis_index("blk") % 2 == 0
+    return lax.axis_index("mem") == jnp.where(even, 1, 2)
+
+
+def piece(target, parts):
+    d = lax.axis_index("mem") ^ target
+    found = [parts[0][j] for j in range(PAIR)]
+    for k in range(1, len(parts)):
+        found = [jnp.where(d == k, parts[k][j], found[j]) for j in range(PAIR)]
+    return found
+
+
+def ahead_of(high, w, turns):
+    return (
+        turned(high[0], turns, 2, True) * w[1:2] + turned(high[1], turns, 1, True) * w[2:3],
+        turned(high[1], turns, 2, True) * w[3:4],
+    )
+
+
+def outward_kernel(x_ref, u0, u2, u3, own_ref, m1, m2, m3, basis_ref, turns_ref, u1_ref, w_ref, o_ref):
+    me = lax.axis_index("mem")
+    u1_ref[...] = jnp.zeros_like(u1_ref)
+
+    @pl.when(one_needed())
     def _():
-        keep(0, u0)
-        keep(3, u3)
-
-    @pl.when(jnp.logical_not(at_end()))
-    def _():
-        project_chunk(x_ref, m1, basis_ref, me ^ 1, chunk_of(u_ref, 1))
-        keep(2, u2)
+        project_chunk(x_ref, m1, basis_ref, me ^ 1, u1_ref)
 
     w_ref[me] = own_ref[:NCODE, :]
     for d, m in ((1, m1), (2, m2), (3, m3)):
         w_ref[me ^ d] = weights_of(m)
-    turns = turns_ref[...]
-    last = nblk - 1
-    w = w_ref[last // PAIR]
     even = lax.axis_index("blk") % 2 == 0
-    ahead = (
-        turned(u_ref[last - 1], turns, 2, True) * w[1:2] + turned(u_ref[last], turns, 1, True) * w[2:3],
-        turned(u_ref[last], turns, 2, True) * w[3:4],
-    )
+    parts = (u0, u1_ref, u2, u3)
+    ahead = ahead_of(piece(3, parts), w_ref[3], turns_ref[...])
+    low = piece(0, parts)
+    for j in range(PAIR):
+        o_ref[j] = jnp.where(even, low[j], ahead[j])
+
+
+def inward_kernel(x_ref, u0, u1, u2, u3, m1, w_ref, basis_ref, turns_ref, u_ref, e_ref):
+    me = lax.axis_index("mem")
+    for d, u in enumerate((u0, u1, u2, u3)):
+        for j in range(PAIR):
+            u_ref[(me ^ d) * PAIR + j] = u[j]
+
+    @pl.when(jnp.logical_not(at_end() | one_needed()))
+    def _():
+        project_chunk(x_ref, m1, basis_ref, me ^ 1, chunk_of(u_ref, 1))
+
+    even = lax.axis_index("blk") % 2 == 0
+    last = u_ref.shape[0] - 1
+    ahead = ahead_of((u_ref[last - 1], u_ref[last]), w_ref[3], turns_ref[...])
     for j in range(PAIR):
         e_ref[j] = jnp.where(even, ahead[j], u_ref[j])
-        o_ref[j] = jnp.where(even, u_ref[j], ahead[j])
 
 
 def expand(x, z, l_ref):
@@ -182,7 +200,7 @@
 
 
 def inner_kernel(
-    x_ref, uin_ref, v_ref, m1, m2, m3, w_ref, l_ref, basis_ref, turns_ref, z_ref, y_ref, u_ref
+    x_ref, uin_ref, m1, m2, w_ref, l_ref, basis_ref, turns_ref, z_ref, y_ref, u_ref
 ):
     me = lax.axis_index("mem")
     u_ref[...] = uin_ref[...]
@@ -190,11 +208,6 @@
     @pl.when(at_end())
     def _():
         for d, m in ((1, m1), (2, m2)):
-            project_chunk(x_ref, m, basis_ref, me ^ d, chunk_of(u_ref, d))
-
-    @pl.when(jnp.logical_not(at_end()))
-    def _():
-        for d, m in ((0, v_ref), (3, m3)):
             project_chunk(x_ref, m, basis_ref, me ^ d, chunk_of(u_ref, d))
 
     nblk = u_ref.shape[0]
@@ -303,26 +316,34 @@
     ]
     products = shape((nblk, members, LANES), F32)
     weights = shape((nmem, NCODE, LANES), F32)
-    uend, wall, e, o = pl.pallas_call(
-        edges_kernel,
-        out_shape=[products, weights, chunk, chunk],
+    u1, wall, o = pl.pallas_call(
+        outward_kernel,
+        out_shape=[chunk, weights, chunk],
         in_specs=[VM] * 10,
-        out_specs=[VM] * 4,
-        compiler_params=LIMIT,
-        name="edges",
+        out_specs=[VM] * 3,
+        compiler_params=LIMIT,
+        name="outward",
     )(x, u0, u2, u3, wown, m1, m2, m3, basis, turns)
+    uend, e = pl.pallas_call(
+        inward_kernel,
+        out_shape=[products, chunk],
+        in_specs=[VM] * 9,
+        out_specs=[VM] * 2,
+        compiler_params=LIMIT,
+        name="inward",
+    )(x, u0, u1, u2, u3, m1, wall, basis, turns)
     nb = lax.axis_size("blk")
     oin = lax.ppermute(o, "blk", partner(nb, 1))
     ein = lax.ppermute(e, "blk", partner(nb, 0))
     z, yi = pl.pallas_call(
         inner_kernel,
         out_shape=[shape((4, members, LANES), F32), shape((2, cols, width), F32)],
-        in_specs=[VM] * 10,
+        in_specs=[VM] * 8,
         out_specs=[VM] * 2,
         scratch_shapes=[pltpu.VMEM((nblk, members, LANES), F32)],
         compiler_params=LIMIT,
         name="inner",
-    )(x, uend, msg, m1, m2, m3, wall, left, basis, turns)
+    )(x, uend, m1, m2, wall, left, basis, turns)
     zo = z[:PAIR] + oin
     outs = pl.pallas_call(
         close_kernel,

time: 27.4 us -> 27.7 us (1.011)
    ppermute x3, waiting for transfers between devices: 4.13 us -> 4.43 us  [body(): total = total + lax.ppermute(outs[d], 'mem', crossed(nmem, d)).astype(F32)]
  transfers between devices with their start and end apart: 8 -> 8, of which waited for: 6 -> 5; matrix products, arithmetic and copies ran while one was open for 0% -> 0% of each run, Pallas kernels for 14% -> 14%
where the time goes in v6:
time: 27.7 us; the launch traced here: 27.6 us
  starting transfers between devices  12.7 us (46%)
  waiting for transfers between devices  7.82 us (28%)
  Pallas kernels  5.48 us (20%)
  between operations  0.79 us (3%)
  other arithmetic  0.69 us (2%)
    ppermute x3, waiting for transfers between devices, body(): total = total + lax.ppermute(outs[d], 'mem', crossed(nmem, d)).astype(F32)  4.43 us
    ppermute x1, starting transfers between devices, body(): oin = lax.ppermute(o, 'blk', partner(nb, 1))  4.24 us
    ppermute x3, starting transfers between devices, body(): total = total + lax.ppermute(outs[d], 'mem', crossed(nmem, d)).astype(F32)  4.17 us
    ppermute x3, starting transfers between devices, body(): m2, m3, m1 = [lax.ppermute(msg, 'mem', crossed(nmem, d)) for d in (2, 3, 1)]  4.17 us
    ppermute x3, waiting for transfers between devices, body(): m2, m3, m1 = [lax.ppermute(msg, 'mem', crossed(nmem, d)) for d in (2, 3, 1)]  3.32 us
    pallas_call x1, Pallas kernels, body(): pl.pallas_call(inner_kernel, out_shape=[shape((4, members, LANES), F32),...  2.22 us
    pallas_call x1, Pallas kernels, body(): pl.pallas_call(own_kernel, out_shape=[chunk, table, shape(x.shape, x.dtyp...  0.84 us
    pallas_call x1, Pallas kernels, body(): pl.pallas_call(close_kernel, out_shape=[shape((cols, width), F32)] + [sha...  0.78 us
  transfers between devices with their start and end apart: 8, of which 5 were waited for; matrix products, arithmetic and copies ran while one was open for 0% of the time, Pallas kernels for 14%

profile of v6, /device:TPU:0, one launch (start us, length us, event | category | flops | bytes accessed | tf_op | source)
XLA Modules:
  0.0 27.6 jit_solution(14129221614255340965)
XLA Ops:
  0.7 0.0 copy-done.4
  0.7 0.0 copy-done.3
  0.7 0.0 copy-done.5
  0.7 0.0 copy-start.1
  0.7 0.0 copy-start
  0.7 0.7 %tables.1 = (f32[16,2048]{1,0:T(8,128)S(1)}, f32[8,128]{1,0:T(8,128)S(1)}, f32[8,128]{1,0:T(8,128)S(1)}, bf16[8,256]{1,0:T(8,128)(2,1)S(1)}) custom-call(s32[4]{0:T(128)S(1)} %copy-done.3, s32[4]{0:T(128)S(1)} %copy-done.4, s32[1]{0:T(128)S(6)} %copy.8.count, f32[8]{0:T(128)S(1)} %copy-done.5), custom_call_target="tpu_custom_call" | custom-call | flops 1000000000 | bytes 4000000 | tf_op jit(solution)/shard_map/tables/pallas_call | solution.py:278
  1.5 0.1 copy-done.1
  1.6 3.2 %collective-permute-start.1 = (bf16[8,4352]{1,0:T(8,128)(2,1)S(1)}, bf16[8,4352]{1,0:T(8,128)(2,1)S(1)}, u32[]{:S(2)}, u32[]{:S(2)}) collective-permute-start(bf16[8,4352]{1,0:T(8,128)(2,1)S(1)} %message.1.v_ref), channel_id=1, source_target_pairs={{3,0},{2,1},{1,2},{0,3},{7,4},{6,5},{5,6},{4,7},{11,8},{10,9},{9,1... | collective-permute-start | bytes 208904 | tf_op jit(solution)/shard_map/ppermute | solution.py:295
  4.8 0.6 %collective-permute-start = (bf16[8,4352]{1,0:T(8,128)(2,1)S(1)}, bf16[8,4352]{1,0:T(8,128)(2,1)S(1)}, u32[]{:S(2)}, u32[]{:S(2)}) collective-permute-start(bf16[8,4352]{1,0:T(8,128)(2,1)S(1)} %message.1.v_ref), channel_id=1, source_target_pairs={{2,0},{3,1},{0,2},{1,3},{6,4},{7,5},{4,6},{5,7},{10,8},{11,9},{8,1... | collective-permute-start | bytes 208904 | tf_op jit(solution)/shard_map/ppermute | solution.py:295
  5.4 0.4 %collective-permute-start.2 = (bf16[8,4352]{1,0:T(8,128)(2,1)S(1)}, bf16[8,4352]{1,0:T(8,128)(2,1)S(1)}, u32[]{:S(2)}, u32[]{:S(2)}) collective-permute-start(bf16[8,4352]{1,0:T(8,128)(2,1)S(1)} %message.1.v_ref), channel_id=1, source_target_pairs={{1,0},{0,1},{3,2},{2,3},{5,4},{4,5},{7,6},{6,7},{9,8},{8,9},{11,10... | collective-permute-start | bytes 208904 | tf_op jit(solution)/shard_map/ppermute | solution.py:295
  5.8 0.0 copy-done
  5.8 0.0 copy-done.2
  5.8 0.8 %own.1 = (f32[2,32,128]{2,1,0:T(8,128)S(1)}, f32[16,2048]{1,0:T(8,128)S(1)}, bf16[32,16384]{1,0:T(8,128)(2,1)S(1)}) custom-call(f32[8]{0:T(128)S(1)} %copy-done.2, bf16[32,16384]{1,0:T(8,128)(2,1)S(1)} %copy-done, bf16[8,4352]{1,0:T(8,128)(2,1)S(1)} %message.1.v_ref, f32[16,2048]{1,0:T(8,128)S(1)} %get-tuple-element.24.basis_ref), custom_call_target="tpu_custom_call" | custom-call | tf_op jit(solution)/shard_map/own/pallas_call | solution.py:297
  6.6 0.9 %collective-permute-done.1.msg_ref.m3 = bf16[8,4352]{1,0:T(8,128)(2,1)S(1)} collective-permute-done((bf16[8,4352]{1,0:T(8,128)(2,1)S(1)}, bf16[8,4352]{1,0:T(8,128)(2,1)S(1)}, u32[]{:S(2)}, u32[]{:S(2)}) %collective-permute-start.1) | collective-permute-done | bytes 69664 | tf_op jit(solution)/shard_map/ppermute | solution.py:295
  7.5 0.7 %project_3.1.u3 = f32[2,32,128]{2,1,0:T(8,128)S(1)} custom-call(bf16[32,16384]{1,0:T(8,128)(2,1)S(1)} %get-tuple-element.25.x_ref, bf16[8,4352]{1,0:T(8,128)(2,1)S(1)} %collective-permute-done.1.msg_ref.m3, f32[16,2048]{1,0:T(8,128)S(1)} %get-tuple-element.24.basis_ref), custom_call_target="tpu_custom_call" | custom-call | tf_op jit(solution)/shard_map/project_3/pallas_call | solution.py:307
  8.2 2.5 %collective-permute-done.msg_ref.m2 = bf16[8,4352]{1,0:T(8,128)(2,1)S(1)} collective-permute-done((bf16[8,4352]{1,0:T(8,128)(2,1)S(1)}, bf16[8,4352]{1,0:T(8,128)(2,1)S(1)}, u32[]{:S(2)}, u32[]{:S(2)}) %collective-permute-start) | collective-permute-done | bytes 69664 | tf_op jit(solution)/shard_map/ppermute | solution.py:295
  10.7 0.0 collective-permute-done.2.m1
  10.7 0.1 outward.1
  10.8 4.2 %collective-permute-start.3 = (f32[2,32,128]{2,1,0:T(8,128)S(1)}, f32[2,32,128]{2,1,0:T(8,128)S(1)}, u32[]{:S(2)}, u32[]{:S(2)}) collective-permute-start(f32[2,32,128]{2,1,0:T(8,128)S(1)} %get-tuple-element.34), channel_id=1, source_target_pairs={{4,8},{12,16},{20,24},{28,32},{36,40},{44,48},{52,56},{60,64},{68,... | collective-permute-start | bytes 98312 | tf_op jit(solution)/shard_map/ppermute | solution.py:336
  15.0 0.1 inward.1
  15.1 0.1 collective-permute-start.4
  15.2 2.2 %inner.1 = (f32[4,32,128]{2,1,0:T(8,128)S(1)}, f32[2,8,4096]{2,1,0:T(8,128)S(1)}) custom-call(bf16[32,16384]{1,0:T(8,128)(2,1)S(1)} %get-tuple-element.25.x_ref, f32[8,32,128]{2,1,0:T(8,128)S(1)} %get-tuple-element.31.uin_ref, bf16[8,4352]{1,0:T(8,128)(2,1)S(1)} %collective-permute-done.2.m1, bf16[8,4352]{1,0:T(8,128)(2,1)S(1)} %collective-permute-done.msg_ref.m2, ...), custom_call_target="tpu_custom_call" | custom-call | tf_op jit(solution)/shard_map/inner/pallas_call | solution.py:338
  17.4 0.1 collective-permute-done.3.oin_ref
  17.5 0.0 collective-permute-done.4.ein_ref
  17.5 0.8 %close.1 = (f32[8,4096]{1,0:T(8,128)S(1)}, bf16[8,4096]{1,0:T(8,128)(2,1)S(1)}, bf16[8,4096]{1,0:T(8,128)(2,1)S(1)}, bf16[8,4096]{1,0:T(8,128)(2,1)S(1)}) custom-call(bf16[32,16384]{1,0:T(8,128)(2,1)S(1)} %get-tuple-element.25.x_ref, f32[4,32,128]{2,1,0:T(8,128)S(1)} %get-tuple-element.33.z_ref, f32[2,32,128]{2,1,0:T(8,128)S(1)} %slice_add_fusion.zo_ref, ...), custom_call_target="tpu_custom_call" | custom-call | tf_op jit(solution)/shard_map/close/pallas_call | solution.py:348
  18.3 2.2 %collective-permute-start.5 = (bf16[8,4096]{1,0:T(8,128)(2,1)S(1)}, bf16[8,4096]{1,0:T(8,128)(2,1)S(1)}, u32[]{:S(2)}, u32[]{:S(2)}) collective-permute-start(bf16[8,4096]{1,0:T(8,128)(2,1)S(1)} %get-tuple-element.38), channel_id=1, source_target_pairs={{3,0},{2,1},{1,2},{0,3},{7,4},{6,5},{5,6},{4,7},{11,8},{10,9},{9,1... | collective-permute-start | bytes 196616 | tf_op jit(solution)/shard_map/ppermute | solution.py:359
  20.5 1.9 %collective-permute-start.6 = (bf16[8,4096]{1,0:T(8,128)(2,1)S(1)}, bf16[8,4096]{1,0:T(8,128)(2,1)S(1)}, u32[]{:S(2)}, u32[]{:S(2)}) collective-permute-start(bf16[8,4096]{1,0:T(8,128)(2,1)S(1)} %get-tuple-element.39), channel_id=1, source_target_pairs={{2,0},{3,1},{0,2},{1,3},{6,4},{7,5},{4,6},{5,7},{10,8},{11,9},{8,1... | collective-permute-start | bytes 196616 | tf_op jit(solution)/shard_map/ppermute | solution.py:359
  22.4 0.1 collective-permute-start.7
  22.5 1.6 %collective-permute-done.5 = bf16[8,4096]{1,0:T(8,128)(2,1)S(1)} collective-permute-done((bf16[8,4096]{1,0:T(8,128)(2,1)S(1)}, bf16[8,4096]{1,0:T(8,128)(2,1)S(1)}, u32[]{:S(2)}, u32[]{:S(2)}) %collective-permute-start.5) | collective-permute-done | bytes 65568 | tf_op jit(solution)/shard_map/ppermute | solution.py:359
  24.0 2.9 %collective-permute-done.6 = bf16[8,4096]{1,0:T(8,128)(2,1)S(1)} collective-permute-done((bf16[8,4096]{1,0:T(8,128)(2,1)S(1)}, bf16[8,4096]{1,0:T(8,128)(2,1)S(1)}, u32[]{:S(2)}, u32[]{:S(2)}) %collective-permute-start.6) | collective-permute-done | bytes 65568 | tf_op jit(solution)/shard_map/ppermute | solution.py:359
  26.9 0.0 collective-permute-done.7
  26.9 0.7 %convert_add_fusion = f32[8,4096]{1,0:T(8,128)} fusion(bf16[8,4096]{1,0:T(8,128)(2,1)S(1)} %collective-permute-done.7, bf16[8,4096]{1,0:T(8,128)(2,1)S(1)} %collective-permute-done.6, f32[8,4096]{1,0:T(8,128)S(1)} %get-tuple-element.37, bf16[8,4096]{1,0:T(8,128)(2,1)S(1)} %collective-permute-done.5), kind=kLoop, calls=%fused_computation | loop fusion | flops 196608 | bytes 458752 | tf_op jit(solution)/shard_map/add | solution.py:359
  (7 shorter events, 0.0 us)
Async XLA Ops:
  0.0 0.7 %copy-start.4 = (s32[4]{0:T(128)S(1)}, s32[4]{0:T(128)}, u32[]{:S(2)}) copy-start(s32[4]{0:T(128)} %klass.1) | copy-start | bytes 52
  0.0 0.7 %copy-start.3 = (s32[4]{0:T(128)S(1)}, s32[4]{0:T(128)}, u32[]{:S(2)}) copy-start(s32[4]{0:T(128)} %code.1) | copy-start | bytes 52
  0.0 0.7 %copy-start.5 = (f32[8]{0:T(128)S(1)}, f32[8]{0:T(128)}, u32[]{:S(2)}) copy-start(f32[8]{0:T(128)} %table.1) | copy-start | bytes 100
  0.7 0.8 %copy-start.1 = (bf16[8,4096]{1,0:T(8,128)(2,1)S(1)}, bf16[8,4096]{1,0:T(8,128)(2,1)}, u32[]{:S(2)}) copy-start(bf16[8,4096]{1,0:T(8,128)(2,1)} %v_ref.1) | copy-start | bytes 196612
  0.7 5.0 %copy-start = (bf16[32,16384]{1,0:T(8,128)(2,1)S(1)}, bf16[32,16384]{1,0:T(8,128)(2,1)}, u32[]{:S(2)}) copy-start(bf16[32,16384]{1,0:T(8,128)(2,1)} %x_ref.1) | copy-start | bytes 3145732
  1.6 4.2 %copy-start.2 = (f32[8]{0:T(128)S(1)}, f32[8]{0:T(128)}, u32[]{:S(2)}) copy-start(f32[8]{0:T(128)} %modes_ref.1) | copy-start | bytes 100
  1.6 5.9 %collective-permute-start.1 = (bf16[8,4352]{1,0:T(8,128)(2,1)S(1)}, bf16[8,4352]{1,0:T(8,128)(2,1)S(1)}, u32[]{:S(2)}, u32[]{:S(2)}) collective-permute-start(bf16[8,4352]{1,0:T(8,128)(2,1)S(1)} %message.1.v_ref), channel_id=1, source_target_pairs={{3,0},{2,1},{1,2},{0,3},{7,4},{6,5},{5,6},{4,7},{11,8},{10,9},{9,1... | collective-permute-start | bytes 208904 | tf_op jit(solution)/shard_map/ppermute | solution.py:295
  4.8 5.9 %collective-permute-start = (bf16[8,4352]{1,0:T(8,128)(2,1)S(1)}, bf16[8,4352]{1,0:T(8,128)(2,1)S(1)}, u32[]{:S(2)}, u32[]{:S(2)}) collective-permute-start(bf16[8,4352]{1,0:T(8,128)(2,1)S(1)} %message.1.v_ref), channel_id=1, source_target_pairs={{2,0},{3,1},{0,2},{1,3},{6,4},{7,5},{4,6},{5,7},{10,8},{11,9},{8,1... | collective-permute-start | bytes 208904 | tf_op jit(solution)/shard_map/ppermute | solution.py:295
  5.4 5.3 %collective-permute-start.2 = (bf16[8,4352]{1,0:T(8,128)(2,1)S(1)}, bf16[8,4352]{1,0:T(8,128)(2,1)S(1)}, u32[]{:S(2)}, u32[]{:S(2)}) collective-permute-start(bf16[8,4352]{1,0:T(8,128)(2,1)S(1)} %message.1.v_ref), channel_id=1, source_target_pairs={{1,0},{0,1},{3,2},{2,3},{5,4},{4,5},{7,6},{6,7},{9,8},{8,9},{11,10... | collective-permute-start | bytes 208904 | tf_op jit(solution)/shard_map/ppermute | solution.py:295
  10.8 6.7 %collective-permute-start.3 = (f32[2,32,128]{2,1,0:T(8,128)S(1)}, f32[2,32,128]{2,1,0:T(8,128)S(1)}, u32[]{:S(2)}, u32[]{:S(2)}) collective-permute-start(f32[2,32,128]{2,1,0:T(8,128)S(1)} %get-tuple-element.34), channel_id=1, source_target_pairs={{4,8},{12,16},{20,24},{28,32},{36,40},{44,48},{52,56},{60,64},{68,... | collective-permute-start | bytes 98312 | tf_op jit(solution)/shard_map/ppermute | solution.py:336
  15.1 2.4 %collective-permute-start.4 = (f32[2,32,128]{2,1,0:T(8,128)S(1)}, f32[2,32,128]{2,1,0:T(8,128)S(1)}, u32[]{:S(2)}, u32[]{:S(2)}) collective-permute-start(f32[2,32,128]{2,1,0:T(8,128)S(1)} %get-tuple-element.35), channel_id=1, source_target_pairs={{0,4},{8,12},{16,20},{24,28},{32,36},{40,44},{48,52},{56,60},{64,6... | collective-permute-start | bytes 98312 | tf_op jit(solution)/shard_map/ppermute | solution.py:337
  18.3 5.7 %collective-permute-start.5 = (bf16[8,4096]{1,0:T(8,128)(2,1)S(1)}, bf16[8,4096]{1,0:T(8,128)(2,1)S(1)}, u32[]{:S(2)}, u32[]{:S(2)}) collective-permute-start(bf16[8,4096]{1,0:T(8,128)(2,1)S(1)} %get-tuple-element.38), channel_id=1, source_target_pairs={{3,0},{2,1},{1,2},{0,3},{7,4},{6,5},{5,6},{4,7},{11,8},{10,9},{9,1... | collective-permute-start | bytes 196616 | tf_op jit(solution)/shard_map/ppermute | solution.py:359
  20.5 6.4 %collective-permute-start.6 = (bf16[8,4096]{1,0:T(8,128)(2,1)S(1)}, bf16[8,4096]{1,0:T(8,128)(2,1)S(1)}, u32[]{:S(2)}, u32[]{:S(2)}) collective-permute-start(bf16[8,4096]{1,0:T(8,128)(2,1)S(1)} %get-tuple-element.39), channel_id=1, source_target_pairs={{2,0},{3,1},{0,2},{1,3},{6,4},{7,5},{4,6},{5,7},{10,8},{11,9},{8,1... | collective-permute-start | bytes 196616 | tf_op jit(solution)/shard_map/ppermute | solution.py:359
  22.4 4.5 %collective-permute-start.7 = (bf16[8,4096]{1,0:T(8,128)(2,1)S(1)}, bf16[8,4096]{1,0:T(8,128)(2,1)S(1)}, u32[]{:S(2)}, u32[]{:S(2)}) collective-permute-start(bf16[8,4096]{1,0:T(8,128)(2,1)S(1)} %get-tuple-element.40), channel_id=1, source_target_pairs={{1,0},{0,1},{3,2},{2,3},{5,4},{4,5},{7,6},{6,7},{9,8},{8,9},{11,10... | collective-permute-start | bytes 196616 | tf_op jit(solution)/shard_map/ppermute | solution.py:359

commit v7 on v5

--- a/solution.py
+++ b/solution.py
@@ -122,15 +122,12 @@
     gain = jnp.sum(jnp.where(row == lane, modes, F32(0.0)), axis=1, keepdims=True)
     l_ref[...] = basis_ref[...] * gain
 
-    @pl.when(at_end())
-    def _():
-        project_chunk(x_ref, v_ref, basis_ref, lax.axis_index("mem"), u_ref)
-
+    project_chunk(x_ref, v_ref, basis_ref, lax.axis_index("mem"), u_ref)
     copy.wait()
 
 
-def project_kernel(distance, ends, x_ref, msg_ref, basis_ref, u_ref):
-    @pl.when(at_end() if ends else jnp.logical_not(at_end()))
+def project_kernel(distance, every, x_ref, msg_ref, basis_ref, u_ref):
+    @pl.when(every | jnp.logical_not(at_end()))
     def _():
         project_chunk(x_ref, msg_ref, basis_ref, lax.axis_index("mem") ^ distance, u_ref)
 
@@ -144,10 +141,8 @@
         for j in range(PAIR):
             u_ref[(me ^ d) * PAIR + j] = u[j]
 
-    @pl.when(at_end())
-    def _():
-        keep(0, u0)
-        keep(3, u3)
+    keep(0, u0)
+    keep(3, u3)
 
     @pl.when(jnp.logical_not(at_end()))
     def _():
@@ -182,7 +177,7 @@
 
 
 def inner_kernel(
-    x_ref, uin_ref, v_ref, m1, m2, m3, w_ref, l_ref, basis_ref, turns_ref, z_ref, y_ref, u_ref
+    x_ref, uin_ref, m1, m2, w_ref, l_ref, basis_ref, turns_ref, z_ref, y_ref, u_ref
 ):
     me = lax.axis_index("mem")
     u_ref[...] = uin_ref[...]
@@ -190,11 +185,6 @@
     @pl.when(at_end())
     def _():
         for d, m in ((1, m1), (2, m2)):
-            project_chunk(x_ref, m, basis_ref, me ^ d, chunk_of(u_ref, d))
-
-    @pl.when(jnp.logical_not(at_end()))
-    def _():
-        for d, m in ((0, v_ref), (3, m3)):
             project_chunk(x_ref, m, basis_ref, me ^ d, chunk_of(u_ref, d))
 
     nblk = u_ref.shape[0]
@@ -317,12 +307,12 @@
     z, yi = pl.pallas_call(
         inner_kernel,
         out_shape=[shape((4, members, LANES), F32), shape((2, cols, width), F32)],
-        in_specs=[VM] * 10,
+        in_specs=[VM] * 8,
         out_specs=[VM] * 2,
         scratch_shapes=[pltpu.VMEM((nblk, members, LANES), F32)],
         compiler_params=LIMIT,
         name="inner",
-    )(x, uend, msg, m1, m2, m3, wall, left, basis, turns)
+    )(x, uend, m1, m2, wall, left, basis, turns)
     zo = z[:PAIR] + oin
     outs = pl.pallas_call(
         close_kernel,

time: 27.4 us -> 27.5 us (level)
  transfers between devices with their start and end apart: 8 -> 8, of which waited for: 6 -> 5; matrix products, arithmetic and copies ran while one was open for 0% -> 0% of each run, Pallas kernels for 14% -> 14%
where the time goes in v7:
time: 27.5 us; the launch traced here: 27.4 us
  starting transfers between devices  12.6 us (46%)
  waiting for transfers between devices  7.81 us (28%)
  Pallas kernels  5.4 us (20%)
  between operations  0.78 us (3%)
  other arithmetic  0.69 us (3%)
    ppermute x1, starting transfers between devices, body(): oin = lax.ppermute(o, 'blk', partner(nb, 1))  4.24 us
    ppermute x3, waiting for transfers between devices, body(): total = total + lax.ppermute(outs[d], 'mem', crossed(nmem, d)).astype(F32)  4.23 us
    ppermute x3, starting transfers between devices, body(): total = total + lax.ppermute(outs[d], 'mem', crossed(nmem, d)).astype(F32)  4.17 us
    ppermute x3, starting transfers between devices, body(): m2, m3, m1 = [lax.ppermute(msg, 'mem', crossed(nmem, d)) for d in (2, 3, 1)]  4.17 us
    ppermute x3, waiting for transfers between devices, body(): m2, m3, m1 = [lax.ppermute(msg, 'mem', crossed(nmem, d)) for d in (2, 3, 1)]  3.32 us
    pallas_call x1, Pallas kernels, body(): pl.pallas_call(inner_kernel, out_shape=[shape((4, members, LANES), F32),...  2.22 us
    pallas_call x1, Pallas kernels, body(): pl.pallas_call(own_kernel, out_shape=[chunk, table, shape(x.shape, x.dtyp...  0.84 us
    pallas_call x1, Pallas kernels, body(): pl.pallas_call(close_kernel, out_shape=[shape((cols, width), F32)] + [sha...  0.78 us
  transfers between devices with their start and end apart: 8, of which 5 were waited for; matrix products, arithmetic and copies ran while one was open for 0% of the time, Pallas kernels for 14%

profile of v7, /device:TPU:0, one launch (start us, length us, event | category | flops | bytes accessed | tf_op | source)
XLA Modules:
  0.0 27.4 jit_solution(808660792090364925)
XLA Ops:
  0.0 0.0 copy-start.4
  0.7 0.0 copy-done.4
  0.7 0.0 copy-done.3
  0.7 0.0 copy-done.5
  0.7 0.0 copy-start.1
  0.7 0.0 copy-start
  0.7 0.7 %tables.1 = (f32[16,2048]{1,0:T(8,128)S(1)}, f32[8,128]{1,0:T(8,128)S(1)}, f32[8,128]{1,0:T(8,128)S(1)}, bf16[8,256]{1,0:T(8,128)(2,1)S(1)}) custom-call(s32[4]{0:T(128)S(1)} %copy-done.3, s32[4]{0:T(128)S(1)} %copy-done.4, s32[1]{0:T(128)S(6)} %copy.8.count, f32[8]{0:T(128)S(1)} %copy-done.5), custom_call_target="tpu_custom_call" | custom-call | flops 1000000000 | bytes 4000000 | tf_op jit(solution)/shard_map/tables/pallas_call | solution.py:255
  1.5 0.1 copy-done.1
  1.6 3.2 %collective-permute-start.1 = (bf16[8,4352]{1,0:T(8,128)(2,1)S(1)}, bf16[8,4352]{1,0:T(8,128)(2,1)S(1)}, u32[]{:S(2)}, u32[]{:S(2)}) collective-permute-start(bf16[8,4352]{1,0:T(8,128)(2,1)S(1)} %message.1.v_ref), channel_id=1, source_target_pairs={{3,0},{2,1},{1,2},{0,3},{7,4},{6,5},{5,6},{4,7},{11,8},{10,9},{9,1... | collective-permute-start | bytes 208904 | tf_op jit(solution)/shard_map/ppermute | solution.py:272
  4.8 0.6 %collective-permute-start = (bf16[8,4352]{1,0:T(8,128)(2,1)S(1)}, bf16[8,4352]{1,0:T(8,128)(2,1)S(1)}, u32[]{:S(2)}, u32[]{:S(2)}) collective-permute-start(bf16[8,4352]{1,0:T(8,128)(2,1)S(1)} %message.1.v_ref), channel_id=1, source_target_pairs={{2,0},{3,1},{0,2},{1,3},{6,4},{7,5},{4,6},{5,7},{10,8},{11,9},{8,1... | collective-permute-start | bytes 208904 | tf_op jit(solution)/shard_map/ppermute | solution.py:272
  5.4 0.4 %collective-permute-start.2 = (bf16[8,4352]{1,0:T(8,128)(2,1)S(1)}, bf16[8,4352]{1,0:T(8,128)(2,1)S(1)}, u32[]{:S(2)}, u32[]{:S(2)}) collective-permute-start(bf16[8,4352]{1,0:T(8,128)(2,1)S(1)} %message.1.v_ref), channel_id=1, source_target_pairs={{1,0},{0,1},{3,2},{2,3},{5,4},{4,5},{7,6},{6,7},{9,8},{8,9},{11,10... | collective-permute-start | bytes 208904 | tf_op jit(solution)/shard_map/ppermute | solution.py:272
  5.8 0.0 copy-done
  5.8 0.0 copy-done.2
  5.8 0.8 %own.1 = (f32[2,32,128]{2,1,0:T(8,128)S(1)}, f32[16,2048]{1,0:T(8,128)S(1)}, bf16[32,16384]{1,0:T(8,128)(2,1)S(1)}) custom-call(f32[8]{0:T(128)S(1)} %copy-done.2, bf16[32,16384]{1,0:T(8,128)(2,1)S(1)} %copy-done, bf16[8,4352]{1,0:T(8,128)(2,1)S(1)} %message.1.v_ref, f32[16,2048]{1,0:T(8,128)S(1)} %get-tuple-element.23.basis_ref), custom_call_target="tpu_custom_call" | custom-call | tf_op jit(solution)/shard_map/own/pallas_call | solution.py:274
  6.6 0.9 %collective-permute-done.1.msg_ref.m3 = bf16[8,4352]{1,0:T(8,128)(2,1)S(1)} collective-permute-done((bf16[8,4352]{1,0:T(8,128)(2,1)S(1)}, bf16[8,4352]{1,0:T(8,128)(2,1)S(1)}, u32[]{:S(2)}, u32[]{:S(2)}) %collective-permute-start.1) | collective-permute-done | bytes 69664 | tf_op jit(solution)/shard_map/ppermute | solution.py:272
  7.5 0.7 %project_3.1.u3 = f32[2,32,128]{2,1,0:T(8,128)S(1)} custom-call(bf16[32,16384]{1,0:T(8,128)(2,1)S(1)} %get-tuple-element.24.x_ref, bf16[8,4352]{1,0:T(8,128)(2,1)S(1)} %collective-permute-done.1.msg_ref.m3, f32[16,2048]{1,0:T(8,128)S(1)} %get-tuple-element.23.basis_ref), custom_call_target="tpu_custom_call" | custom-call | tf_op jit(solution)/shard_map/project_3/pallas_call | solution.py:284
  8.2 2.5 %collective-permute-done.msg_ref.m2 = bf16[8,4352]{1,0:T(8,128)(2,1)S(1)} collective-permute-done((bf16[8,4352]{1,0:T(8,128)(2,1)S(1)}, bf16[8,4352]{1,0:T(8,128)(2,1)S(1)}, u32[]{:S(2)}, u32[]{:S(2)}) %collective-permute-start) | collective-permute-done | bytes 69664 | tf_op jit(solution)/shard_map/ppermute | solution.py:272
  10.7 0.0 collective-permute-done.2.m1
  10.7 0.1 edges.1
  10.8 4.2 %collective-permute-start.3 = (f32[2,32,128]{2,1,0:T(8,128)S(1)}, f32[2,32,128]{2,1,0:T(8,128)S(1)}, u32[]{:S(2)}, u32[]{:S(2)}) collective-permute-start(f32[2,32,128]{2,1,0:T(8,128)S(1)} %get-tuple-element.32), channel_id=1, source_target_pairs={{4,8},{12,16},{20,24},{28,32},{36,40},{44,48},{52,56},{60,64},{68,... | collective-permute-start | bytes 98312 | tf_op jit(solution)/shard_map/ppermute | solution.py:305
  15.0 0.0 collective-permute-start.4
  15.0 2.2 %inner.1 = (f32[4,32,128]{2,1,0:T(8,128)S(1)}, f32[2,8,4096]{2,1,0:T(8,128)S(1)}) custom-call(bf16[32,16384]{1,0:T(8,128)(2,1)S(1)} %get-tuple-element.24.x_ref, f32[8,32,128]{2,1,0:T(8,128)S(1)} %get-tuple-element.28.uin_ref, bf16[8,4352]{1,0:T(8,128)(2,1)S(1)} %collective-permute-done.2.m1, bf16[8,4352]{1,0:T(8,128)(2,1)S(1)} %collective-permute-done.msg_ref.m2, ...), custom_call_target="tpu_custom_call" | custom-call | tf_op jit(solution)/shard_map/inner/pallas_call | solution.py:307
  17.2 0.3 collective-permute-done.3.oin_ref
  17.5 0.0 collective-permute-done.4.ein_ref
  17.5 0.8 %close.1 = (f32[8,4096]{1,0:T(8,128)S(1)}, bf16[8,4096]{1,0:T(8,128)(2,1)S(1)}, bf16[8,4096]{1,0:T(8,128)(2,1)S(1)}, bf16[8,4096]{1,0:T(8,128)(2,1)S(1)}) custom-call(bf16[32,16384]{1,0:T(8,128)(2,1)S(1)} %get-tuple-element.24.x_ref, f32[4,32,128]{2,1,0:T(8,128)S(1)} %get-tuple-element.31.z_ref, f32[2,32,128]{2,1,0:T(8,128)S(1)} %slice_add_fusion.zo_ref, ...), custom_call_target="tpu_custom_call" | custom-call | tf_op jit(solution)/shard_map/close/pallas_call | solution.py:317
  18.3 2.0 %collective-permute-start.5 = (bf16[8,4096]{1,0:T(8,128)(2,1)S(1)}, bf16[8,4096]{1,0:T(8,128)(2,1)S(1)}, u32[]{:S(2)}, u32[]{:S(2)}) collective-permute-start(bf16[8,4096]{1,0:T(8,128)(2,1)S(1)} %get-tuple-element.36), channel_id=1, source_target_pairs={{3,0},{2,1},{1,2},{0,3},{7,4},{6,5},{5,6},{4,7},{11,8},{10,9},{9,1... | collective-permute-start | bytes 196616 | tf_op jit(solution)/shard_map/ppermute | solution.py:328
  20.3 2.1 %collective-permute-start.6 = (bf16[8,4096]{1,0:T(8,128)(2,1)S(1)}, bf16[8,4096]{1,0:T(8,128)(2,1)S(1)}, u32[]{:S(2)}, u32[]{:S(2)}) collective-permute-start(bf16[8,4096]{1,0:T(8,128)(2,1)S(1)} %get-tuple-element.37), channel_id=1, source_target_pairs={{2,0},{3,1},{0,2},{1,3},{6,4},{7,5},{4,6},{5,7},{10,8},{11,9},{8,1... | collective-permute-start | bytes 196616 | tf_op jit(solution)/shard_map/ppermute | solution.py:328
  22.3 0.1 collective-permute-start.7
  22.5 1.4 %collective-permute-done.5 = bf16[8,4096]{1,0:T(8,128)(2,1)S(1)} collective-permute-done((bf16[8,4096]{1,0:T(8,128)(2,1)S(1)}, bf16[8,4096]{1,0:T(8,128)(2,1)S(1)}, u32[]{:S(2)}, u32[]{:S(2)}) %collective-permute-start.5) | collective-permute-done | bytes 65568 | tf_op jit(solution)/shard_map/ppermute | solution.py:328
  23.9 2.8 %collective-permute-done.6 = bf16[8,4096]{1,0:T(8,128)(2,1)S(1)} collective-permute-done((bf16[8,4096]{1,0:T(8,128)(2,1)S(1)}, bf16[8,4096]{1,0:T(8,128)(2,1)S(1)}, u32[]{:S(2)}, u32[]{:S(2)}) %collective-permute-start.6) | collective-permute-done | bytes 65568 | tf_op jit(solution)/shard_map/ppermute | solution.py:328
  26.7 0.0 collective-permute-done.7
  26.7 0.7 %convert_add_fusion = f32[8,4096]{1,0:T(8,128)} fusion(bf16[8,4096]{1,0:T(8,128)(2,1)S(1)} %collective-permute-done.7, bf16[8,4096]{1,0:T(8,128)(2,1)S(1)} %collective-permute-done.6, f32[8,4096]{1,0:T(8,128)S(1)} %get-tuple-element.35, bf16[8,4096]{1,0:T(8,128)(2,1)S(1)} %collective-permute-done.5), kind=kLoop, calls=%fused_computation | loop fusion | flops 196608 | bytes 458752 | tf_op jit(solution)/shard_map/add | solution.py:328
  (6 shorter events, 0.0 us)
Async XLA Ops:
  0.0 0.7 %copy-start.4 = (s32[4]{0:T(128)S(1)}, s32[4]{0:T(128)}, u32[]{:S(2)}) copy-start(s32[4]{0:T(128)} %klass.1) | copy-start | bytes 52
  0.0 0.7 %copy-start.3 = (s32[4]{0:T(128)S(1)}, s32[4]{0:T(128)}, u32[]{:S(2)}) copy-start(s32[4]{0:T(128)} %code.1) | copy-start | bytes 52
  0.0 0.7 %copy-start.5 = (f32[8]{0:T(128)S(1)}, f32[8]{0:T(128)}, u32[]{:S(2)}) copy-start(f32[8]{0:T(128)} %table.1) | copy-start | bytes 100
  0.7 0.8 %copy-start.1 = (bf16[8,4096]{1,0:T(8,128)(2,1)S(1)}, bf16[8,4096]{1,0:T(8,128)(2,1)}, u32[]{:S(2)}) copy-start(bf16[8,4096]{1,0:T(8,128)(2,1)} %v_ref.1) | copy-start | bytes 196612
  0.7 5.0 %copy-start = (bf16[32,16384]{1,0:T(8,128)(2,1)S(1)}, bf16[32,16384]{1,0:T(8,128)(2,1)}, u32[]{:S(2)}) copy-start(bf16[32,16384]{1,0:T(8,128)(2,1)} %x_ref.1) | copy-start | bytes 3145732
  1.6 4.2 %copy-start.2 = (f32[8]{0:T(128)S(1)}, f32[8]{0:T(128)}, u32[]{:S(2)}) copy-start(f32[8]{0:T(128)} %modes_ref.1) | copy-start | bytes 100
  1.6 5.9 %collective-permute-start.1 = (bf16[8,4352]{1,0:T(8,128)(2,1)S(1)}, bf16[8,4352]{1,0:T(8,128)(2,1)S(1)}, u32[]{:S(2)}, u32[]{:S(2)}) collective-permute-start(bf16[8,4352]{1,0:T(8,128)(2,1)S(1)} %message.1.v_ref), channel_id=1, source_target_pairs={{3,0},{2,1},{1,2},{0,3},{7,4},{6,5},{5,6},{4,7},{11,8},{10,9},{9,1... | collective-permute-start | bytes 208904 | tf_op jit(solution)/shard_map/ppermute | solution.py:272
  4.8 5.9 %collective-permute-start = (bf16[8,4352]{1,0:T(8,128)(2,1)S(1)}, bf16[8,4352]{1,0:T(8,128)(2,1)S(1)}, u32[]{:S(2)}, u32[]{:S(2)}) collective-permute-start(bf16[8,4352]{1,0:T(8,128)(2,1)S(1)} %message.1.v_ref), channel_id=1, source_target_pairs={{2,0},{3,1},{0,2},{1,3},{6,4},{7,5},{4,6},{5,7},{10,8},{11,9},{8,1... | collective-permute-start | bytes 208904 | tf_op jit(solution)/shard_map/ppermute | solution.py:272
  5.4 5.3 %collective-permute-start.2 = (bf16[8,4352]{1,0:T(8,128)(2,1)S(1)}, bf16[8,4352]{1,0:T(8,128)(2,1)S(1)}, u32[]{:S(2)}, u32[]{:S(2)}) collective-permute-start(bf16[8,4352]{1,0:T(8,128)(2,1)S(1)} %message.1.v_ref), channel_id=1, source_target_pairs={{1,0},{0,1},{3,2},{2,3},{5,4},{4,5},{7,6},{6,7},{9,8},{8,9},{11,10... | collective-permute-start | bytes 208904 | tf_op jit(solution)/shard_map/ppermute | solution.py:272
  10.8 6.7 %collective-permute-start.3 = (f32[2,32,128]{2,1,0:T(8,128)S(1)}, f32[2,32,128]{2,1,0:T(8,128)S(1)}, u32[]{:S(2)}, u32[]{:S(2)}) collective-permute-start(f32[2,32,128]{2,1,0:T(8,128)S(1)} %get-tuple-element.32), channel_id=1, source_target_pairs={{4,8},{12,16},{20,24},{28,32},{36,40},{44,48},{52,56},{60,64},{68,... | collective-permute-start | bytes 98312 | tf_op jit(solution)/shard_map/ppermute | solution.py:305
  15.0 2.5 %collective-permute-start.4 = (f32[2,32,128]{2,1,0:T(8,128)S(1)}, f32[2,32,128]{2,1,0:T(8,128)S(1)}, u32[]{:S(2)}, u32[]{:S(2)}) collective-permute-start(f32[2,32,128]{2,1,0:T(8,128)S(1)} %get-tuple-element.33), channel_id=1, source_target_pairs={{0,4},{8,12},{16,20},{24,28},{32,36},{40,44},{48,52},{56,60},{64,6... | collective-permute-start | bytes 98312 | tf_op jit(solution)/shard_map/ppermute | solution.py:306
  18.3 5.6 %collective-permute-start.5 = (bf16[8,4096]{1,0:T(8,128)(2,1)S(1)}, bf16[8,4096]{1,0:T(8,128)(2,1)S(1)}, u32[]{:S(2)}, u32[]{:S(2)}) collective-permute-start(bf16[8,4096]{1,0:T(8,128)(2,1)S(1)} %get-tuple-element.36), channel_id=1, source_target_pairs={{3,0},{2,1},{1,2},{0,3},{7,4},{6,5},{5,6},{4,7},{11,8},{10,9},{9,1... | collective-permute-start | bytes 196616 | tf_op jit(solution)/shard_map/ppermute | solution.py:328
  20.3 6.4 %collective-permute-start.6 = (bf16[8,4096]{1,0:T(8,128)(2,1)S(1)}, bf16[8,4096]{1,0:T(8,128)(2,1)S(1)}, u32[]{:S(2)}, u32[]{:S(2)}) collective-permute-start(bf16[8,4096]{1,0:T(8,128)(2,1)S(1)} %get-tuple-element.37), channel_id=1, source_target_pairs={{2,0},{3,1},{0,2},{1,3},{6,4},{7,5},{4,6},{5,7},{10,8},{11,9},{8,1... | collective-permute-start | bytes 196616 | tf_op jit(solution)/shard_map/ppermute | solution.py:328
  22.3 4.4 %collective-permute-start.7 = (bf16[8,4096]{1,0:T(8,128)(2,1)S(1)}, bf16[8,4096]{1,0:T(8,128)(2,1)S(1)}, u32[]{:S(2)}, u32[]{:S(2)}) collective-permute-start(bf16[8,4096]{1,0:T(8,128)(2,1)S(1)} %get-tuple-element.38), channel_id=1, source_target_pairs={{1,0},{0,1},{3,2},{2,3},{5,4},{4,5},{7,6},{6,7},{9,8},{8,9},{11,10... | collective-permute-start | bytes 196616 | tf_op jit(solution)/shard_map/ppermute | solution.py:328
